TPU v7x, 256 devices: a whole 4x4x8 slice. The times are simulated.
256 devices in a mesh: elem: 64 (over z, y, core), sec: 4 (over x).
Axes of the slice: x: 4, y: 4, z: 8, core: 2. Of those that a mesh axis runs over, the one named last changes fastest.
Arguments:
- fields: float32 [8192, 16, 640], P(('elem', 'sec')), may hold values from -6 to 6
- neighbours: int32 [8192, 4], P(('elem', 'sec')), may hold values from 0 to 8191, as said below
- operator: float32 [16, 16], replicated, may hold values from -1.5 to 1.5
- rates: float32 [640], replicated, may hold values from 0.05 to 0.5
- regime_ids: int32 [131072, 1], P(('elem', 'sec')), may hold values from 0 to 63; in each aligned block of 512 rows (0 to 511, 512 to 1023, ...) at most 16 rows name the same one
- input_proj: bfloat16 [64, 640, 1024], P('elem', None, 'sec'), may hold values from -0.4375 to 0.4375
- hidden_proj: bfloat16 [64, 2, 1024, 1024], P('elem', None, None, 'sec'), may hold values from -0.25 to 0.25
- output_proj: bfloat16 [64, 1024, 640], P('elem', None, 'sec'), may hold values from -0.25 to 0.25
Outputs:
- updated: float32 [8192, 16, 640], P(('elem', 'sec'))
Inputs may be any that keep to these rules, and one draw needn't show every extreme that they name: If edge k of element a names b, the opposite edge (west with east, south with north) of b names a. West and east neighbours are among the 32 elements of the same device along elem+sec, where element g lies on device g // 32; south neighbours lie on the device before and north neighbours on the device after, wrapping around. `regime_ids`: of the 512 columns of one device, at most 16 name the same regime, and some device reaches that.
All inputs are finite; a program needn't handle non-finite values.
Results may differ from a plain program's by a relative error of at most 0.015.
Values may be sent and summed in bfloat16 or wider, within the bound.
No kernel may reach another device: no remote copies, remote signals or barrier semaphores. Data moves between devices by JAX's collectives and lax.ppermute only.
A program may use at most 64 MiB of HBM per device.

v0:
```python
import jax
import jax.numpy as jnp
import numpy as np
from jax import lax
from jax.sharding import PartitionSpec as P

DYN_STEPS = 2


west_points = np.array([0, 4, 8, 12])
east_points = np.array([3, 7, 11, 15])
south_points = np.array([0, 1, 2, 3])
north_points = np.array([12, 13, 14, 15])


def padded(cells, sides, width):
    for axis, dim in sides:
        count = lax.axis_size(axis)
        head = lax.slice_in_dim(cells, 0, width, axis=dim)
        tail = lax.slice_in_dim(cells, cells.shape[dim] - width, cells.shape[dim], axis=dim)
        cells = jnp.concatenate(
            [
                lax.ppermute(tail, axis, [(i, (i + 1) % count) for i in range(count)]),
                cells,
                lax.ppermute(head, axis, [((i + 1) % count, i) for i in range(count)]),
            ],
            axis=dim,
        )
    return cells


def dynamics(state, neighbours, operator, rates):
    count = state.shape[0]
    owner = lax.axis_index(("elem", "sec"))
    total = lax.axis_size(("elem", "sec")) * count
    base = owner * count
    moved = jnp.einsum("pq,eqf->epf", operator, state, precision=lax.Precision.HIGHEST)
    first = state + rates * moved
    left = first[:, west_points]
    right = first[:, east_points]
    new_left = 0.5 * (left + jnp.take(right, neighbours[:, 0] - base, axis=0))
    new_right = 0.5 * (right + jnp.take(left, neighbours[:, 1] - base, axis=0))
    second = first.at[:, west_points].set(new_left).at[:, east_points].set(new_right)
    lower = second[:, south_points]
    upper = second[:, north_points]
    margin = padded(second, ((("elem", "sec"), 0),), count)
    below_index = jnp.mod(neighbours[:, 2] - base + count, total)
    above_index = jnp.mod(neighbours[:, 3] - base + count, total)
    upper_far = jnp.take(margin[:, north_points], below_index, axis=0)
    lower_far = jnp.take(margin[:, south_points], above_index, axis=0)
    new_lower = 0.5 * (lower + upper_far)
    new_upper = 0.5 * (upper + lower_far)
    return second.at[:, south_points].set(new_lower).at[:, north_points].set(new_upper)


def activate(rows, matrix):
    return jax.nn.silu(jnp.dot(rows, matrix, preferred_element_type=jnp.float32)).astype(
        jnp.bfloat16
    )


def on_device(
    fields, neighbours, operator, rates, regime_ids, input_proj, hidden_proj, output_proj
):
    state = fields
    for _ in range(DYN_STEPS):
        state = dynamics(state, neighbours, operator, rates)
    rows_dev = regime_ids.shape[0]
    width = state.shape[2]
    groups = lax.axis_size("elem")
    capacity = 2 * rows_dev // groups
    target = regime_ids[:, 0]
    onehot = (target[:, None] == jnp.arange(groups, dtype=jnp.int32)[None, :]).astype(jnp.int32)
    ranking = jnp.sum((jnp.cumsum(onehot, axis=0) - 1) * onehot, axis=1)
    slot_index = target * capacity + ranking
    columns = state.reshape(rows_dev, width).astype(jnp.bfloat16)
    outgoing = jnp.zeros((groups * capacity, width), jnp.bfloat16).at[slot_index].set(columns)
    incoming = lax.all_to_all(
        outgoing.reshape(groups, capacity, width), "elem", split_axis=0, concat_axis=0, tiled=True
    )
    rows = incoming.reshape(groups * capacity, width)
    hidden = activate(rows, lax.all_gather(input_proj[0], "sec", axis=1, tiled=True))
    for layer in range(hidden_proj.shape[1]):
        current = hidden
        hidden = activate(current, lax.all_gather(hidden_proj[0, layer], "sec", axis=1, tiled=True))
    result = jnp.dot(
        hidden,
        lax.all_gather(output_proj[0], "sec", axis=1, tiled=True),
        preferred_element_type=jnp.float32,
    ).astype(jnp.bfloat16)
    returned = lax.all_to_all(
        result.reshape(groups, capacity, width), "elem", split_axis=0, concat_axis=0, tiled=True
    )
    tendency = jnp.take(returned.reshape(groups * capacity, width), slot_index, axis=0)
    return state + tendency.astype(jnp.float32).reshape(state.shape)


def solution(mesh):
    return jax.shard_map(
        on_device,
        mesh=mesh,
        in_specs=(
            P(("elem", "sec"), None, None),
            P(("elem", "sec"), None),
            P(),
            P(),
            P(("elem", "sec"), None),
            P("elem", None, "sec"),
            P("elem", None, None, "sec"),
            P("elem", None, "sec"),
        ),
        out_specs=P(("elem", "sec"), None, None),
        check_vma=False,
    )
```

profile of v0, /device:TPU:1, one launch (start us, length us, event | category | flops | bytes accessed | tf_op | source)
XLA Modules:
  0.0 263.2 jit_solution(10200903932517203389)
XLA Ops:
  7.3 3.2 %fusion.9 = f32[32,16,640]{2,1,0:T(8,128)S(1)} fusion(f32[32,16,640]{2,1,0:T(8,128)} %param.36, f32[640]{0:T(1024)} %param.39, f32[16,16]{1,0:T(8,128)S(1)} %copy-done), kind=kOutput, calls=%fused_computation.44 | convolution fusion | flops 63569920 | bytes 2625024 | tf_op jit(solution)/shard_map/pq,eqf->epf/dot_general | solution.py:37
  16.0 2.1 collective-permute-start
  18.1 1.9 collective-permute-start.1
  20.0 2.3 fusion.54
  25.2 33.8 %collective-permute-done = f32[32,16,640]{2,0,1:T(8,128)} collective-permute-done((f32[32,16,640]{2,0,1:T(8,128)S(1)}, f32[32,16,640]{2,0,1:T(8,128)}, u32[]{:S(2)}, u32[]{:S(2)}) %collective-permute-start) | collective-permute-done | bytes 1310752 | tf_op jit(solution)/shard_map/ppermute | solution.py:23
  59.0 2.5 constant_dynamic-update-slice_fusion.2
  63.8 2.7 %gather_fusion.5 = f32[4,96,640]{2,1,0:T(8,128)S(1)} fusion(f32[96,16,640]{2,0,1:T(8,128)} %constant_dynamic-update-slice_fusion, s32[1024]{0:T(1024)S(1)} %get-tuple-element.28), kind=kCustom, calls=%fused_computation.13 | custom fusion | bytes 1966096 | tf_op jit(solution)/shard_map/gather | solution.py:50
  66.5 2.7 %gather_fusion.3 = f32[4,96,640]{2,1,0:T(8,128)S(1)} fusion(f32[96,16,640]{2,0,1:T(8,128)} %constant_dynamic-update-slice_fusion, s32[1024]{0:T(1024)S(1)} %get-tuple-element.27), kind=kCustom, calls=%fused_computation.11 | custom fusion | bytes 1966096 | tf_op jit(solution)/shard_map/gather | solution.py:49
  71.5 2.7 %gather_fusion.16 = f32[32,4,640]{2,1,0:T(4,128)} fusion(f32[96,4,640]{2,1,0:T(4,128)} %copy.77, s32[1024]{0:T(1024)S(1)} %get-tuple-element.25), kind=kCustom, calls=%fused_computation.5.clone | custom fusion | bytes 655488 | tf_op jit(solution)/shard_map/jit(_take)/gather | solution.py:50
  78.4 2.6 %fusion.7 = f32[32,16,640]{2,1,0:T(8,128)S(1)} fusion(f32[32,16,640]{2,0,1:T(8,128)S(1)} %scatter_fusion.3, f32[640]{0:T(1024)S(1)} %copy-done.7, f32[16,16]{1,0:T(8,128)S(1)} %copy-done), kind=kOutput, calls=%fused_computation.41 | convolution fusion | flops 63569920 | bytes 2625024 | tf_op jit(solution)/shard_map/pq,eqf->epf/dot_general | solution.py:37
  86.3 2.9 %collective-permute-start.3 = (f32[32,16,640]{2,0,1:T(8,128)S(1)}, f32[32,16,640]{2,0,1:T(8,128)S(1)}, u32[]{:S(2)}, u32[]{:S(2)}) collective-permute-start(f32[32,16,640]{2,0,1:T(8,128)S(1)} %scatter_fusion.5), channel_id=1, source_target_pairs={{1,0},{2,1},{3,2},{4,3},{5,4},{6,5},{7,6},{8,7},{9,8},{10,9},{11,1... | collective-permute-start | bytes 3932168 | tf_op jit(solution)/shard_map/ppermute | solution.py:25
  93.5 32.6 %collective-permute-done.2 = f32[32,16,640]{2,0,1:T(8,128)} collective-permute-done((f32[32,16,640]{2,0,1:T(8,128)S(1)}, f32[32,16,640]{2,0,1:T(8,128)}, u32[]{:S(2)}, u32[]{:S(2)}) %collective-permute-start.2) | collective-permute-done | bytes 1310752 | tf_op jit(solution)/shard_map/ppermute | solution.py:23
  126.2 2.5 constant_dynamic-update-slice_fusion.5
  131.0 2.7 %gather_fusion.11 = f32[4,96,640]{2,1,0:T(8,128)S(1)} fusion(f32[96,16,640]{2,0,1:T(8,128)} %constant_dynamic-update-slice_fusion.3, s32[1024]{0:T(1024)S(1)} %get-tuple-element.28), kind=kCustom, calls=%fused_computation.19 | custom fusion | bytes 1966096 | tf_op jit(solution)/shard_map/gather | solution.py:50
  133.7 2.8 %gather_fusion.9 = f32[4,96,640]{2,1,0:T(8,128)S(1)} fusion(f32[96,16,640]{2,0,1:T(8,128)} %constant_dynamic-update-slice_fusion.3, s32[1024]{0:T(1024)S(1)} %get-tuple-element.27), kind=kCustom, calls=%fused_computation.17 | custom fusion | bytes 1966096 | tf_op jit(solution)/shard_map/gather | solution.py:49
  138.1 2.7 %gather_fusion.20 = f32[32,4,640]{2,1,0:T(4,128)} fusion(f32[96,4,640]{2,1,0:T(4,128)} %copy.90, s32[1024]{0:T(1024)S(1)} %get-tuple-element.25), kind=kCustom, calls=%fused_computation.7.clone | custom fusion | bytes 655488 | tf_op jit(solution)/shard_map/jit(_take)/gather | solution.py:50
  145.9 3.6 %scatter_custom_fusion.8 = bf16[1024,640]{1,0:T(8,128)(2,1)} fusion(s32[512]{0:T(512)S(1)} %bitcast.140, bf16[512,640]{1,0:T(8,128)(2,1)S(1)} %bitcast.136, bf16[]{:T(256)} %constant.105.clone.1), kind=kCustom, calls=%fused_computation.51 | custom fusion | bytes 1310722 | tf_op jit(solution)/shard_map/scatter | solution.py:77
  149.5 11.4 %all-to-all-start = ((bf16[64,16,640]{2,1,0:T(8,128)(2,1)}), bf16[64,16,640]{2,1,0:T(8,128)(2,1)S(1)}, u32[]{:S(2)}, u32[]{:S(2)}) async-start(bf16[64,16,640]{2,1,0:T(8,128)(2,1)} %bitcast.33), calls=%async_computation | async-start | bytes 2621440 | tf_op jit(solution)/shard_map/all_to_all | solution.py:78
  161.6 33.0 %all-to-all-done = bf16[64,16,640]{2,1,0:T(8,128)(2,1)S(1)} async-done(((bf16[64,16,640]{2,1,0:T(8,128)(2,1)}), bf16[64,16,640]{2,1,0:T(8,128)(2,1)S(1)}, u32[]{:S(2)}, u32[]{:S(2)}) %all-to-all-start) | async-done | bytes 1310752 | tf_op jit(solution)/shard_map/all_to_all | solution.py:78
  194.5 8.1 %fusion.2 = f32[1024,1024]{1,0:T(8,128)} fusion(bf16[1,1,1024,1024]{3,2,1,0:T(8,128)(2,1)} %all-gather.11.cloned.1.call-done, bf16[1024,640]{1,0:T(8,128)(2,1)S(1)} %bitcast.134, bf16[1,640,1024]{2,1,0:T(8,128)(2,1)} %all-gather.9.cloned.1.call-done), kind=kOutput, calls=%fused_computation.35 | convolution fusion | flops 3494903808 | bytes 8912896 | tf_op jit(solution)/shard_map/dot_general | solution.py:57
  202.7 8.9 %fusion.5 = bf16[1024,640]{1,0:T(8,128)(2,1)} fusion(bf16[1,1024,640]{1,2,0:T(8,128)(2,1)} %all-gather.15.cloned.1.call-done, bf16[1,1,1024,1024]{3,2,1,0:T(8,128)(2,1)} %all-gather.13.cloned.1.call-done, f32[1024,1024]{1,0:T(8,128)} %fusion.2), kind=kOutput, calls=%fused_computation.38 | convolution fusion | flops 3500802048 | bytes 8912896 | tf_op jit(solution)/shard_map/dot_general | solution.py:86
  211.6 7.4 %all-to-all-start.1 = ((bf16[64,16,640]{2,1,0:T(8,128)(2,1)}), bf16[64,16,640]{2,1,0:T(8,128)(2,1)S(1)}, u32[]{:S(2)}, u32[]{:S(2)}) async-start(bf16[64,16,640]{2,1,0:T(8,128)(2,1)} %bitcast.135), calls=%async_computation.1 | async-start | bytes 2621440 | tf_op jit(solution)/shard_map/all_to_all | solution.py:91
  219.2 33.4 %all-to-all-done.1 = bf16[64,16,640]{2,1,0:T(8,128)(2,1)S(1)} async-done(((bf16[64,16,640]{2,1,0:T(8,128)(2,1)}), bf16[64,16,640]{2,1,0:T(8,128)(2,1)S(1)}, u32[]{:S(2)}, u32[]{:S(2)}) %all-to-all-start.1) | async-done | bytes 1310752 | tf_op jit(solution)/shard_map/all_to_all | solution.py:91
  252.6 2.0 gather_fusion.12
  (104 shorter events, 38.8 us)
Async XLA Ops:
  6.5 0.8 copy-start
  6.5 155.0 %all-gather.9.cloned.1.call-start = ((), (), s32[]{:S(2)}) async-start(), calls=%async_computation.2 | async-start | bytes 1638400 | tf_op jit(solution)/shard_map/all_gather | solution.py:82
  7.3 154.3 %all-gather.11.cloned.1.call-start = ((), (), s32[]{:S(2)}) async-start(), calls=%async_computation.3 | async-start | bytes 2621440 | tf_op jit(solution)/shard_map/all_gather | solution.py:85
  10.5 0.7 copy-start.9
  10.9 1.6 copy-start.10
  16.0 6.6 %copy-start.8 = (s32[4]{0:T(128)S(1)}, s32[4]{0:T(128)}, u32[]{:S(2)}) copy-start(s32[4]{0:T(128)} %constant.121) | copy-start | bytes 52
  16.0 43.0 %collective-permute-start = (f32[32,16,640]{2,0,1:T(8,128)S(1)}, f32[32,16,640]{2,0,1:T(8,128)}, u32[]{:S(2)}, u32[]{:S(2)}) collective-permute-start(f32[32,16,640]{2,0,1:T(8,128)S(1)} %scatter_fusion.1), channel_id=1, source_target_pairs={{0,1},{1,2},{2,3},{3,4},{4,5},{5,6},{6,7},{7,8},{8,9},{9,10},{10,1... | collective-permute-start | bytes 3932168 | tf_op jit(solution)/shard_map/ppermute | solution.py:23
  18.1 44.6 %collective-permute-start.1 = (f32[32,16,640]{2,0,1:T(8,128)S(1)}, f32[32,16,640]{2,0,1:T(8,128)S(1)}, u32[]{:S(2)}, u32[]{:S(2)}) collective-permute-start(f32[32,16,640]{2,0,1:T(8,128)S(1)} %scatter_fusion.1), channel_id=1, source_target_pairs={{1,0},{2,1},{3,2},{4,3},{5,4},{6,5},{7,6},{8,7},{9,8},{10,9},{11,1... | collective-permute-start | bytes 3932168 | tf_op jit(solution)/shard_map/ppermute | solution.py:25
  22.3 180.4 %all-gather.15.cloned.1.call-start = ((), (), s32[]{:S(2)}) async-start(), calls=%async_computation.5 | async-start | bytes 1638400 | tf_op jit(solution)/shard_map/all_gather | solution.py:88
  71.5 4.2 %copy-start.3 = (f32[4,32,640]{2,1,0:T(8,128)S(1)}, f32[4,32,640]{2,1,0:T(8,128)}, u32[]{:S(2)}) copy-start(f32[4,32,640]{2,1,0:T(8,128)} %gather_fusion.2) | copy-start | bytes 983044
  74.2 3.3 %copy-start.1 = (f32[4,32,640]{2,1,0:T(8,128)S(1)}, f32[4,32,640]{2,1,0:T(8,128)}, u32[]{:S(2)}) copy-start(f32[4,32,640]{2,1,0:T(8,128)} %gather_fusion.4) | copy-start | bytes 983044
  75.7 1.9 copy-start.5
  76.8 1.5 copy-start.7
  85.4 3.9 %copy-start.6 = (s32[512,1]{0,1:T(1,128)S(1)}, s32[512,1]{0,1:T(1,128)}, u32[]{:S(2)}) copy-start(s32[512,1]{0,1:T(1,128)} %param.40) | copy-start | bytes 6148
  86.2 40.0 %collective-permute-start.2 = (f32[32,16,640]{2,0,1:T(8,128)S(1)}, f32[32,16,640]{2,0,1:T(8,128)}, u32[]{:S(2)}, u32[]{:S(2)}) collective-permute-start(f32[32,16,640]{2,0,1:T(8,128)S(1)} %scatter_fusion.5), channel_id=1, source_target_pairs={{0,1},{1,2},{2,3},{3,4},{4,5},{5,6},{6,7},{7,8},{8,9},{9,10},{10,1... | collective-permute-start | bytes 3932168 | tf_op jit(solution)/shard_map/ppermute | solution.py:23
  86.3 43.5 %collective-permute-start.3 = (f32[32,16,640]{2,0,1:T(8,128)S(1)}, f32[32,16,640]{2,0,1:T(8,128)S(1)}, u32[]{:S(2)}, u32[]{:S(2)}) collective-permute-start(f32[32,16,640]{2,0,1:T(8,128)S(1)} %scatter_fusion.5), channel_id=1, source_target_pairs={{1,0},{2,1},{3,2},{4,3},{5,4},{6,5},{7,6},{8,7},{9,8},{10,9},{11,1... | collective-permute-start | bytes 3932168 | tf_op jit(solution)/shard_map/ppermute | solution.py:25
  141.4 3.4 %copy-start.2 = (f32[4,32,640]{2,1,0:T(8,128)S(1)}, f32[4,32,640]{2,1,0:T(8,128)}, u32[]{:S(2)}) copy-start(f32[4,32,640]{2,1,0:T(8,128)} %gather_fusion.10) | copy-start | bytes 983044
  141.4 3.4 %copy-start.4 = (f32[32,4,640]{2,1,0:T(4,128)S(1)}, f32[32,4,640]{2,1,0:T(4,128)}, u32[]{:S(2)}) copy-start(f32[32,4,640]{2,1,0:T(4,128)} %gather_fusion.20) | copy-start | bytes 983044
  149.5 45.0 %all-to-all-start = ((bf16[64,16,640]{2,1,0:T(8,128)(2,1)}), bf16[64,16,640]{2,1,0:T(8,128)(2,1)S(1)}, u32[]{:S(2)}, u32[]{:S(2)}) async-start(bf16[64,16,640]{2,1,0:T(8,128)(2,1)} %bitcast.33), calls=%async_computation | async-start | bytes 2621440 | tf_op jit(solution)/shard_map/all_to_all | solution.py:78
  160.9 41.7 %all-gather.13.cloned.1.call-start = ((), (), s32[]{:S(2)}) async-start(), calls=%async_computation.4 | async-start | bytes 2621440 | tf_op jit(solution)/shard_map/all_gather | solution.py:85
  211.6 41.0 %all-to-all-start.1 = ((bf16[64,16,640]{2,1,0:T(8,128)(2,1)}), bf16[64,16,640]{2,1,0:T(8,128)(2,1)S(1)}, u32[]{:S(2)}, u32[]{:S(2)}) async-start(bf16[64,16,640]{2,1,0:T(8,128)(2,1)} %bitcast.135), calls=%async_computation.1 | async-start | bytes 2621440 | tf_op jit(solution)/shard_map/all_to_all | solution.py:91
Sparse Core Ops, SparseCore 0:
  9.2 48.2 all-gather.8
  59.3 56.2 all-gather.10
  117.3 33.0 all-gather.14
  163.3 35.1 all-gather.12
where the time goes:
time: 264 us; the launch traced here: 263 us
  waiting for transfers between devices  134 us (51%)
  local copies, waits for them, and re-layouts  61.5 us (23%)
  starting transfers between devices  26.4 us (10%)
  matrix products  22.9 us (9%)
  between operations  13.7 us (5%)
  other arithmetic  4.78 us (2%)
    ppermute x2, waiting for transfers between devices, padded(): lax.ppermute(tail, axis, [(i, (i + 1) % count) for i in range(count)])  66.5 us
    all_to_all x1, waiting for transfers between devices, on_device(): lax.all_to_all(result.reshape(groups, capacity, width), 'elem', split_axi...  33.4 us
    all_to_all x1, waiting for transfers between devices, on_device(): lax.all_to_all(outgoing.reshape(groups, capacity, width), 'elem', split_a...  33 us
    gather x6, local copies, waits for them, and re-layouts, dynamics(): lower_far = jnp.take(margin[:, south_points], above_index, axis=0)  14 us
    all_to_all x1, starting transfers between devices, on_device(): lax.all_to_all(outgoing.reshape(groups, capacity, width), 'elem', split_a...  11.4 us
    gather x6, local copies, waits for them, and re-layouts, dynamics(): upper_far = jnp.take(margin[:, north_points], below_index, axis=0)  9.67 us
    dot_general x1, matrix products, on_device(): jnp.dot(hidden, lax.all_gather(output_proj[0], 'sec', axis=1, tiled=True)...  8.94 us
    dot_general x1, matrix products, activate(): jnp.dot(rows, matrix, preferred_element_type=jnp.float32)  8.13 us
  transfers between devices with their start and end apart: 10, of which 4 were waited for; matrix products, arithmetic and copies ran while one was open for 29% of the time, Pallas kernels for 0%

commit v1 on v0

v1 whole, which is shorter than its diff:
```python
import functools

import jax
import jax.numpy as jnp
from jax import lax
from jax.experimental import pallas as pl
from jax.experimental.pallas import tpu as pltpu
from jax.sharding import PartitionSpec as P

F32 = jnp.float32
BF16 = jnp.bfloat16
POINTS = 16
SIDE = 4
DEVICE_AXES = ("elem", "sec")
NT = (((1,), (1,)), ((), ()))
VMEM_LIMIT = 48 * 1024 * 1024


def iota(shape, axis):
    return lax.broadcasted_iota(jnp.int32, shape, axis)


def ones_where(mask):
    return jnp.where(mask, 1.0, 0.0).astype(BF16)


def mul(a, b):
    return jnp.dot(a, b, preferred_element_type=F32)


def mul_nt(a, b):
    return lax.dot_general(a, b, NT, preferred_element_type=F32)


def halves(x):
    high = x.astype(BF16)
    return high, (x - high.astype(F32)).astype(BF16)


def operator_blocks(op):
    size = POINTS * POINTS
    repeat = ones_where((iota((size, POINTS), 0) & (POINTS - 1)) == iota((size, POINTS), 1))
    same = (iota((size, size), 0) >> 4) == (iota((size, size), 1) >> 4)
    blocks = []
    for part in halves(op):
        tall = mul(repeat, part).astype(BF16)
        blocks.append(jnp.where(same, mul_nt(tall, repeat), 0.0).astype(BF16))
    return blocks


def neighbour_columns(nbt):
    count = nbt.shape[1]
    rows = count * POINTS
    spread = ones_where((iota((rows, count), 0) >> 4) == iota((rows, count), 1))
    local = (nbt & (count - 1)).astype(F32).astype(BF16)
    return mul_nt(spread, local)


def advance(state, op, rates, nbt):
    rows = state.shape[0]
    size = POINTS * POINTS
    op_high, op_low = operator_blocks(op)
    moved = []
    for start in range(0, rows, size):
        high, low = halves(state[start : start + size])
        moved.append(mul(op_high, high) + (mul(op_high, low) + mul(op_low, high)))
    first = state + rates * jnp.concatenate(moved, axis=0)
    near = neighbour_columns(nbt)
    place = iota((rows, 1), 0) & (POINTS - 1)
    column = place & (SIDE - 1)
    west = column == 0
    east = column == SIDE - 1
    placef = place.astype(F32)
    source = jnp.where(
        west,
        near[:, 0:1] * POINTS + placef + (SIDE - 1),
        jnp.where(east, near[:, 1:2] * POINTS + placef - (SIDE - 1), -1.0),
    )
    pick = ones_where(iota((rows, rows), 1).astype(F32) == source)
    high, low = halves(first)
    far = mul(pick, high) + mul(pick, low)
    return jnp.where(west | east, 0.5 * (first + far), first)


def edges(second):
    rows = second.shape[0]
    count = rows // POINTS * SIDE
    j = iota((2 * count, 1), 0)
    k = j & (count - 1)
    source = (k >> 2) * POINTS + (k & (SIDE - 1)) + jnp.where(j < count, POINTS - SIDE, 0)
    pick = ones_where(iota((2 * count, rows), 1) == source)
    return mul(pick, second.astype(BF16)).astype(BF16)


def meet(second, below, above, nbt):
    rows = second.shape[0]
    count = below.shape[0]
    near = neighbour_columns(nbt)
    place = iota((rows, 1), 0) & (POINTS - 1)
    south = place < SIDE
    north = place >= POINTS - SIDE
    placef = place.astype(F32)
    source = jnp.where(
        south,
        near[:, 2:3] * SIDE + placef,
        jnp.where(north, near[:, 3:4] * SIDE + placef + (count - (POINTS - SIDE)), -1.0),
    )
    pick = ones_where(iota((rows, 2 * count), 1).astype(F32) == source)
    far = mul(pick, jnp.concatenate([below, above], axis=0))
    return jnp.where(south | north, 0.5 * (second + far), second)


def start_kernel(state_ref, nbt_ref, op_ref, rates_ref, second_ref, north_ref, south_ref):
    second = advance(state_ref[...], op_ref[...], rates_ref[...], nbt_ref[...])
    second_ref[...] = second
    sides = edges(second)
    count = north_ref.shape[0]
    north_ref[...] = sides[:count]
    south_ref[...] = sides[count:]


def step_kernel(
    prev_ref, below_ref, above_ref, nbt_ref, op_ref, rates_ref, second_ref, north_ref, south_ref
):
    nbt = nbt_ref[...]
    state = meet(prev_ref[...], below_ref[...], above_ref[...], nbt)
    second = advance(state, op_ref[...], rates_ref[...], nbt)
    second_ref[...] = second
    sides = edges(second)
    count = north_ref.shape[0]
    north_ref[...] = sides[:count]
    south_ref[...] = sides[count:]


def send_kernel(capacity, groups, prev_ref, below_ref, above_ref, nbt_ref, ids_ref, state_ref, out_ref):
    state = meet(prev_ref[...], below_ref[...], above_ref[...], nbt_ref[...])
    state_ref[...] = state
    rows = state.shape[0]
    named = iota((groups, rows), 0) == ids_ref[...]
    upto = ones_where(iota((rows, rows), 0) <= iota((rows, rows), 1))
    rank = mul(ones_where(named), upto)
    base = (iota((groups, rows), 0) * capacity - 1).astype(F32)
    slot = jnp.sum(jnp.where(named, base + rank, 0.0), axis=0, keepdims=True)
    pick = ones_where(iota((groups * capacity, rows), 0).astype(F32) == slot)
    out_ref[...] = mul(pick, state.astype(BF16)).astype(BF16)


def add_kernel(capacity, groups, state_ref, back_ref, ids_ref, out_ref):
    rows = state_ref.shape[0]
    same = ones_where(iota((rows, rows), 0) == iota((rows, rows), 1))
    ids = jnp.broadcast_to(ids_ref[...].astype(F32).astype(BF16), (8, rows))
    regime = mul_nt(same, ids)[:, 0:1]
    lanes = iota((rows, groups), 1)
    named = lanes.astype(F32) == regime
    upto = ones_where(iota((rows, rows), 1) <= iota((rows, rows), 0))
    rank = mul(upto, ones_where(named))
    base = (lanes * capacity - 1).astype(F32)
    slot = jnp.sum(jnp.where(named, base + rank, 0.0), axis=1, keepdims=True)
    pick = ones_where(iota((rows, groups * capacity), 1).astype(F32) == slot)
    out_ref[...] = state_ref[...] + mul(pick, back_ref[...])


def silu(v):
    half = 0.5 * v
    return (half + half * jnp.tanh(half)).astype(BF16)


def network_kernel(tile, sec_ref, rows_ref, *refs):
    first, middle, last = refs[0:4], refs[4:8], refs[8:12]
    out_ref, hold_a, hold_b, last_all = refs[12:]
    places = [(sec_ref[0] + k) & 3 for k in range(4)]
    width = first[0].shape[1]
    for k in range(4):
        last_all[places[k]] = last[k][...]

    def body(step, carry):
        at = pl.ds(pl.multiple_of(step * tile, tile), tile)
        rows = rows_ref[at, :]
        for k in range(4):
            spot = pl.ds(pl.multiple_of(places[k] * width, width), width)
            hold_a[:, spot] = silu(mul(rows, first[k][...]))
        now, later = hold_a, hold_b
        for layer in range(middle[0].shape[0]):
            for k in range(4):
                spot = pl.ds(pl.multiple_of(places[k] * width, width), width)
                later[:, spot] = silu(mul(now[...], middle[k][layer]))
            now, later = later, now
        matrix = last_all[...].reshape(out_ref.shape[1], now.shape[1])
        out_ref[at, :] = mul_nt(now[...], matrix).astype(BF16)
        return carry

    lax.fori_loop(0, rows_ref.shape[0] // tile, body, 0)


def call(kernel, out, *args, scratch=(), flops=0, specs=None):
    size = sum(a.size * a.dtype.itemsize for a in args)
    size += sum(o.size * o.dtype.itemsize for o in out)
    vmem = pl.BlockSpec(memory_space=pltpu.VMEM)
    return pl.pallas_call(
        kernel,
        out_shape=out,
        in_specs=specs or [vmem] * len(args),
        out_specs=[vmem] * len(out),
        scratch_shapes=scratch,
        compiler_params=pltpu.CompilerParams(vmem_limit_bytes=VMEM_LIMIT),
        cost_estimate=pl.CostEstimate(flops=flops, bytes_accessed=size, transcendentals=0),
    )(*args)


def ring(count, step):
    return [(i, (i + step) % count) for i in range(count)]


def exchange(north, south):
    total = lax.axis_size(DEVICE_AXES)
    below = lax.ppermute(north, DEVICE_AXES, ring(total, 1))
    above = lax.ppermute(south, DEVICE_AXES, ring(total, -1))
    return below, above


def gathered(shard):
    return [shard] + [lax.ppermute(shard, "sec", ring(4, -k)) for k in (1, 2, 3)]


def on_device(
    fields, neighbours, operator, rates, regime_ids, input_proj, hidden_proj, output_proj
):
    count, points, width = fields.shape
    rows_dev = count * points
    groups = lax.axis_size("elem")
    capacity = 2 * rows_dev // groups
    slots = groups * capacity
    shape = jax.ShapeDtypeStruct
    nbt = neighbours.T
    ids = regime_ids.T
    rate_row = rates.reshape(1, width)

    first = gathered(input_proj[0])
    middle = gathered(hidden_proj[0])
    last = gathered(output_proj[0].T)

    edge = shape((count * SIDE, width), BF16)
    moved = [shape((rows_dev, width), F32), edge, edge]
    second, north, south = call(
        start_kernel, moved, fields.reshape(rows_dev, width), nbt, operator, rate_row, flops=3 * 10**9
    )
    below, above = exchange(north, south)
    second, north, south = call(
        step_kernel, moved, second, below, above, nbt, operator, rate_row, flops=3 * 10**9
    )
    below, above = exchange(north, south)
    state, outgoing = call(
        functools.partial(send_kernel, capacity, groups),
        [shape((rows_dev, width), F32), shape((slots, width), BF16)],
        second, below, above, nbt, ids, flops=3 * 10**9,
    )
    incoming = lax.all_to_all(
        outgoing.reshape(groups, capacity, width), "elem", split_axis=0, concat_axis=0, tiled=True
    )
    hid = hidden_proj.shape[2]
    tile = 512
    vmem = pl.BlockSpec(memory_space=pltpu.VMEM)
    sec = lax.axis_index("sec").astype(jnp.int32).reshape(1)
    (result,) = call(
        functools.partial(network_kernel, tile),
        [shape((slots, width), BF16)],
        sec, incoming.reshape(slots, width), *first, *middle, *last,
        scratch=[
            pltpu.VMEM((tile, hid), BF16),
            pltpu.VMEM((tile, hid), BF16),
            pltpu.VMEM((4, width // 4, hid), BF16),
        ],
        specs=[pl.BlockSpec(memory_space=pltpu.SMEM)] + [vmem] * 13,
        flops=7 * 10**9,
    )
    returned = lax.all_to_all(
        result.reshape(groups, capacity, width), "elem", split_axis=0, concat_axis=0, tiled=True
    )
    (updated,) = call(
        functools.partial(add_kernel, capacity, groups),
        [shape((rows_dev, width), F32)],
        state, returned.reshape(slots, width), ids, flops=10**9,
    )
    return updated.reshape(count, points, width)


def solution(mesh):
    return jax.shard_map(
        on_device,
        mesh=mesh,
        in_specs=(
            P(DEVICE_AXES, None, None),
            P(DEVICE_AXES, None),
            P(),
            P(),
            P(DEVICE_AXES, None),
            P("elem", None, "sec"),
            P("elem", None, None, "sec"),
            P("elem", None, "sec"),
        ),
        out_specs=P(DEVICE_AXES, None, None),
        check_vma=False,
    )
```

time: 264 us -> 204 us (0.77)
  waiting for transfers between devices: 134 us -> 83.1 us
  local copies, waits for them, and re-layouts: 61.5 us -> 12.1 us
  blocking collectives: 0 us -> 44.4 us
  Pallas kernels: 0 us -> 24.3 us
  matrix products: 22.9 us -> 0 us
  between operations: 13.7 us -> 0.08 us
  starting transfers between devices: 26.4 us -> 39 us
  other arithmetic: 4.78 us -> 0 us
    all_to_all x0 -> x1, blocking collectives: none -> 44.4 us  [on_device(): lax.all_to_all(result.reshape(groups, capacity, width), 'elem', split_axi...]
    gather x29 -> x0, local copies, waits for them, and re-layouts: 37 us -> none  [the longest x6 14 us: dynamics(): lower_far = jnp.take(margin[:, south_points], above_index, axis=0)]
    all_to_all x1 -> x0, waiting for transfers between devices: 33.4 us -> none  [on_device(): lax.all_to_all(result.reshape(groups, capacity, width), 'elem', split_axi...]
    all_to_all x1, waiting for transfers between devices: 33 us -> 0.01 us  [on_device(): lax.all_to_all(outgoing.reshape(groups, capacity, width), 'elem', split_a...]
    pallas_call x0 -> x5, Pallas kernels: none -> 24.3 us  [call(): pl.pallas_call(kernel, out_shape=out, in_specs=specs or [vmem] * len(args...]
    dot_general x4 -> x0, matrix products: 22.9 us -> none  [the longest x1 8.94 us: on_device(): jnp.dot(hidden, lax.all_gather(output_proj[0], 'sec', axis=1, tiled=True)...]
    ppermute x4 -> x13, waiting for transfers between devices: 66.5 us -> 83.1 us  [the longest x9 76.3 us: gathered(): lax.ppermute(shard, 'sec', ring(4, -k))]
    ppermute x4 -> x13, starting transfers between devices: 7.08 us -> 21.4 us  [the longest x9 14.4 us: gathered(): lax.ppermute(shard, 'sec', ring(4, -k))]
  transfers between devices with their start and end apart: 10 -> 14, of which waited for: 4 -> 6; matrix products, arithmetic and copies ran while one was open for 29% -> 0% of each run, Pallas kernels for 0% -> 0%
where the time goes in v1:
time: 204 us; the launch traced here: 203 us
  waiting for transfers between devices  83.1 us (41%)
  blocking collectives  44.4 us (22%)
  starting transfers between devices  39 us (19%)
  Pallas kernels  24.3 us (12%)
  local copies, waits for them, and re-layouts  12.1 us (6%)
    ppermute x9, waiting for transfers between devices, gathered(): lax.ppermute(shard, 'sec', ring(4, -k))  76.3 us
    all_to_all x1, blocking collectives, on_device(): lax.all_to_all(result.reshape(groups, capacity, width), 'elem', split_axi...  44.4 us
    pallas_call x5, Pallas kernels, call(): pl.pallas_call(kernel, out_shape=out, in_specs=specs or [vmem] * len(args...  24.3 us
    all_to_all x1, starting transfers between devices, on_device(): lax.all_to_all(outgoing.reshape(groups, capacity, width), 'elem', split_a...  17.6 us
    ppermute x9, starting transfers between devices, gathered(): lax.ppermute(shard, 'sec', ring(4, -k))  14.4 us
    unnamed x32, local copies, waits for them, and re-layouts  11.4 us
    ppermute x2, waiting for transfers between devices, exchange(): below = lax.ppermute(north, DEVICE_AXES, ring(total, 1))  6.76 us
    ppermute x2, starting transfers between devices, exchange(): above = lax.ppermute(south, DEVICE_AXES, ring(total, -1))  4.61 us
  transfers between devices with their start and end apart: 14, of which 6 were waited for; matrix products, arithmetic and copies ran while one was open for 0% of the time, Pallas kernels for 0%

profile of v1, /device:TPU:1, one launch (start us, length us, event | category | flops | bytes accessed | tf_op | source)
XLA Modules:
  0.0 203.0 jit_solution(2192089822244568407)
XLA Ops:
  0.7 1.3 copy-done.1
  3.4 2.7 %shard_map.82 = (f32[512,640]{1,0:T(8,128)S(1)}, bf16[128,640]{1,0:T(8,128)(2,1)S(1)}, bf16[128,640]{1,0:T(8,128)(2,1)S(1)}) custom-call(f32[512,640]{1,0:T(8,128)S(1)} %bitcast.17, s32[4,32]{1,0:T(4,128)S(1)} %bitcast.30, f32[16,16]{1,0:T(8,128)S(1)} %copy-done.13, f32[1,640]{1,0:T(1,128)S(1)} %reshape.25.rates_ref), custom_call_target="tpu_custom_call" | custom-call | flops 3000000000 | bytes 2953216 | tf_op jit(solution)/shard_map/pallas_call | solution.py:199
  6.1 2.1 %collective-permute-start = (bf16[128,640]{1,0:T(8,128)(2,1)S(1)}, bf16[128,640]{1,0:T(8,128)(2,1)S(1)}, u32[]{:S(2)}, u32[]{:S(2)}) collective-permute-start(bf16[128,640]{1,0:T(8,128)(2,1)S(1)} %get-tuple-element.14), channel_id=1, source_target_pairs={{0,1},{1,2},{2,3},{3,4},{4,5},{5,6},{6,7},{7,8},{8,9},{9,10},{10,1... | collective-permute-start | bytes 491528 | tf_op jit(solution)/shard_map/ppermute | solution.py:216
  8.2 1.9 collective-permute-start.1
  10.1 3.8 %collective-permute-done.below_ref = bf16[128,640]{1,0:T(8,128)(2,1)S(1)} collective-permute-done((bf16[128,640]{1,0:T(8,128)(2,1)S(1)}, bf16[128,640]{1,0:T(8,128)(2,1)S(1)}, u32[]{:S(2)}, u32[]{:S(2)}) %collective-permute-start) | collective-permute-done | bytes 163872 | tf_op jit(solution)/shard_map/ppermute | solution.py:216
  13.9 2.9 %shard_map.83 = (f32[512,640]{1,0:T(8,128)S(1)}, bf16[128,640]{1,0:T(8,128)(2,1)S(1)}, bf16[128,640]{1,0:T(8,128)(2,1)S(1)}) custom-call(f32[512,640]{1,0:T(8,128)S(1)} %get-tuple-element.13.prev_ref, bf16[128,640]{1,0:T(8,128)(2,1)S(1)} %collective-permute-done.below_ref, bf16[128,640]{1,0:T(8,128)(2,1)S(1)} %collective-permute-done.1.above_ref, ...), custom_call_target="tpu_custom_call" | custom-call | flops 3000000000 | bytes 3280896 | tf_op jit(solution)/shard_map/pallas_call | solution.py:199
  17.2 2.7 %collective-permute-start.3 = (bf16[128,640]{1,0:T(8,128)(2,1)S(1)}, bf16[128,640]{1,0:T(8,128)(2,1)S(1)}, u32[]{:S(2)}, u32[]{:S(2)}) collective-permute-start(bf16[128,640]{1,0:T(8,128)(2,1)S(1)} %get-tuple-element.18), channel_id=1, source_target_pairs={{0,255},{1,0},{2,1},{3,2},{4,3},{5,4},{6,5},{7,6},{8,7},{9,8},{10,... | collective-permute-start | bytes 491528 | tf_op jit(solution)/shard_map/ppermute | solution.py:217
  19.9 3.0 %collective-permute-done.2.below_ref = bf16[128,640]{1,0:T(8,128)(2,1)S(1)} collective-permute-done((bf16[128,640]{1,0:T(8,128)(2,1)S(1)}, bf16[128,640]{1,0:T(8,128)(2,1)S(1)}, u32[]{:S(2)}, u32[]{:S(2)}) %collective-permute-start.2) | collective-permute-done | bytes 163872 | tf_op jit(solution)/shard_map/ppermute | solution.py:216
  22.9 2.8 %shard_map.84 = (f32[512,640]{1,0:T(8,128)S(1)}, bf16[1024,640]{1,0:T(8,128)(2,1)}) custom-call(f32[512,640]{1,0:T(8,128)S(1)} %get-tuple-element.16.prev_ref, bf16[128,640]{1,0:T(8,128)(2,1)S(1)} %collective-permute-done.2.below_ref, bf16[128,640]{1,0:T(8,128)(2,1)S(1)} %collective-permute-done.3.above_ref, s32[4,32]{1,0:T(4,128)S(1)} %bitcast.32, ...), custom_call_target="tpu_custom_call" | custom-call | flops 3000000000 | bytes 4262400 | tf_op jit(solution)/shard_map/pallas_call | solution.py:199
  25.7 17.6 %all-to-all-start = ((bf16[64,16,640]{2,1,0:T(8,128)(2,1)}), bf16[64,16,640]{2,1,0:T(8,128)(2,1)}, u32[]{:S(2)}, u32[]{:S(2)}) async-start(bf16[64,16,640]{2,1,0:T(8,128)(2,1)} %bitcast.4), calls=%async_computation | async-start | bytes 2621440 | tf_op jit(solution)/shard_map/all_to_all | solution.py:257
  43.3 4.9 %collective-permute-start.7 = (bf16[2,1024,256]{2,1,0:T(8,128)(2,1)S(1)}, bf16[2,1024,256]{2,1,0:T(8,128)(2,1)S(1)}, u32[]{:S(2)}, u32[]{:S(2)}) collective-permute-start(bf16[2,1024,256]{2,1,0:T(8,128)(2,1)S(1)} %bitcast.18), channel_id=1, source_target_pairs={{0,3},{1,0},{2,1},{3,2},{4,7},{5,4},{6,5},{7,6},{8,11},{9,8},{10,9... | collective-permute-start | bytes 3145736 | tf_op jit(solution)/shard_map/ppermute | solution.py:222
  48.8 2.0 collective-permute-start.4
  50.8 1.8 collective-permute-start.5
  52.6 54.2 %collective-permute-done.4.refs_1_ = bf16[640,256]{1,0:T(8,128)(2,1)S(1)} collective-permute-done((bf16[640,256]{1,0:T(8,128)(2,1)}, bf16[640,256]{1,0:T(8,128)(2,1)S(1)}, u32[]{:S(2)}, u32[]{:S(2)}) %collective-permute-start.4) | collective-permute-done | bytes 327712 | tf_op jit(solution)/shard_map/ppermute | solution.py:222
  108.2 3.3 %collective-permute-start.10 = (bf16[160,1024]{1,0:T(8,128)(2,1)}, bf16[160,1024]{1,0:T(8,128)(2,1)S(1)}, u32[]{:S(2)}, u32[]{:S(2)}) collective-permute-start(bf16[160,1024]{1,0:T(8,128)(2,1)} %bitcast.26), channel_id=1, source_target_pairs={{0,3},{1,0},{2,1},{3,2},{4,7},{5,4},{6,5},{7,6},{8,11},{9,8},{10,9... | collective-permute-start | bytes 983048 | tf_op jit(solution)/shard_map/ppermute | solution.py:222
  111.5 6.1 %collective-permute-done.6.refs_3_ = bf16[640,256]{1,0:T(8,128)(2,1)S(1)} collective-permute-done((bf16[640,256]{1,0:T(8,128)(2,1)}, bf16[640,256]{1,0:T(8,128)(2,1)S(1)}, u32[]{:S(2)}, u32[]{:S(2)}) %collective-permute-start.6) | collective-permute-done | bytes 327712 | tf_op jit(solution)/shard_map/ppermute | solution.py:222
  119.4 1.5 collective-permute-start.12
  120.8 6.6 %collective-permute-done.11.refs_10_ = bf16[160,1024]{1,0:T(8,128)(2,1)} collective-permute-done((bf16[160,1024]{1,0:T(8,128)(2,1)}, bf16[160,1024]{1,0:T(8,128)(2,1)}, u32[]{:S(2)}, u32[]{:S(2)}) %collective-permute-start.11) | collective-permute-done | bytes 327712 | tf_op jit(solution)/shard_map/ppermute | solution.py:222
  127.4 9.4 %collective-permute-done.12.refs_11_ = bf16[160,1024]{1,0:T(8,128)(2,1)} collective-permute-done((bf16[160,1024]{1,0:T(8,128)(2,1)}, bf16[160,1024]{1,0:T(8,128)(2,1)}, u32[]{:S(2)}, u32[]{:S(2)}) %collective-permute-start.12) | collective-permute-done | bytes 327712 | tf_op jit(solution)/shard_map/ppermute | solution.py:222
  137.8 1.0 copy-done.4
  138.8 1.0 copy-done.6
  142.7 13.1 %shard_map.85 = bf16[1024,640]{1,0:T(8,128)(2,1)} custom-call(s32[1]{0:T(128)} %bitcast.3.sec_ref, bf16[1024,640]{1,0:T(8,128)(2,1)} %bitcast.5.rows_ref, bf16[640,256]{1,0:T(8,128)(2,1)S(1)} %bitcast.25, bf16[640,256]{1,0:T(8,128)(2,1)S(1)} %copy-done.6, bf16[640,256]{1,0:T(8,128)(2,1)S(1)} %copy-done.8, bf16[640,256]{1,0:T(8,128)(2,1)S(1)} %copy-done.10, ...), custom_call_target="tpu_custom_call" | custom-call | flops 7000000000 | bytes 9437188 | tf_op jit(solution)/shard_map/pallas_call | solution.py:199
  155.8 44.4 %all_to_all.10 = bf16[64,16,640]{2,1,0:T(8,128)(2,1)S(1)} all-to-all(bf16[64,16,640]{2,1,0:T(8,128)(2,1)} %bitcast.33), channel_id=1, replica_groups=mesh['elem'=64,'sec'=4] {'elem'}, dimensions={0} | all-to-all | bytes 2621440 | tf_op jit(solution)/shard_map/all_to_all | solution.py:276
  200.2 2.8 %shard_map.86 = f32[512,640]{1,0:T(8,128)} custom-call(f32[512,640]{1,0:T(8,128)S(1)} %get-tuple-element.19.state_ref, bf16[1024,640]{1,0:T(8,128)(2,1)S(1)} %bitcast.14, s32[1,512]{1,0:T(1,128)S(1)} %bitcast.16), custom_call_target="tpu_custom_call" | custom-call | flops 1000000000 | bytes 3934208 | tf_op jit(solution)/shard_map/pallas_call | solution.py:199
  (43 shorter events, 10.2 us)
Async XLA Ops:
  0.7 1.3 copy-start.1
  3.4 10.5 %copy-start.15 = (s32[32,4]{0,1:T(4,128)S(1)}, s32[32,4]{0,1:T(4,128)}, u32[]{:S(2)}) copy-start(s32[32,4]{0,1:T(4,128)} %param.9) | copy-start | bytes 1540
  6.1 7.8 %collective-permute-start = (bf16[128,640]{1,0:T(8,128)(2,1)S(1)}, bf16[128,640]{1,0:T(8,128)(2,1)S(1)}, u32[]{:S(2)}, u32[]{:S(2)}) collective-permute-start(bf16[128,640]{1,0:T(8,128)(2,1)S(1)} %get-tuple-element.14), channel_id=1, source_target_pairs={{0,1},{1,2},{2,3},{3,4},{4,5},{5,6},{6,7},{7,8},{8,9},{9,10},{10,1... | collective-permute-start | bytes 491528 | tf_op jit(solution)/shard_map/ppermute | solution.py:216
  8.2 5.7 %collective-permute-start.1 = (bf16[128,640]{1,0:T(8,128)(2,1)S(1)}, bf16[128,640]{1,0:T(8,128)(2,1)S(1)}, u32[]{:S(2)}, u32[]{:S(2)}) collective-permute-start(bf16[128,640]{1,0:T(8,128)(2,1)S(1)} %get-tuple-element.15), channel_id=1, source_target_pairs={{0,255},{1,0},{2,1},{3,2},{4,3},{5,4},{6,5},{7,6},{8,7},{9,8},{10,... | collective-permute-start | bytes 491528 | tf_op jit(solution)/shard_map/ppermute | solution.py:217
  13.9 8.9 %copy-start = (s32[512,1]{0,1:T(1,128)S(1)}, s32[512,1]{0,1:T(1,128)}, u32[]{:S(2)}) copy-start(s32[512,1]{0,1:T(1,128)} %param.12) | copy-start | bytes 6148
  16.8 6.0 %collective-permute-start.2 = (bf16[128,640]{1,0:T(8,128)(2,1)S(1)}, bf16[128,640]{1,0:T(8,128)(2,1)S(1)}, u32[]{:S(2)}, u32[]{:S(2)}) collective-permute-start(bf16[128,640]{1,0:T(8,128)(2,1)S(1)} %get-tuple-element.17), channel_id=1, source_target_pairs={{0,1},{1,2},{2,3},{3,4},{4,5},{5,6},{6,7},{7,8},{8,9},{9,10},{10,1... | collective-permute-start | bytes 491528 | tf_op jit(solution)/shard_map/ppermute | solution.py:216
  17.2 5.7 %collective-permute-start.3 = (bf16[128,640]{1,0:T(8,128)(2,1)S(1)}, bf16[128,640]{1,0:T(8,128)(2,1)S(1)}, u32[]{:S(2)}, u32[]{:S(2)}) collective-permute-start(bf16[128,640]{1,0:T(8,128)(2,1)S(1)} %get-tuple-element.18), channel_id=1, source_target_pairs={{0,255},{1,0},{2,1},{3,2},{4,3},{5,4},{6,5},{7,6},{8,7},{9,8},{10,... | collective-permute-start | bytes 491528 | tf_op jit(solution)/shard_map/ppermute | solution.py:217
  25.7 17.6 %copy-start.2 = (bf16[1,2,1024,256]{3,2,1,0:T(8,128)(2,1)S(1)}, bf16[1,2,1024,256]{3,2,1,0:T(8,128)(2,1)}, u32[]{:S(2)}) copy-start(bf16[1,2,1024,256]{3,2,1,0:T(8,128)(2,1)} %param.14) | copy-start | bytes 3145732
  25.7 111.2 %all-to-all-start = ((bf16[64,16,640]{2,1,0:T(8,128)(2,1)}), bf16[64,16,640]{2,1,0:T(8,128)(2,1)}, u32[]{:S(2)}, u32[]{:S(2)}) async-start(bf16[64,16,640]{2,1,0:T(8,128)(2,1)} %bitcast.4), calls=%async_computation | async-start | bytes 2621440 | tf_op jit(solution)/shard_map/all_to_all | solution.py:257
  43.3 93.6 %collective-permute-start.7 = (bf16[2,1024,256]{2,1,0:T(8,128)(2,1)S(1)}, bf16[2,1024,256]{2,1,0:T(8,128)(2,1)S(1)}, u32[]{:S(2)}, u32[]{:S(2)}) collective-permute-start(bf16[2,1024,256]{2,1,0:T(8,128)(2,1)S(1)} %bitcast.18), channel_id=1, source_target_pairs={{0,3},{1,0},{2,1},{3,2},{4,7},{5,4},{6,5},{7,6},{8,11},{9,8},{10,9... | collective-permute-start | bytes 3145736 | tf_op jit(solution)/shard_map/ppermute | solution.py:222
  48.1 88.7 %collective-permute-start.8 = (bf16[2,1024,256]{2,1,0:T(8,128)(2,1)S(1)}, bf16[2,1024,256]{2,1,0:T(8,128)(2,1)}, u32[]{:S(2)}, u32[]{:S(2)}) collective-permute-start(bf16[2,1024,256]{2,1,0:T(8,128)(2,1)S(1)} %bitcast.19), channel_id=1, source_target_pairs={{0,2},{1,3},{2,0},{3,1},{4,6},{5,7},{6,4},{7,5},{8,10},{9,11},{10,... | collective-permute-start | bytes 3145736 | tf_op jit(solution)/shard_map/ppermute | solution.py:222
  48.1 88.7 %collective-permute-start.9 = (bf16[2,1024,256]{2,1,0:T(8,128)(2,1)S(1)}, bf16[2,1024,256]{2,1,0:T(8,128)(2,1)}, u32[]{:S(2)}, u32[]{:S(2)}) collective-permute-start(bf16[2,1024,256]{2,1,0:T(8,128)(2,1)S(1)} %bitcast.20), channel_id=1, source_target_pairs={{0,1},{1,2},{2,3},{3,0},{4,5},{5,6},{6,7},{7,4},{8,9},{9,10},{10,1... | collective-permute-start | bytes 3145736 | tf_op jit(solution)/shard_map/ppermute | solution.py:222
  48.8 57.9 %collective-permute-start.4 = (bf16[640,256]{1,0:T(8,128)(2,1)}, bf16[640,256]{1,0:T(8,128)(2,1)S(1)}, u32[]{:S(2)}, u32[]{:S(2)}) collective-permute-start(bf16[640,256]{1,0:T(8,128)(2,1)} %bitcast.22), channel_id=1, source_target_pairs={{0,3},{1,0},{2,1},{3,2},{4,7},{5,4},{6,5},{7,6},{8,11},{9,8},{10,9... | collective-permute-start | bytes 983048 | tf_op jit(solution)/shard_map/ppermute | solution.py:222
  50.8 56.7 %collective-permute-start.5 = (bf16[640,256]{1,0:T(8,128)(2,1)}, bf16[640,256]{1,0:T(8,128)(2,1)S(1)}, u32[]{:S(2)}, u32[]{:S(2)}) collective-permute-start(bf16[640,256]{1,0:T(8,128)(2,1)} %bitcast.23), channel_id=1, source_target_pairs={{0,2},{1,3},{2,0},{3,1},{4,6},{5,7},{6,4},{7,5},{8,10},{9,11},{10,... | collective-permute-start | bytes 983048 | tf_op jit(solution)/shard_map/ppermute | solution.py:222
  107.5 10.2 %collective-permute-start.6 = (bf16[640,256]{1,0:T(8,128)(2,1)}, bf16[640,256]{1,0:T(8,128)(2,1)S(1)}, u32[]{:S(2)}, u32[]{:S(2)}) collective-permute-start(bf16[640,256]{1,0:T(8,128)(2,1)} %bitcast.24), channel_id=1, source_target_pairs={{0,1},{1,2},{2,3},{3,0},{4,5},{5,6},{6,7},{7,4},{8,9},{9,10},{10,1... | collective-permute-start | bytes 983048 | tf_op jit(solution)/shard_map/ppermute | solution.py:222
  108.2 10.4 %collective-permute-start.10 = (bf16[160,1024]{1,0:T(8,128)(2,1)}, bf16[160,1024]{1,0:T(8,128)(2,1)S(1)}, u32[]{:S(2)}, u32[]{:S(2)}) collective-permute-start(bf16[160,1024]{1,0:T(8,128)(2,1)} %bitcast.26), channel_id=1, source_target_pairs={{0,3},{1,0},{2,1},{3,2},{4,7},{5,4},{6,5},{7,6},{8,11},{9,8},{10,9... | collective-permute-start | bytes 983048 | tf_op jit(solution)/shard_map/ppermute | solution.py:222
  118.4 9.1 %collective-permute-start.11 = (bf16[160,1024]{1,0:T(8,128)(2,1)}, bf16[160,1024]{1,0:T(8,128)(2,1)}, u32[]{:S(2)}, u32[]{:S(2)}) collective-permute-start(bf16[160,1024]{1,0:T(8,128)(2,1)} %bitcast.27), channel_id=1, source_target_pairs={{0,2},{1,3},{2,0},{3,1},{4,6},{5,7},{6,4},{7,5},{8,10},{9,11},{10,... | collective-permute-start | bytes 983048 | tf_op jit(solution)/shard_map/ppermute | solution.py:222
  119.4 17.5 %collective-permute-start.12 = (bf16[160,1024]{1,0:T(8,128)(2,1)}, bf16[160,1024]{1,0:T(8,128)(2,1)}, u32[]{:S(2)}, u32[]{:S(2)}) collective-permute-start(bf16[160,1024]{1,0:T(8,128)(2,1)} %bitcast.28), channel_id=1, source_target_pairs={{0,1},{1,2},{2,3},{3,0},{4,5},{5,6},{6,7},{7,4},{8,9},{9,10},{10,1... | collective-permute-start | bytes 983048 | tf_op jit(solution)/shard_map/ppermute | solution.py:222
  136.9 1.0 copy-start.3
  137.8 1.0 copy-start.4
  138.8 1.0 copy-start.6
  139.8 1.0 copy-start.8
  140.7 1.0 copy-start.10
  141.7 1.0 copy-start.12
  (6 other events, 4.3 us)

commit v2 on v1

--- a/solution.py
+++ b/solution.py
@@ -13,7 +13,7 @@
 SIDE = 4
 DEVICE_AXES = ("elem", "sec")
 NT = (((1,), (1,)), ((), ()))
-VMEM_LIMIT = 48 * 1024 * 1024
+VMEM_LIMIT = 40 * 1024 * 1024
 
 
 def iota(shape, axis):
@@ -110,8 +110,16 @@
     return jnp.where(south | north, 0.5 * (second + far), second)
 
 
-def start_kernel(state_ref, nbt_ref, op_ref, rates_ref, second_ref, north_ref, south_ref):
-    second = advance(state_ref[...], op_ref[...], rates_ref[...], nbt_ref[...])
+def start_kernel(
+    state_ref, nbt_ref, op_ref, rates_ref, second_ref, north_ref, south_ref, state, nbt, op, rates, sems
+):
+    pairs = [(state_ref, state), (nbt_ref, nbt), (op_ref, op), (rates_ref, rates)]
+    copies = [pltpu.make_async_copy(a, b, sems.at[i]) for i, (a, b) in enumerate(pairs)]
+    for copy in copies:
+        copy.start()
+    for copy in copies:
+        copy.wait()
+    second = advance(state[...], op[...], rates[...].reshape(1, -1), nbt[...])
     second_ref[...] = second
     sides = edges(second)
     count = north_ref.shape[0]
@@ -120,11 +128,12 @@
 
 
 def step_kernel(
-    prev_ref, below_ref, above_ref, nbt_ref, op_ref, rates_ref, second_ref, north_ref, south_ref
+    prev_ref, below_ref, above_ref, nbt_ref, op_ref, rates_ref, *refs
 ):
+    second_ref, north_ref, south_ref = refs[-3:]
     nbt = nbt_ref[...]
     state = meet(prev_ref[...], below_ref[...], above_ref[...], nbt)
-    second = advance(state, op_ref[...], rates_ref[...], nbt)
+    second = advance(state, op_ref[...], rates_ref[...].reshape(1, -1), nbt)
     second_ref[...] = second
     sides = edges(second)
     count = north_ref.shape[0]
@@ -132,7 +141,8 @@
     south_ref[...] = sides[count:]
 
 
-def send_kernel(capacity, groups, prev_ref, below_ref, above_ref, nbt_ref, ids_ref, state_ref, out_ref):
+def send_kernel(capacity, groups, prev_ref, below_ref, above_ref, nbt_ref, ids_ref, *refs):
+    state_ref, out_ref = refs[-2:]
     state = meet(prev_ref[...], below_ref[...], above_ref[...], nbt_ref[...])
     state_ref[...] = state
     rows = state.shape[0]
@@ -166,45 +176,58 @@
 
 
 def network_kernel(tile, sec_ref, rows_ref, *refs):
-    first, middle, last = refs[0:4], refs[4:8], refs[8:12]
-    out_ref, hold_a, hold_b, last_all = refs[12:]
+    shards, out_ref = refs[0:12], refs[12]
+    first, middle, last, hold_a, hold_b, sems = refs[13:]
+    layers = middle.shape[1]
     places = [(sec_ref[0] + k) & 3 for k in range(4)]
-    width = first[0].shape[1]
+    width = first.shape[2]
+    waits = [[] for _ in range(layers + 2)]
     for k in range(4):
-        last_all[places[k]] = last[k][...]
-
-    def body(step, carry):
-        at = pl.ds(pl.multiple_of(step * tile, tile), tile)
-        rows = rows_ref[at, :]
+        pairs = [(shards[k], first.at[k], 0)]
+        pairs += [(shards[4 + k].at[layer], middle.at[k, layer], 1 + layer) for layer in range(layers)]
+        pairs += [(shards[8 + k], last.at[places[k]], 1 + layers)]
+        for source, target, group in pairs:
+            waits[group].append(pltpu.make_async_copy(source, target, sems.at[k, group]))
+    for group in waits:
+        for copy in group:
+            copy.start()
+
+    def arrived(start, group):
+        if start == 0:
+            for copy in waits[group]:
+                copy.wait()
+
+    for start in range(0, rows_ref.shape[0], tile):
+        rows = rows_ref[start : start + tile]
+        arrived(start, 0)
         for k in range(4):
             spot = pl.ds(pl.multiple_of(places[k] * width, width), width)
-            hold_a[:, spot] = silu(mul(rows, first[k][...]))
+            hold_a[:, spot] = silu(mul(rows, first[k]))
         now, later = hold_a, hold_b
-        for layer in range(middle[0].shape[0]):
+        for layer in range(layers):
+            arrived(start, 1 + layer)
             for k in range(4):
                 spot = pl.ds(pl.multiple_of(places[k] * width, width), width)
-                later[:, spot] = silu(mul(now[...], middle[k][layer]))
+                later[:, spot] = silu(mul(now[...], middle[k, layer]))
             now, later = later, now
-        matrix = last_all[...].reshape(out_ref.shape[1], now.shape[1])
-        out_ref[at, :] = mul_nt(now[...], matrix).astype(BF16)
-        return carry
-
-    lax.fori_loop(0, rows_ref.shape[0] // tile, body, 0)
-
-
-def call(kernel, out, *args, scratch=(), flops=0, specs=None):
+        arrived(start, 1 + layers)
+        matrix = last[...].reshape(out_ref.shape[1], now.shape[1])
+        out_ref[start : start + tile] = mul_nt(now[...], matrix).astype(BF16)
+
+
+def call(kernel, out, *args, passed=(), scratch=(), flops=0, specs=None, limit=VMEM_LIMIT):
     size = sum(a.size * a.dtype.itemsize for a in args)
     size += sum(o.size * o.dtype.itemsize for o in out)
     vmem = pl.BlockSpec(memory_space=pltpu.VMEM)
     return pl.pallas_call(
         kernel,
         out_shape=out,
-        in_specs=specs or [vmem] * len(args),
+        in_specs=(specs or [vmem] * len(args)) + [pl.BlockSpec(memory_space=pl.ANY)] * len(passed),
         out_specs=[vmem] * len(out),
         scratch_shapes=scratch,
-        compiler_params=pltpu.CompilerParams(vmem_limit_bytes=VMEM_LIMIT),
+        compiler_params=pltpu.CompilerParams(vmem_limit_bytes=limit),
         cost_estimate=pl.CostEstimate(flops=flops, bytes_accessed=size, transcendentals=0),
-    )(*args)
+    )(*args, *passed)
 
 
 def ring(count, step):
@@ -233,7 +256,6 @@
     shape = jax.ShapeDtypeStruct
     nbt = neighbours.T
     ids = regime_ids.T
-    rate_row = rates.reshape(1, width)
 
     first = gathered(input_proj[0])
     middle = gathered(hidden_proj[0])
@@ -242,17 +264,27 @@
     edge = shape((count * SIDE, width), BF16)
     moved = [shape((rows_dev, width), F32), edge, edge]
     second, north, south = call(
-        start_kernel, moved, fields.reshape(rows_dev, width), nbt, operator, rate_row, flops=3 * 10**9
+        start_kernel, moved, fields.reshape(rows_dev, width), nbt, operator, rates,
+        scratch=[
+            pltpu.VMEM((rows_dev, width), F32),
+            pltpu.VMEM(nbt.shape, jnp.int32),
+            pltpu.VMEM(operator.shape, F32),
+            pltpu.VMEM(rates.shape, F32),
+            pltpu.SemaphoreType.DMA((4,)),
+        ],
+        specs=[pl.BlockSpec(memory_space=pl.ANY)] * 4,
+        limit=58 * 1024 * 1024,
+        flops=3 * 10**9,
     )
     below, above = exchange(north, south)
     second, north, south = call(
-        step_kernel, moved, second, below, above, nbt, operator, rate_row, flops=3 * 10**9
+        step_kernel, moved, second, below, above, nbt, operator, rates, passed=first[1:], flops=3 * 10**9
     )
     below, above = exchange(north, south)
     state, outgoing = call(
         functools.partial(send_kernel, capacity, groups),
         [shape((rows_dev, width), F32), shape((slots, width), BF16)],
-        second, below, above, nbt, ids, flops=3 * 10**9,
+        second, below, above, nbt, ids, passed=last[1:], flops=3 * 10**9,
     )
     incoming = lax.all_to_all(
         outgoing.reshape(groups, capacity, width), "elem", split_axis=0, concat_axis=0, tiled=True
@@ -266,11 +298,15 @@
         [shape((slots, width), BF16)],
         sec, incoming.reshape(slots, width), *first, *middle, *last,
         scratch=[
+            pltpu.VMEM((4, *input_proj.shape[1:2], hid // 4), BF16),
+            pltpu.VMEM((4, *hidden_proj.shape[1:3], hid // 4), BF16),
+            pltpu.VMEM((4, width // 4, hid), BF16),
             pltpu.VMEM((tile, hid), BF16),
             pltpu.VMEM((tile, hid), BF16),
-            pltpu.VMEM((4, width // 4, hid), BF16),
+            pltpu.SemaphoreType.DMA((4, 2 + hidden_proj.shape[1])),
         ],
-        specs=[pl.BlockSpec(memory_space=pltpu.SMEM)] + [vmem] * 13,
+        specs=[pl.BlockSpec(memory_space=pltpu.SMEM), vmem] + [pl.BlockSpec(memory_space=pl.ANY)] * 12,
+        limit=55 * 1024 * 1024,
         flops=7 * 10**9,
     )
     returned = lax.all_to_all(

time: 204 us -> 174 us (0.85)
  waiting for transfers between devices: 83.1 us -> 71.7 us
  starting transfers between devices: 39 us -> 27.7 us
  local copies, waits for them, and re-layouts: 12.1 us -> 2.61 us
  Pallas kernels: 24.3 us -> 26.8 us
    ppermute x9, waiting for transfers between devices: 76.3 us -> 56.5 us  [gathered(): lax.ppermute(shard, 'sec', ring(4, -k))]
    unnamed x32 -> x26, local copies, waits for them, and re-layouts: 11.4 us -> 2.61 us
    ppermute x2, waiting for transfers between devices: 6.76 us -> 15.2 us  [exchange(): below = lax.ppermute(north, DEVICE_AXES, ring(total, 1))]
    ppermute x9, starting transfers between devices: 14.4 us -> 8.01 us  [gathered(): lax.ppermute(shard, 'sec', ring(4, -k))]
    all_to_all x1, starting transfers between devices: 17.6 us -> 12.3 us  [on_device(): lax.all_to_all(outgoing.reshape(groups, capacity, width), 'elem', split_a...]
    pallas_call x5, Pallas kernels: 24.3 us -> 26.8 us  [call(): pl.pallas_call(kernel, out_shape=out, in_specs=(specs or [vmem] * len(arg...]
  transfers between devices with their start and end apart: 14 -> 14, of which waited for: 6 -> 6; matrix products, arithmetic and copies ran while one was open for 0% -> 0% of each run, Pallas kernels for 0% -> 5%
where the time goes in v2:
time: 174 us; the launch traced here: 173 us
  waiting for transfers between devices  71.7 us (41%)
  blocking collectives  44.4 us (26%)
  starting transfers between devices  27.7 us (16%)
  Pallas kernels  26.8 us (15%)
  local copies, waits for them, and re-layouts  2.61 us (2%)
    ppermute x9, waiting for transfers between devices, gathered(): lax.ppermute(shard, 'sec', ring(4, -k))  56.5 us
    all_to_all x1, blocking collectives, on_device(): lax.all_to_all(result.reshape(groups, capacity, width), 'elem', split_axi...  44.4 us
    pallas_call x5, Pallas kernels, call(): pl.pallas_call(kernel, out_shape=out, in_specs=(specs or [vmem] * len(arg...  26.8 us
    ppermute x2, waiting for transfers between devices, exchange(): below = lax.ppermute(north, DEVICE_AXES, ring(total, 1))  15.2 us
    all_to_all x1, starting transfers between devices, on_device(): lax.all_to_all(outgoing.reshape(groups, capacity, width), 'elem', split_a...  12.3 us
    ppermute x9, starting transfers between devices, gathered(): lax.ppermute(shard, 'sec', ring(4, -k))  8.01 us
    ppermute x2, starting transfers between devices, exchange(): above = lax.ppermute(south, DEVICE_AXES, ring(total, -1))  4.52 us
  transfers between devices with their start and end apart: 14, of which 6 were waited for; matrix products, arithmetic and copies ran while one was open for 0% of the time, Pallas kernels for 5%

profile of v2, /device:TPU:1, one launch (start us, length us, event | category | flops | bytes accessed | tf_op | source)
XLA Modules:
  0.0 173.4 jit_solution(620218514557361368)
XLA Ops:
  0.0 3.3 %collective-permute-start.2 = (bf16[640,256]{1,0:T(8,128)(2,1)}, bf16[640,256]{1,0:T(8,128)(2,1)S(1)}, u32[]{:S(2)}, u32[]{:S(2)}) collective-permute-start(bf16[640,256]{1,0:T(8,128)(2,1)} %bitcast.27), channel_id=1, source_target_pairs={{0,3},{1,0},{2,1},{3,2},{4,7},{5,4},{6,5},{7,6},{8,11},{9,8},{10,9... | collective-permute-start | bytes 983048 | tf_op jit(solution)/shard_map/ppermute | solution.py:245
  4.4 5.0 %shard_map.82 = (f32[512,640]{1,0:T(8,128)}, bf16[128,640]{1,0:T(8,128)(2,1)}, bf16[128,640]{1,0:T(8,128)(2,1)}) custom-call(f32[512,640]{1,0:T(8,128)} %bitcast.22, s32[4,32]{1,0:T(4,128)} %bitcast.17, f32[16,16]{1,0:T(8,128)} %op_ref.3, f32[640]{0:T(1024)} %rates_ref.3), custom_call_target="tpu_custom_call" | custom-call | flops 3000000000 | bytes 2953216 | tf_op jit(solution)/shard_map/pallas_call | solution.py:222
  9.5 1.6 collective-permute-start
  11.1 2.0 %collective-permute-start.1 = (bf16[128,640]{1,0:T(8,128)(2,1)}, bf16[128,640]{1,0:T(8,128)(2,1)S(1)}, u32[]{:S(2)}, u32[]{:S(2)}) collective-permute-start(bf16[128,640]{1,0:T(8,128)(2,1)} %get-tuple-element.15), channel_id=1, source_target_pairs={{0,255},{1,0},{2,1},{3,2},{4,3},{5,4},{6,5},{7,6},{8,7},{9,8},{10,... | collective-permute-start | bytes 491528 | tf_op jit(solution)/shard_map/ppermute | solution.py:240
  13.1 11.9 %collective-permute-done.below_ref = bf16[128,640]{1,0:T(8,128)(2,1)S(1)} collective-permute-done((bf16[128,640]{1,0:T(8,128)(2,1)}, bf16[128,640]{1,0:T(8,128)(2,1)S(1)}, u32[]{:S(2)}, u32[]{:S(2)}) %collective-permute-start) | collective-permute-done | bytes 163872 | tf_op jit(solution)/shard_map/ppermute | solution.py:239
  25.0 0.8 collective-permute-start.8
  25.8 0.8 collective-permute-start.9
  26.6 1.5 copy-done.10
  28.2 2.9 %shard_map.83 = (f32[512,640]{1,0:T(8,128)S(1)}, bf16[128,640]{1,0:T(8,128)(2,1)S(1)}, bf16[128,640]{1,0:T(8,128)(2,1)S(1)}) custom-call(f32[512,640]{1,0:T(8,128)S(1)} %copy-done.10, bf16[128,640]{1,0:T(8,128)(2,1)S(1)} %collective-permute-done.below_ref, bf16[128,640]{1,0:T(8,128)(2,1)S(1)} %collective-permute-done.1.above_ref, s32[4,32]{1,0:T(4,128)S(1)} %bitcast.18, ...), custom_call_target="tpu_custom_call" | custom-call | flops 3000000000 | bytes 3280896 | tf_op jit(solution)/shard_map/pallas_call | solution.py:222
  31.1 1.3 collective-permute-start.5
  32.3 2.5 %collective-permute-start.6 = (bf16[128,640]{1,0:T(8,128)(2,1)S(1)}, bf16[128,640]{1,0:T(8,128)(2,1)S(1)}, u32[]{:S(2)}, u32[]{:S(2)}) collective-permute-start(bf16[128,640]{1,0:T(8,128)(2,1)S(1)} %get-tuple-element.18), channel_id=1, source_target_pairs={{0,255},{1,0},{2,1},{3,2},{4,3},{5,4},{6,5},{7,6},{8,7},{9,8},{10,... | collective-permute-start | bytes 491528 | tf_op jit(solution)/shard_map/ppermute | solution.py:240
  34.8 8.4 %collective-permute-done.9.refs_2_.refs_11_ = bf16[160,1024]{1,0:T(8,128)(2,1)S(1)} collective-permute-done((bf16[160,1024]{1,0:T(8,128)(2,1)S(1)}, bf16[160,1024]{1,0:T(8,128)(2,1)S(1)}, u32[]{:S(2)}, u32[]{:S(2)}) %collective-permute-start.9) | collective-permute-done | bytes 327712 | tf_op jit(solution)/shard_map/ppermute | solution.py:245
  43.3 3.3 %collective-permute-done.5.below_ref = bf16[128,640]{1,0:T(8,128)(2,1)S(1)} collective-permute-done((bf16[128,640]{1,0:T(8,128)(2,1)S(1)}, bf16[128,640]{1,0:T(8,128)(2,1)S(1)}, u32[]{:S(2)}, u32[]{:S(2)}) %collective-permute-start.5) | collective-permute-done | bytes 163872 | tf_op jit(solution)/shard_map/ppermute | solution.py:239
  46.6 2.8 %shard_map.84 = (f32[512,640]{1,0:T(8,128)S(1)}, bf16[1024,640]{1,0:T(8,128)(2,1)}) custom-call(f32[512,640]{1,0:T(8,128)S(1)} %get-tuple-element.16.prev_ref, bf16[128,640]{1,0:T(8,128)(2,1)S(1)} %collective-permute-done.5.below_ref, bf16[128,640]{1,0:T(8,128)(2,1)S(1)} %collective-permute-done.6.above_ref, s32[4,32]{1,0:T(4,128)S(1)} %bitcast.19, ...), custom_call_target="tpu_custom_call" | custom-call | flops 3000000000 | bytes 4262400 | tf_op jit(solution)/shard_map/pallas_call | solution.py:222
  49.4 12.3 %all-to-all-start = ((bf16[64,16,640]{2,1,0:T(8,128)(2,1)}), bf16[64,16,640]{2,1,0:T(8,128)(2,1)S(1)}, u32[]{:S(2)}, u32[]{:S(2)}) async-start(bf16[64,16,640]{2,1,0:T(8,128)(2,1)} %bitcast.8), calls=%async_computation | async-start | bytes 2621440 | tf_op jit(solution)/shard_map/all_to_all | solution.py:289
  61.7 1.3 collective-permute-start.10
  63.0 0.7 collective-permute-start.12
  63.7 22.7 %collective-permute-done.10.refs_5_ = bf16[2,1024,256]{2,1,0:T(8,128)(2,1)} collective-permute-done((bf16[2,1024,256]{2,1,0:T(8,128)(2,1)}, bf16[2,1024,256]{2,1,0:T(8,128)(2,1)}, u32[]{:S(2)}, u32[]{:S(2)}) %collective-permute-start.10) | collective-permute-done | bytes 1048608 | tf_op jit(solution)/shard_map/ppermute | solution.py:245
  86.4 2.5 %collective-permute-done.11.refs_6_ = bf16[2,1024,256]{2,1,0:T(8,128)(2,1)} collective-permute-done((bf16[2,1024,256]{2,1,0:T(8,128)(2,1)}, bf16[2,1024,256]{2,1,0:T(8,128)(2,1)}, u32[]{:S(2)}, u32[]{:S(2)}) %collective-permute-start.11) | collective-permute-done | bytes 1048608 | tf_op jit(solution)/shard_map/ppermute | solution.py:245
  88.9 22.9 %collective-permute-done.12.refs_7_ = bf16[2,1024,256]{2,1,0:T(8,128)(2,1)} collective-permute-done((bf16[2,1024,256]{2,1,0:T(8,128)(2,1)}, bf16[2,1024,256]{2,1,0:T(8,128)(2,1)}, u32[]{:S(2)}, u32[]{:S(2)}) %collective-permute-start.12) | collective-permute-done | bytes 1048608 | tf_op jit(solution)/shard_map/ppermute | solution.py:245
  111.8 1.1 copy-done.11
  112.9 13.4 %shard_map.85 = bf16[1024,640]{1,0:T(8,128)(2,1)} custom-call(s32[1]{0:T(128)} %bitcast.7.sec_ref, bf16[1024,640]{1,0:T(8,128)(2,1)} %bitcast.20, bf16[640,256]{1,0:T(8,128)(2,1)} %bitcast.30, bf16[640,256]{1,0:T(8,128)(2,1)} %copy-done.1, bf16[640,256]{1,0:T(8,128)(2,1)} %copy-done.2, bf16[640,256]{1,0:T(8,128)(2,1)} %copy-done.3, ...), custom_call_target="tpu_custom_call" | custom-call | flops 7000000000 | bytes 9437188 | tf_op jit(solution)/shard_map/pallas_call | solution.py:222
  126.2 44.4 %all_to_all.10 = bf16[64,16,640]{2,1,0:T(8,128)(2,1)S(1)} all-to-all(bf16[64,16,640]{2,1,0:T(8,128)(2,1)} %bitcast.21), channel_id=1, replica_groups=mesh['elem'=64,'sec'=4] {'elem'}, dimensions={0} | all-to-all | bytes 2621440 | tf_op jit(solution)/shard_map/all_to_all | solution.py:312
  170.6 2.8 %shard_map.86 = f32[512,640]{1,0:T(8,128)} custom-call(f32[512,640]{1,0:T(8,128)S(1)} %get-tuple-element.19.state_ref, bf16[1024,640]{1,0:T(8,128)(2,1)S(1)} %bitcast.14, s32[1,512]{1,0:T(1,128)S(1)} %bitcast.16), custom_call_target="tpu_custom_call" | custom-call | flops 1000000000 | bytes 3934208 | tf_op jit(solution)/shard_map/pallas_call | solution.py:222
  (36 shorter events, 1.2 us)
Async XLA Ops:
  0.0 25.8 %collective-permute-start.2 = (bf16[640,256]{1,0:T(8,128)(2,1)}, bf16[640,256]{1,0:T(8,128)(2,1)S(1)}, u32[]{:S(2)}, u32[]{:S(2)}) collective-permute-start(bf16[640,256]{1,0:T(8,128)(2,1)} %bitcast.27), channel_id=1, source_target_pairs={{0,3},{1,0},{2,1},{3,2},{4,7},{5,4},{6,5},{7,6},{8,11},{9,8},{10,9... | collective-permute-start | bytes 983048 | tf_op jit(solution)/shard_map/ppermute | solution.py:245
  3.3 23.3 %collective-permute-start.3 = (bf16[640,256]{1,0:T(8,128)(2,1)}, bf16[640,256]{1,0:T(8,128)(2,1)S(1)}, u32[]{:S(2)}, u32[]{:S(2)}) collective-permute-start(bf16[640,256]{1,0:T(8,128)(2,1)} %bitcast.28), channel_id=1, source_target_pairs={{0,2},{1,3},{2,0},{3,1},{4,6},{5,7},{6,4},{7,5},{8,10},{9,11},{10,... | collective-permute-start | bytes 983048 | tf_op jit(solution)/shard_map/ppermute | solution.py:245
  3.8 22.8 %collective-permute-start.4 = (bf16[640,256]{1,0:T(8,128)(2,1)}, bf16[640,256]{1,0:T(8,128)(2,1)S(1)}, u32[]{:S(2)}, u32[]{:S(2)}) collective-permute-start(bf16[640,256]{1,0:T(8,128)(2,1)} %bitcast.29), channel_id=1, source_target_pairs={{0,1},{1,2},{2,3},{3,0},{4,5},{5,6},{6,7},{7,4},{8,9},{9,10},{10,1... | collective-permute-start | bytes 983048 | tf_op jit(solution)/shard_map/ppermute | solution.py:245
  4.4 20.6 %copy-start.12 = (bf16[1,1024,160]{1,2,0:T(8,128)(2,1)S(1)}, bf16[1,1024,160]{1,2,0:T(8,128)(2,1)}, u32[]{:S(2)}) copy-start(bf16[1,1024,160]{1,2,0:T(8,128)(2,1)} %param.15) | copy-start | bytes 983044
  4.4 22.2 %copy-start.7 = (f32[16,16]{1,0:T(8,128)S(1)}, f32[16,16]{1,0:T(8,128)}, u32[]{:S(2)}) copy-start(f32[16,16]{1,0:T(8,128)} %op_ref.3) | copy-start | bytes 3076
  4.4 22.2 %copy-start.8 = (f32[640]{0:T(1024)S(1)}, f32[640]{0:T(1024)}, u32[]{:S(2)}) copy-start(f32[640]{0:T(1024)} %rates_ref.3) | copy-start | bytes 7684
  4.4 22.2 %copy-start.9 = (s32[32,4]{0,1:T(4,128)S(1)}, s32[32,4]{0,1:T(4,128)}, u32[]{:S(2)}) copy-start(s32[32,4]{0,1:T(4,128)} %param.9) | copy-start | bytes 1540
  9.5 15.5 %collective-permute-start = (bf16[128,640]{1,0:T(8,128)(2,1)}, bf16[128,640]{1,0:T(8,128)(2,1)S(1)}, u32[]{:S(2)}, u32[]{:S(2)}) collective-permute-start(bf16[128,640]{1,0:T(8,128)(2,1)} %get-tuple-element.14), channel_id=1, source_target_pairs={{0,1},{1,2},{2,3},{3,4},{4,5},{5,6},{6,7},{7,8},{8,9},{9,10},{10,1... | collective-permute-start | bytes 491528 | tf_op jit(solution)/shard_map/ppermute | solution.py:239
  11.1 13.9 %collective-permute-start.1 = (bf16[128,640]{1,0:T(8,128)(2,1)}, bf16[128,640]{1,0:T(8,128)(2,1)S(1)}, u32[]{:S(2)}, u32[]{:S(2)}) collective-permute-start(bf16[128,640]{1,0:T(8,128)(2,1)} %get-tuple-element.15), channel_id=1, source_target_pairs={{0,255},{1,0},{2,1},{3,2},{4,3},{5,4},{6,5},{7,6},{8,7},{9,8},{10,... | collective-permute-start | bytes 491528 | tf_op jit(solution)/shard_map/ppermute | solution.py:240
  25.0 9.8 %collective-permute-start.7 = (bf16[160,1024]{1,0:T(8,128)(2,1)S(1)}, bf16[160,1024]{1,0:T(8,128)(2,1)S(1)}, u32[]{:S(2)}, u32[]{:S(2)}) collective-permute-start(bf16[160,1024]{1,0:T(8,128)(2,1)S(1)} %bitcast.32), channel_id=1, source_target_pairs={{0,3},{1,0},{2,1},{3,2},{4,7},{5,4},{6,5},{7,6},{8,11},{9,8},{10,9... | collective-permute-start | bytes 983048 | tf_op jit(solution)/shard_map/ppermute | solution.py:245
  25.0 9.8 %collective-permute-start.8 = (bf16[160,1024]{1,0:T(8,128)(2,1)S(1)}, bf16[160,1024]{1,0:T(8,128)(2,1)S(1)}, u32[]{:S(2)}, u32[]{:S(2)}) collective-permute-start(bf16[160,1024]{1,0:T(8,128)(2,1)S(1)} %bitcast.33), channel_id=1, source_target_pairs={{0,2},{1,3},{2,0},{3,1},{4,6},{5,7},{6,4},{7,5},{8,10},{9,11},{10,... | collective-permute-start | bytes 983048 | tf_op jit(solution)/shard_map/ppermute | solution.py:245
  25.8 5.2 %copy-start.1 = (bf16[640,256]{1,0:T(8,128)(2,1)}, bf16[640,256]{1,0:T(8,128)(2,1)S(1)}, u32[]{:S(2)}) copy-start(bf16[640,256]{1,0:T(8,128)(2,1)S(1)} %collective-permute-done.2.refs_0_.refs_1_) | copy-start | bytes 983044
  25.8 17.4 %collective-permute-start.9 = (bf16[160,1024]{1,0:T(8,128)(2,1)S(1)}, bf16[160,1024]{1,0:T(8,128)(2,1)S(1)}, u32[]{:S(2)}, u32[]{:S(2)}) collective-permute-start(bf16[160,1024]{1,0:T(8,128)(2,1)S(1)} %bitcast.34), channel_id=1, source_target_pairs={{0,1},{1,2},{2,3},{3,0},{4,5},{5,6},{6,7},{7,4},{8,9},{9,10},{10,1... | collective-permute-start | bytes 983048 | tf_op jit(solution)/shard_map/ppermute | solution.py:245
  26.6 4.5 %copy-start.3 = (bf16[640,256]{1,0:T(8,128)(2,1)}, bf16[640,256]{1,0:T(8,128)(2,1)S(1)}, u32[]{:S(2)}) copy-start(bf16[640,256]{1,0:T(8,128)(2,1)S(1)} %collective-permute-done.4.refs_2_.refs_3_) | copy-start | bytes 983044
  28.2 18.4 %copy-start = (s32[512,1]{0,1:T(1,128)S(1)}, s32[512,1]{0,1:T(1,128)}, u32[]{:S(2)}) copy-start(s32[512,1]{0,1:T(1,128)} %param.12) | copy-start | bytes 6148
  31.1 15.5 %collective-permute-start.5 = (bf16[128,640]{1,0:T(8,128)(2,1)S(1)}, bf16[128,640]{1,0:T(8,128)(2,1)S(1)}, u32[]{:S(2)}, u32[]{:S(2)}) collective-permute-start(bf16[128,640]{1,0:T(8,128)(2,1)S(1)} %get-tuple-element.17), channel_id=1, source_target_pairs={{0,1},{1,2},{2,3},{3,4},{4,5},{5,6},{6,7},{7,8},{8,9},{9,10},{10,1... | collective-permute-start | bytes 491528 | tf_op jit(solution)/shard_map/ppermute | solution.py:239
  32.3 14.2 %collective-permute-start.6 = (bf16[128,640]{1,0:T(8,128)(2,1)S(1)}, bf16[128,640]{1,0:T(8,128)(2,1)S(1)}, u32[]{:S(2)}, u32[]{:S(2)}) collective-permute-start(bf16[128,640]{1,0:T(8,128)(2,1)S(1)} %get-tuple-element.18), channel_id=1, source_target_pairs={{0,255},{1,0},{2,1},{3,2},{4,3},{5,4},{6,5},{7,6},{8,7},{9,8},{10,... | collective-permute-start | bytes 491528 | tf_op jit(solution)/shard_map/ppermute | solution.py:240
  34.8 14.6 %copy-start.4 = (bf16[160,1024]{1,0:T(8,128)(2,1)}, bf16[160,1024]{1,0:T(8,128)(2,1)S(1)}, u32[]{:S(2)}) copy-start(bf16[160,1024]{1,0:T(8,128)(2,1)S(1)} %collective-permute-done.7.refs_0_.refs_9_) | copy-start | bytes 983044
  34.8 14.6 %copy-start.5 = (bf16[160,1024]{1,0:T(8,128)(2,1)}, bf16[160,1024]{1,0:T(8,128)(2,1)S(1)}, u32[]{:S(2)}) copy-start(bf16[160,1024]{1,0:T(8,128)(2,1)S(1)} %collective-permute-done.8.refs_1_.refs_10_) | copy-start | bytes 983044
  43.3 6.1 %copy-start.6 = (bf16[160,1024]{1,0:T(8,128)(2,1)}, bf16[160,1024]{1,0:T(8,128)(2,1)S(1)}, u32[]{:S(2)}) copy-start(bf16[160,1024]{1,0:T(8,128)(2,1)S(1)} %collective-permute-done.9.refs_2_.refs_11_) | copy-start | bytes 983044
  49.4 62.4 %all-to-all-start = ((bf16[64,16,640]{2,1,0:T(8,128)(2,1)}), bf16[64,16,640]{2,1,0:T(8,128)(2,1)S(1)}, u32[]{:S(2)}, u32[]{:S(2)}) async-start(bf16[64,16,640]{2,1,0:T(8,128)(2,1)} %bitcast.8), calls=%async_computation | async-start | bytes 2621440 | tf_op jit(solution)/shard_map/all_to_all | solution.py:289
  61.7 24.7 %collective-permute-start.10 = (bf16[2,1024,256]{2,1,0:T(8,128)(2,1)}, bf16[2,1024,256]{2,1,0:T(8,128)(2,1)}, u32[]{:S(2)}, u32[]{:S(2)}) collective-permute-start(bf16[2,1024,256]{2,1,0:T(8,128)(2,1)} %bitcast.23), channel_id=1, source_target_pairs={{0,3},{1,0},{2,1},{3,2},{4,7},{5,4},{6,5},{7,6},{8,11},{9,8},{10,9... | collective-permute-start | bytes 3145736 | tf_op jit(solution)/shard_map/ppermute | solution.py:245
  63.0 25.9 %collective-permute-start.11 = (bf16[2,1024,256]{2,1,0:T(8,128)(2,1)}, bf16[2,1024,256]{2,1,0:T(8,128)(2,1)}, u32[]{:S(2)}, u32[]{:S(2)}) collective-permute-start(bf16[2,1024,256]{2,1,0:T(8,128)(2,1)} %bitcast.24), channel_id=1, source_target_pairs={{0,2},{1,3},{2,0},{3,1},{4,6},{5,7},{6,4},{7,5},{8,10},{9,11},{10,... | collective-permute-start | bytes 3145736 | tf_op jit(solution)/shard_map/ppermute | solution.py:245
  63.0 48.8 %collective-permute-start.12 = (bf16[2,1024,256]{2,1,0:T(8,128)(2,1)}, bf16[2,1024,256]{2,1,0:T(8,128)(2,1)}, u32[]{:S(2)}, u32[]{:S(2)}) collective-permute-start(bf16[2,1024,256]{2,1,0:T(8,128)(2,1)} %bitcast.25), channel_id=1, source_target_pairs={{0,1},{1,2},{2,3},{3,0},{4,5},{5,6},{6,7},{7,4},{8,9},{9,10},{10,1... | collective-permute-start | bytes 3145736 | tf_op jit(solution)/shard_map/ppermute | solution.py:245
  (3 other events, 7.1 us)

commit v3 on v2

--- a/solution.py
+++ b/solution.py
@@ -141,8 +141,12 @@
     south_ref[...] = sides[count:]
 
 
-def send_kernel(capacity, groups, prev_ref, below_ref, above_ref, nbt_ref, ids_ref, *refs):
-    state_ref, out_ref = refs[-2:]
+def send_kernel(
+    capacity, groups, prev_ref, below_ref, above_ref, nbt_ref, ids_ref, hidden_ref, *refs
+):
+    state_ref, out_ref, copy_ref, sem = refs[-4:]
+    hand_on = pltpu.make_async_copy(hidden_ref, copy_ref, sem.at[0])
+    hand_on.start()
     state = meet(prev_ref[...], below_ref[...], above_ref[...], nbt_ref[...])
     state_ref[...] = state
     rows = state.shape[0]
@@ -153,6 +157,7 @@
     slot = jnp.sum(jnp.where(named, base + rank, 0.0), axis=0, keepdims=True)
     pick = ones_where(iota((groups * capacity, rows), 0).astype(F32) == slot)
     out_ref[...] = mul(pick, state.astype(BF16)).astype(BF16)
+    hand_on.wait()
 
 
 def add_kernel(capacity, groups, state_ref, back_ref, ids_ref, out_ref):
@@ -170,52 +175,71 @@
     out_ref[...] = state_ref[...] + mul(pick, back_ref[...])
 
 
+def halves_kernel(below_ref, above_ref, low_ref, high_ref):
+    low_ref[...] = below_ref[0]
+    high_ref[...] = above_ref[1]
+
+
 def silu(v):
     half = 0.5 * v
     return (half + half * jnp.tanh(half)).astype(BF16)
 
 
 def network_kernel(tile, sec_ref, rows_ref, *refs):
-    shards, out_ref = refs[0:12], refs[12]
-    first, middle, last, hold_a, hold_b, sems = refs[13:]
+    first_in, hidden_in, last_in, out_ref = refs[0:4], refs[4:9], refs[9:13], refs[13]
+    first, middle, last, hold_a, hold_b, rows, result, sems, row_sems, out_sems = refs[14:]
     layers = middle.shape[1]
+    tiles = rows.shape[0]
     places = [(sec_ref[0] + k) & 3 for k in range(4)]
     width = first.shape[2]
-    waits = [[] for _ in range(layers + 2)]
+    at = [pl.ds(step * tile, tile) for step in range(tiles)]
+    incoming = [pltpu.make_async_copy(rows_ref.at[at[i]], rows.at[i], row_sems.at[i]) for i in range(tiles)]
+    outgoing = [pltpu.make_async_copy(result.at[i], out_ref.at[at[i]], out_sems.at[i]) for i in range(tiles)]
+    weights = [[] for _ in range(layers + 2)]
     for k in range(4):
-        pairs = [(shards[k], first.at[k], 0)]
-        pairs += [(shards[4 + k].at[layer], middle.at[k, layer], 1 + layer) for layer in range(layers)]
-        pairs += [(shards[8 + k], last.at[places[k]], 1 + layers)]
+        pairs = [(first_in[k], first.at[k], 0)]
+        for layer in range(layers):
+            source = hidden_in[2 + layer] if k == 2 else hidden_in[(0, 1, 2, 4)[k]].at[layer]
+            pairs += [(source, middle.at[k, layer], 1 + layer)]
+        pairs += [(last_in[k], last.at[places[k]], 1 + layers)]
         for source, target, group in pairs:
-            waits[group].append(pltpu.make_async_copy(source, target, sems.at[k, group]))
-    for group in waits:
-        for copy in group:
-            copy.start()
-
-    def arrived(start, group):
-        if start == 0:
-            for copy in waits[group]:
+            weights[group].append(pltpu.make_async_copy(source, target, sems.at[k, group]))
+    incoming[0].start()
+    for copy in weights[0]:
+        copy.start()
+    for step in range(tiles):
+        incoming[step].wait()
+        if step == 0:
+            for copy in weights[0]:
                 copy.wait()
-
-    for start in range(0, rows_ref.shape[0], tile):
-        rows = rows_ref[start : start + tile]
-        arrived(start, 0)
+            for group in weights[1:]:
+                for copy in group:
+                    copy.start()
+            for copy in incoming[1:]:
+                copy.start()
         for k in range(4):
             spot = pl.ds(pl.multiple_of(places[k] * width, width), width)
-            hold_a[:, spot] = silu(mul(rows, first[k]))
+            hold_a[:, spot] = silu(mul(rows[step], first[k]))
         now, later = hold_a, hold_b
         for layer in range(layers):
-            arrived(start, 1 + layer)
+            if step == 0:
+                for copy in weights[1 + layer]:
+                    copy.wait()
             for k in range(4):
                 spot = pl.ds(pl.multiple_of(places[k] * width, width), width)
                 later[:, spot] = silu(mul(now[...], middle[k, layer]))
             now, later = later, now
-        arrived(start, 1 + layers)
+        if step == 0:
+            for copy in weights[1 + layers]:
+                copy.wait()
         matrix = last[...].reshape(out_ref.shape[1], now.shape[1])
-        out_ref[start : start + tile] = mul_nt(now[...], matrix).astype(BF16)
-
-
-def call(kernel, out, *args, passed=(), scratch=(), flops=0, specs=None, limit=VMEM_LIMIT):
+        result[step] = mul_nt(now[...], matrix).astype(BF16)
+        outgoing[step].start()
+    for copy in outgoing:
+        copy.wait()
+
+
+def call(kernel, out, *args, passed=(), scratch=(), flops=0, specs=None, outs=None, limit=VMEM_LIMIT):
     size = sum(a.size * a.dtype.itemsize for a in args)
     size += sum(o.size * o.dtype.itemsize for o in out)
     vmem = pl.BlockSpec(memory_space=pltpu.VMEM)
@@ -223,7 +247,7 @@
         kernel,
         out_shape=out,
         in_specs=(specs or [vmem] * len(args)) + [pl.BlockSpec(memory_space=pl.ANY)] * len(passed),
-        out_specs=[vmem] * len(out),
+        out_specs=outs or [vmem] * len(out),
         scratch_shapes=scratch,
         compiler_params=pltpu.CompilerParams(vmem_limit_bytes=limit),
         cost_estimate=pl.CostEstimate(flops=flops, bytes_accessed=size, transcendentals=0),
@@ -241,8 +265,14 @@
     return below, above
 
 
-def gathered(shard):
-    return [shard] + [lax.ppermute(shard, "sec", ring(4, -k)) for k in (1, 2, 3)]
+def from_sides(*shards):
+    below = [lax.ppermute(x, "sec", ring(4, 1)) for x in shards]
+    above = [lax.ppermute(x, "sec", ring(4, -1)) for x in shards]
+    return below, above
+
+
+def from_far(below, above):
+    return lax.ppermute(below, "sec", ring(4, 1)), lax.ppermute(above, "sec", ring(4, -1))
 
 
 def on_device(
@@ -257,9 +287,11 @@
     nbt = neighbours.T
     ids = regime_ids.T
 
-    first = gathered(input_proj[0])
-    middle = gathered(hidden_proj[0])
-    last = gathered(output_proj[0].T)
+    mine = (input_proj[0], output_proj[0].T)
+    below, above = from_sides(*mine)
+    first, last = ([m, a, None, b] for m, a, b in zip(mine, above, below))
+    first[2], last[2] = from_far(below[0], above[1])
+    anywhere = pl.BlockSpec(memory_space=pl.ANY)
 
     edge = shape((count * SIDE, width), BF16)
     moved = [shape((rows_dev, width), F32), edge, edge]
@@ -272,41 +304,62 @@
             pltpu.VMEM(rates.shape, F32),
             pltpu.SemaphoreType.DMA((4,)),
         ],
-        specs=[pl.BlockSpec(memory_space=pl.ANY)] * 4,
+        specs=[anywhere] * 4,
         limit=58 * 1024 * 1024,
         flops=3 * 10**9,
     )
-    below, above = exchange(north, south)
+    prev, next_ = exchange(north, south)
+    vmem = pl.BlockSpec(memory_space=pltpu.VMEM)
     second, north, south = call(
-        step_kernel, moved, second, below, above, nbt, operator, rates, passed=first[1:], flops=3 * 10**9
-    )
-    below, above = exchange(north, south)
-    state, outgoing = call(
+        step_kernel, moved, second, prev, next_, nbt, operator, rates,
+        passed=(below[0], above[0]), flops=3 * 10**9,
+    )
+    prev, next_ = exchange(north, south)
+    state, outgoing, hidden_copy = call(
         functools.partial(send_kernel, capacity, groups),
-        [shape((rows_dev, width), F32), shape((slots, width), BF16)],
-        second, below, above, nbt, ids, passed=last[1:], flops=3 * 10**9,
-    )
+        [
+            shape((rows_dev, width), F32),
+            shape((slots, width), BF16),
+            shape(hidden_proj.shape[1:], BF16),
+        ],
+        second, prev, next_, nbt, ids, hidden_proj[0],
+        passed=(below[1], above[1]),
+        specs=[vmem] * 5 + [anywhere],
+        outs=[vmem] * 2 + [anywhere],
+        scratch=[pltpu.SemaphoreType.DMA((1,))],
+        flops=3 * 10**9,
+    )
+    hidden_below, hidden_above = from_sides(hidden_copy)
+    handed = call(
+        halves_kernel, [shape(hidden_proj.shape[2:], BF16)] * 2, *hidden_below, *hidden_above,
+        limit=16 * 1024 * 1024, flops=20 * 10**9,
+    )
+    far = from_far(*handed)
     incoming = lax.all_to_all(
         outgoing.reshape(groups, capacity, width), "elem", split_axis=0, concat_axis=0, tiled=True
     )
     hid = hidden_proj.shape[2]
     tile = 512
-    vmem = pl.BlockSpec(memory_space=pltpu.VMEM)
     sec = lax.axis_index("sec").astype(jnp.int32).reshape(1)
     (result,) = call(
         functools.partial(network_kernel, tile),
         [shape((slots, width), BF16)],
-        sec, incoming.reshape(slots, width), *first, *middle, *last,
+        sec, incoming.reshape(slots, width), *first, hidden_proj[0], *hidden_above, *far, *hidden_below, *last,
         scratch=[
             pltpu.VMEM((4, *input_proj.shape[1:2], hid // 4), BF16),
             pltpu.VMEM((4, *hidden_proj.shape[1:3], hid // 4), BF16),
             pltpu.VMEM((4, width // 4, hid), BF16),
             pltpu.VMEM((tile, hid), BF16),
             pltpu.VMEM((tile, hid), BF16),
+            pltpu.VMEM((slots // tile, tile, width), BF16),
+            pltpu.VMEM((slots // tile, tile, width), BF16),
             pltpu.SemaphoreType.DMA((4, 2 + hidden_proj.shape[1])),
+            pltpu.SemaphoreType.DMA((slots // tile,)),
+            pltpu.SemaphoreType.DMA((slots // tile,)),
         ],
-        specs=[pl.BlockSpec(memory_space=pltpu.SMEM), vmem] + [pl.BlockSpec(memory_space=pl.ANY)] * 12,
-        limit=55 * 1024 * 1024,
+        specs=[pl.BlockSpec(memory_space=pltpu.SMEM)] + [anywhere] * 14,
+        outs=[anywhere],
+        limit=58 * 1024 * 1024,
         flops=7 * 10**9,
     )
     returned = lax.all_to_all(

time: 174 us -> 149 us (0.86)
  waiting for transfers between devices: 71.7 us -> 35.2 us
  starting transfers between devices: 27.7 us -> 36.1 us
  blocking collectives: 44.4 us -> 47.2 us
    ppermute x9 -> x10, waiting for transfers between devices: 56.5 us -> 20.5 us  [the longest x2 12.4 us: from_far(): lax.ppermute(below, 'sec', ring(4, 1))]
    ppermute x2, starting transfers between devices: 4.52 us -> 11.6 us  [exchange(): above = lax.ppermute(south, DEVICE_AXES, ring(total, -1))]
    ppermute x2, waiting for transfers between devices: 15.2 us -> 8.26 us  [exchange(): below = lax.ppermute(north, DEVICE_AXES, ring(total, 1))]
    all_to_all x1, waiting for transfers between devices: 0.01 us -> 6.07 us  [on_device(): lax.all_to_all(outgoing.reshape(groups, capacity, width), 'elem', split_a...]
    ppermute x9 -> x10, starting transfers between devices: 8.01 us -> 12.1 us  [the longest x3 6.62 us: from_sides(): above = [lax.ppermute(x, 'sec', ring(4, -1)) for x in shards]]
    all_to_all x1, blocking collectives: 44.4 us -> 47.2 us  [on_device(): lax.all_to_all(result.reshape(groups, capacity, width), 'elem', split_axi...]
    ppermute x2, starting transfers between devices: 2.85 us -> 0.37 us  [exchange(): below = lax.ppermute(north, DEVICE_AXES, ring(total, 1))]
    pallas_call x5 -> x6, Pallas kernels: 26.8 us -> 27.9 us  [call(): pl.pallas_call(kernel, out_shape=out, in_specs=(specs or [vmem] * len(arg...]
  transfers between devices with their start and end apart: 14 -> 15, of which waited for: 6 -> 6; matrix products, arithmetic and copies ran while one was open for 0% -> 0% of each run, Pallas kernels for 5% -> 6%
where the time goes in v3:
time: 149 us
  blocking collectives  47.2 us (32%)
  starting transfers between devices  36.1 us (24%)
  waiting for transfers between devices  35.2 us (24%)
  Pallas kernels  27.9 us (19%)
  local copies, waits for them, and re-layouts  1.91 us (1%)
    all_to_all x1, blocking collectives, on_device(): lax.all_to_all(result.reshape(groups, capacity, width), 'elem', split_axi...  47.2 us
    pallas_call x6, Pallas kernels, call(): pl.pallas_call(kernel, out_shape=out, in_specs=(specs or [vmem] * len(arg...  27.9 us
    ppermute x2, waiting for transfers between devices, from_far(): lax.ppermute(below, 'sec', ring(4, 1))  12.4 us
    all_to_all x1, starting transfers between devices, on_device(): lax.all_to_all(outgoing.reshape(groups, capacity, width), 'elem', split_a...  12.1 us
    ppermute x2, starting transfers between devices, exchange(): above = lax.ppermute(south, DEVICE_AXES, ring(total, -1))  11.6 us
    ppermute x2, waiting for transfers between devices, exchange(): below = lax.ppermute(north, DEVICE_AXES, ring(total, 1))  8.26 us
    ppermute x3, waiting for transfers between devices, from_sides(): below = [lax.ppermute(x, 'sec', ring(4, 1)) for x in shards]  8.01 us
    ppermute x3, starting transfers between devices, from_sides(): above = [lax.ppermute(x, 'sec', ring(4, -1)) for x in shards]  6.62 us
  transfers between devices with their start and end apart: 15, of which 6 were waited for; matrix products, arithmetic and copies ran while one was open for 0% of the time, Pallas kernels for 6%

profile of v3, /device:TPU:1, one launch (start us, length us, event | category | flops | bytes accessed | tf_op | source)
XLA Modules:
  0.0 148.5 jit_solution(13424638633907369737)
XLA Ops:
  0.0 3.3 %collective-permute-start.3 = (bf16[640,256]{1,0:T(8,128)(2,1)}, bf16[640,256]{1,0:T(8,128)(2,1)S(1)}, u32[]{:S(2)}, u32[]{:S(2)}) collective-permute-start(bf16[640,256]{1,0:T(8,128)(2,1)} %bitcast.24), channel_id=1, source_target_pairs={{0,3},{1,0},{2,1},{3,2},{4,7},{5,4},{6,5},{7,6},{8,11},{9,8},{10,9... | collective-permute-start | bytes 983048 | tf_op jit(solution)/shard_map/ppermute | solution.py:270
  3.3 5.0 %shard_map.82 = (f32[512,640]{1,0:T(8,128)}, bf16[128,640]{1,0:T(8,128)(2,1)}, bf16[128,640]{1,0:T(8,128)(2,1)}) custom-call(f32[512,640]{1,0:T(8,128)} %bitcast.23, s32[4,32]{1,0:T(4,128)} %bitcast.19, f32[16,16]{1,0:T(8,128)} %op_ref.3, f32[640]{0:T(1024)} %rates_ref.3), custom_call_target="tpu_custom_call" | custom-call | flops 3000000000 | bytes 2953216 | tf_op jit(solution)/shard_map/pallas_call | solution.py:246
  8.3 0.3 collective-permute-start
  8.6 3.7 %collective-permute-start.1 = (bf16[128,640]{1,0:T(8,128)(2,1)}, bf16[128,640]{1,0:T(8,128)(2,1)S(1)}, u32[]{:S(2)}, u32[]{:S(2)}) collective-permute-start(bf16[128,640]{1,0:T(8,128)(2,1)} %get-tuple-element.18), channel_id=1, source_target_pairs={{0,255},{1,0},{2,1},{3,2},{4,3},{5,4},{6,5},{7,6},{8,7},{9,8},{10,... | collective-permute-start | bytes 491528 | tf_op jit(solution)/shard_map/ppermute | solution.py:264
  12.3 0.7 collective-permute-start.7
  13.0 4.7 %collective-permute-done.below_ref = bf16[128,640]{1,0:T(8,128)(2,1)S(1)} collective-permute-done((bf16[128,640]{1,0:T(8,128)(2,1)}, bf16[128,640]{1,0:T(8,128)(2,1)S(1)}, u32[]{:S(2)}, u32[]{:S(2)}) %collective-permute-start) | collective-permute-done | bytes 163872 | tf_op jit(solution)/shard_map/ppermute | solution.py:263
  17.7 1.4 copy-done.9
  19.1 2.8 %shard_map.83 = (f32[512,640]{1,0:T(8,128)S(1)}, bf16[128,640]{1,0:T(8,128)(2,1)S(1)}, bf16[128,640]{1,0:T(8,128)(2,1)S(1)}) custom-call(f32[512,640]{1,0:T(8,128)S(1)} %copy-done.9, bf16[128,640]{1,0:T(8,128)(2,1)S(1)} %collective-permute-done.below_ref, bf16[128,640]{1,0:T(8,128)(2,1)S(1)} %collective-permute-done.1.above_ref, s32[4,32]{1,0:T(4,128)S(1)} %bitcast.20, ...), custom_call_target="tpu_custom_call" | custom-call | flops 3000000000 | bytes 3280896 | tf_op jit(solution)/shard_map/pallas_call | solution.py:246
  22.1 7.9 %collective-permute-start.5 = (bf16[128,640]{1,0:T(8,128)(2,1)S(1)}, bf16[128,640]{1,0:T(8,128)(2,1)S(1)}, u32[]{:S(2)}, u32[]{:S(2)}) collective-permute-start(bf16[128,640]{1,0:T(8,128)(2,1)S(1)} %get-tuple-element.21), channel_id=1, source_target_pairs={{0,255},{1,0},{2,1},{3,2},{4,3},{5,4},{6,5},{7,6},{8,7},{9,8},{10,... | collective-permute-start | bytes 491528 | tf_op jit(solution)/shard_map/ppermute | solution.py:264
  30.0 3.6 %collective-permute-done.4.below_ref = bf16[128,640]{1,0:T(8,128)(2,1)S(1)} collective-permute-done((bf16[128,640]{1,0:T(8,128)(2,1)S(1)}, bf16[128,640]{1,0:T(8,128)(2,1)S(1)}, u32[]{:S(2)}, u32[]{:S(2)}) %collective-permute-start.4) | collective-permute-done | bytes 163872 | tf_op jit(solution)/shard_map/ppermute | solution.py:263
  33.5 0.4 collective-permute-done.5.above_ref
  34.0 2.8 %shard_map.84 = (f32[512,640]{1,0:T(8,128)S(1)}, bf16[1024,640]{1,0:T(8,128)(2,1)}, bf16[2,1024,256]{2,1,0:T(8,128)(2,1)}) custom-call(f32[512,640]{1,0:T(8,128)S(1)} %get-tuple-element.19.prev_ref, bf16[128,640]{1,0:T(8,128)(2,1)S(1)} %collective-permute-done.4.below_ref, bf16[128,640]{1,0:T(8,128)(2,1)S(1)} %collective-permute-done.5.above_ref, ...), custom_call_target="tpu_custom_call" | custom-call | flops 3000000000 | bytes 6359552 | tf_op jit(solution)/shard_map/pallas_call | solution.py:246
  36.9 2.7 %collective-permute-start.9 = (bf16[2,1024,256]{2,1,0:T(8,128)(2,1)}, bf16[2,1024,256]{2,1,0:T(8,128)(2,1)S(1)}, u32[]{:S(2)}, u32[]{:S(2)}) collective-permute-start(bf16[2,1024,256]{2,1,0:T(8,128)(2,1)} %get-tuple-element.24), channel_id=1, source_target_pairs={{0,3},{1,0},{2,1},{3,2},{4,7},{5,4},{6,5},{7,6},{8,11},{9,8},{10,9... | collective-permute-start | bytes 3145736 | tf_op jit(solution)/shard_map/ppermute | solution.py:270
  39.6 12.1 %all-to-all-start = ((bf16[64,16,640]{2,1,0:T(8,128)(2,1)}), bf16[64,16,640]{2,1,0:T(8,128)(2,1)}, u32[]{:S(2)}, u32[]{:S(2)}) async-start(bf16[64,16,640]{2,1,0:T(8,128)(2,1)} %bitcast.9), calls=%async_computation | async-start | bytes 2621440 | tf_op jit(solution)/shard_map/all_to_all | solution.py:338
  51.7 8.0 %collective-permute-done.10.below_ref.refs_8_ = bf16[2,1024,256]{2,1,0:T(8,128)(2,1)S(1)} collective-permute-done((bf16[2,1024,256]{2,1,0:T(8,128)(2,1)}, bf16[2,1024,256]{2,1,0:T(8,128)(2,1)S(1)}, u32[]{:S(2)}, u32[]{:S(2)}) %collective-permute-start.10) | collective-permute-done | bytes 1048608 | tf_op jit(solution)/shard_map/ppermute | solution.py:269
  59.7 1.2 shard_map.85
  61.1 0.3 copy-done.3
  61.4 2.7 %collective-permute-start.12 = (bf16[1024,256]{1,0:T(8,128)(2,1)}, bf16[1024,256]{1,0:T(8,128)(2,1)S(1)}, u32[]{:S(2)}, u32[]{:S(2)}) collective-permute-start(bf16[1024,256]{1,0:T(8,128)(2,1)} %get-tuple-element.26), channel_id=1, source_target_pairs={{0,3},{1,0},{2,1},{3,2},{4,7},{5,4},{6,5},{7,6},{8,11},{9,8},{10,9... | collective-permute-start | bytes 1572872 | tf_op jit(solution)/shard_map/ppermute | solution.py:275
  64.0 2.7 %collective-permute-start.13 = (bf16[160,1024]{1,0:T(8,128)(2,1)}, bf16[160,1024]{1,0:T(8,128)(2,1)S(1)}, u32[]{:S(2)}, u32[]{:S(2)}) collective-permute-start(bf16[160,1024]{1,0:T(8,128)(2,1)} %collective-permute-done.7.refs_1_.refs_10_), channel_id=1, source_target_pairs={{0,3},{1,0},{2,1},{3,2},{4,7},{5,4},{6,5},{7,6},{8,11},{9,8},{10,9... | collective-permute-start | bytes 983048 | tf_op jit(solution)/shard_map/ppermute | solution.py:275
  66.7 12.4 %collective-permute-done.8.refs_2_ = bf16[640,256]{1,0:T(8,128)(2,1)S(1)} collective-permute-done((bf16[640,256]{1,0:T(8,128)(2,1)}, bf16[640,256]{1,0:T(8,128)(2,1)S(1)}, u32[]{:S(2)}, u32[]{:S(2)}) %collective-permute-start.8) | collective-permute-done | bytes 327712 | tf_op jit(solution)/shard_map/ppermute | solution.py:275
  79.2 6.1 %all-to-all-done = bf16[64,16,640]{2,1,0:T(8,128)(2,1)} async-done(((bf16[64,16,640]{2,1,0:T(8,128)(2,1)}), bf16[64,16,640]{2,1,0:T(8,128)(2,1)}, u32[]{:S(2)}, u32[]{:S(2)}) %all-to-all-start) | async-done | bytes 1310752 | tf_op jit(solution)/shard_map/all_to_all | solution.py:338
  85.3 13.3 %shard_map.86 = bf16[1024,640]{1,0:T(8,128)(2,1)} custom-call(s32[1]{0:T(128)} %bitcast.8.sec_ref, bf16[1024,640]{1,0:T(8,128)(2,1)} %bitcast.10.rows_ref, bf16[640,256]{1,0:T(8,128)(2,1)} %bitcast.26, bf16[640,256]{1,0:T(8,128)(2,1)} %copy-done.4, bf16[640,256]{1,0:T(8,128)(2,1)} %copy-done.13, bf16[640,256]{1,0:T(8,128)(2,1)} %collective-permute-done.2.refs_0_.refs_3_, ...), custom_call_target="tpu_custom_call" | custom-call | flops 7000000000 | bytes 9437188 | tf_op jit(solution)/shard_map/pallas_call | solution.py:246
  98.6 47.2 %all_to_all.10 = bf16[64,16,640]{2,1,0:T(8,128)(2,1)S(1)} all-to-all(bf16[64,16,640]{2,1,0:T(8,128)(2,1)} %bitcast.22), channel_id=1, replica_groups=mesh['elem'=64,'sec'=4] {'elem'}, dimensions={0} | all-to-all | bytes 2621440 | tf_op jit(solution)/shard_map/all_to_all | solution.py:365
  145.8 2.8 %shard_map.87 = f32[512,640]{1,0:T(8,128)} custom-call(f32[512,640]{1,0:T(8,128)S(1)} %get-tuple-element.22.state_ref, bf16[1024,640]{1,0:T(8,128)(2,1)S(1)} %bitcast.14, s32[1,512]{1,0:T(1,128)S(1)} %bitcast.16), custom_call_target="tpu_custom_call" | custom-call | flops 1000000000 | bytes 3934208 | tf_op jit(solution)/shard_map/pallas_call | solution.py:246
  (43 shorter events, 0.4 us)
Async XLA Ops:
  0.0 17.7 %collective-permute-start.3 = (bf16[640,256]{1,0:T(8,128)(2,1)}, bf16[640,256]{1,0:T(8,128)(2,1)S(1)}, u32[]{:S(2)}, u32[]{:S(2)}) collective-permute-start(bf16[640,256]{1,0:T(8,128)(2,1)} %bitcast.24), channel_id=1, source_target_pairs={{0,3},{1,0},{2,1},{3,2},{4,7},{5,4},{6,5},{7,6},{8,11},{9,8},{10,9... | collective-permute-start | bytes 983048 | tf_op jit(solution)/shard_map/ppermute | solution.py:270
  3.3 14.4 %collective-permute-start.2 = (bf16[640,256]{1,0:T(8,128)(2,1)}, bf16[640,256]{1,0:T(8,128)(2,1)}, u32[]{:S(2)}, u32[]{:S(2)}) collective-permute-start(bf16[640,256]{1,0:T(8,128)(2,1)} %bitcast.25), channel_id=1, source_target_pairs={{0,1},{1,2},{2,3},{3,0},{4,5},{5,6},{6,7},{7,4},{8,9},{9,10},{10,1... | collective-permute-start | bytes 983048 | tf_op jit(solution)/shard_map/ppermute | solution.py:269
  3.3 9.0 %copy-start.12 = (bf16[1,1024,160]{1,2,0:T(8,128)(2,1)S(1)}, bf16[1,1024,160]{1,2,0:T(8,128)(2,1)}, u32[]{:S(2)}) copy-start(bf16[1,1024,160]{1,2,0:T(8,128)(2,1)} %param.15) | copy-start | bytes 983044
  3.3 14.4 %copy-start.6 = (f32[16,16]{1,0:T(8,128)S(1)}, f32[16,16]{1,0:T(8,128)}, u32[]{:S(2)}) copy-start(f32[16,16]{1,0:T(8,128)} %op_ref.3) | copy-start | bytes 3076
  3.3 14.4 %copy-start.7 = (f32[640]{0:T(1024)S(1)}, f32[640]{0:T(1024)}, u32[]{:S(2)}) copy-start(f32[640]{0:T(1024)} %rates_ref.3) | copy-start | bytes 7684
  3.3 14.4 %copy-start.8 = (s32[32,4]{0,1:T(4,128)S(1)}, s32[32,4]{0,1:T(4,128)}, u32[]{:S(2)}) copy-start(s32[32,4]{0,1:T(4,128)} %param.9) | copy-start | bytes 1540
  8.3 9.3 %collective-permute-start = (bf16[128,640]{1,0:T(8,128)(2,1)}, bf16[128,640]{1,0:T(8,128)(2,1)S(1)}, u32[]{:S(2)}, u32[]{:S(2)}) collective-permute-start(bf16[128,640]{1,0:T(8,128)(2,1)} %get-tuple-element.17), channel_id=1, source_target_pairs={{0,1},{1,2},{2,3},{3,4},{4,5},{5,6},{6,7},{7,8},{8,9},{9,10},{10,1... | collective-permute-start | bytes 491528 | tf_op jit(solution)/shard_map/ppermute | solution.py:263
  8.6 9.0 %collective-permute-start.1 = (bf16[128,640]{1,0:T(8,128)(2,1)}, bf16[128,640]{1,0:T(8,128)(2,1)S(1)}, u32[]{:S(2)}, u32[]{:S(2)}) collective-permute-start(bf16[128,640]{1,0:T(8,128)(2,1)} %get-tuple-element.18), channel_id=1, source_target_pairs={{0,255},{1,0},{2,1},{3,2},{4,3},{5,4},{6,5},{7,6},{8,7},{9,8},{10,... | collective-permute-start | bytes 491528 | tf_op jit(solution)/shard_map/ppermute | solution.py:264
  12.3 17.7 %collective-permute-start.7 = (bf16[160,1024]{1,0:T(8,128)(2,1)S(1)}, bf16[160,1024]{1,0:T(8,128)(2,1)}, u32[]{:S(2)}, u32[]{:S(2)}) collective-permute-start(bf16[160,1024]{1,0:T(8,128)(2,1)S(1)} %bitcast.28), channel_id=1, source_target_pairs={{0,3},{1,0},{2,1},{3,2},{4,7},{5,4},{6,5},{7,6},{8,11},{9,8},{10,9... | collective-permute-start | bytes 983048 | tf_op jit(solution)/shard_map/ppermute | solution.py:270
  17.7 12.3 %collective-permute-start.6 = (bf16[160,1024]{1,0:T(8,128)(2,1)S(1)}, bf16[160,1024]{1,0:T(8,128)(2,1)S(1)}, u32[]{:S(2)}, u32[]{:S(2)}) collective-permute-start(bf16[160,1024]{1,0:T(8,128)(2,1)S(1)} %bitcast.29), channel_id=1, source_target_pairs={{0,1},{1,2},{2,3},{3,0},{4,5},{5,6},{6,7},{7,4},{8,9},{9,10},{10,1... | collective-permute-start | bytes 983048 | tf_op jit(solution)/shard_map/ppermute | solution.py:269
  19.1 14.9 %copy-start = (s32[512,1]{0,1:T(1,128)S(1)}, s32[512,1]{0,1:T(1,128)}, u32[]{:S(2)}) copy-start(s32[512,1]{0,1:T(1,128)} %param.12) | copy-start | bytes 6148
  19.1 14.9 %copy-start.1 = (bf16[1,2,1024,256]{3,2,1,0:T(8,128)(2,1)S(1)}, bf16[1,2,1024,256]{3,2,1,0:T(8,128)(2,1)}, u32[]{:S(2)}) copy-start(bf16[1,2,1024,256]{3,2,1,0:T(8,128)(2,1)} %param.14) | copy-start | bytes 3145732
  22.0 11.6 %collective-permute-start.4 = (bf16[128,640]{1,0:T(8,128)(2,1)S(1)}, bf16[128,640]{1,0:T(8,128)(2,1)S(1)}, u32[]{:S(2)}, u32[]{:S(2)}) collective-permute-start(bf16[128,640]{1,0:T(8,128)(2,1)S(1)} %get-tuple-element.20), channel_id=1, source_target_pairs={{0,1},{1,2},{2,3},{3,4},{4,5},{5,6},{6,7},{7,8},{8,9},{9,10},{10,1... | collective-permute-start | bytes 491528 | tf_op jit(solution)/shard_map/ppermute | solution.py:263
  22.1 11.9 %collective-permute-start.5 = (bf16[128,640]{1,0:T(8,128)(2,1)S(1)}, bf16[128,640]{1,0:T(8,128)(2,1)S(1)}, u32[]{:S(2)}, u32[]{:S(2)}) collective-permute-start(bf16[128,640]{1,0:T(8,128)(2,1)S(1)} %get-tuple-element.21), channel_id=1, source_target_pairs={{0,255},{1,0},{2,1},{3,2},{4,3},{5,4},{6,5},{7,6},{8,7},{9,8},{10,... | collective-permute-start | bytes 491528 | tf_op jit(solution)/shard_map/ppermute | solution.py:264
  30.0 6.8 %copy-start.5 = (bf16[160,1024]{1,0:T(8,128)(2,1)}, bf16[160,1024]{1,0:T(8,128)(2,1)S(1)}, u32[]{:S(2)}) copy-start(bf16[160,1024]{1,0:T(8,128)(2,1)S(1)} %collective-permute-done.6.refs_0_.refs_12_) | copy-start | bytes 983044
  36.8 22.9 %collective-permute-start.10 = (bf16[2,1024,256]{2,1,0:T(8,128)(2,1)}, bf16[2,1024,256]{2,1,0:T(8,128)(2,1)S(1)}, u32[]{:S(2)}, u32[]{:S(2)}) collective-permute-start(bf16[2,1024,256]{2,1,0:T(8,128)(2,1)} %get-tuple-element.24), channel_id=1, source_target_pairs={{0,1},{1,2},{2,3},{3,0},{4,5},{5,6},{6,7},{7,4},{8,9},{9,10},{10,1... | collective-permute-start | bytes 3145736 | tf_op jit(solution)/shard_map/ppermute | solution.py:269
  36.9 22.8 %collective-permute-start.9 = (bf16[2,1024,256]{2,1,0:T(8,128)(2,1)}, bf16[2,1024,256]{2,1,0:T(8,128)(2,1)S(1)}, u32[]{:S(2)}, u32[]{:S(2)}) collective-permute-start(bf16[2,1024,256]{2,1,0:T(8,128)(2,1)} %get-tuple-element.24), channel_id=1, source_target_pairs={{0,3},{1,0},{2,1},{3,2},{4,7},{5,4},{6,5},{7,6},{8,11},{9,8},{10,9... | collective-permute-start | bytes 3145736 | tf_op jit(solution)/shard_map/ppermute | solution.py:270
  39.6 45.7 %all-to-all-start = ((bf16[64,16,640]{2,1,0:T(8,128)(2,1)}), bf16[64,16,640]{2,1,0:T(8,128)(2,1)}, u32[]{:S(2)}, u32[]{:S(2)}) async-start(bf16[64,16,640]{2,1,0:T(8,128)(2,1)} %bitcast.9), calls=%async_computation | async-start | bytes 2621440 | tf_op jit(solution)/shard_map/all_to_all | solution.py:338
  61.4 17.8 %collective-permute-start.11 = (bf16[1024,256]{1,0:T(8,128)(2,1)}, bf16[1024,256]{1,0:T(8,128)(2,1)S(1)}, u32[]{:S(2)}, u32[]{:S(2)}) collective-permute-start(bf16[1024,256]{1,0:T(8,128)(2,1)} %get-tuple-element.25), channel_id=1, source_target_pairs={{0,1},{1,2},{2,3},{3,0},{4,5},{5,6},{6,7},{7,4},{8,9},{9,10},{10,1... | collective-permute-start | bytes 1572872 | tf_op jit(solution)/shard_map/ppermute | solution.py:275
  61.4 17.8 %collective-permute-start.12 = (bf16[1024,256]{1,0:T(8,128)(2,1)}, bf16[1024,256]{1,0:T(8,128)(2,1)S(1)}, u32[]{:S(2)}, u32[]{:S(2)}) collective-permute-start(bf16[1024,256]{1,0:T(8,128)(2,1)} %get-tuple-element.26), channel_id=1, source_target_pairs={{0,3},{1,0},{2,1},{3,2},{4,7},{5,4},{6,5},{7,6},{8,11},{9,8},{10,9... | collective-permute-start | bytes 1572872 | tf_op jit(solution)/shard_map/ppermute | solution.py:275
  64.0 15.1 %collective-permute-start.8 = (bf16[640,256]{1,0:T(8,128)(2,1)}, bf16[640,256]{1,0:T(8,128)(2,1)S(1)}, u32[]{:S(2)}, u32[]{:S(2)}) collective-permute-start(bf16[640,256]{1,0:T(8,128)(2,1)} %collective-permute-done.2.refs_0_.refs_3_), channel_id=1, source_target_pairs={{0,1},{1,2},{2,3},{3,0},{4,5},{5,6},{6,7},{7,4},{8,9},{9,10},{10,1... | collective-permute-start | bytes 983048 | tf_op jit(solution)/shard_map/ppermute | solution.py:275
  64.0 15.1 %collective-permute-start.13 = (bf16[160,1024]{1,0:T(8,128)(2,1)}, bf16[160,1024]{1,0:T(8,128)(2,1)S(1)}, u32[]{:S(2)}, u32[]{:S(2)}) collective-permute-start(bf16[160,1024]{1,0:T(8,128)(2,1)} %collective-permute-done.7.refs_1_.refs_10_), channel_id=1, source_target_pairs={{0,3},{1,0},{2,1},{3,2},{4,7},{5,4},{6,5},{7,6},{8,11},{9,8},{10,9... | collective-permute-start | bytes 983048 | tf_op jit(solution)/shard_map/ppermute | solution.py:275
  79.1 6.1 %copy-start.13 = (bf16[640,256]{1,0:T(8,128)(2,1)}, bf16[640,256]{1,0:T(8,128)(2,1)S(1)}, u32[]{:S(2)}) copy-start(bf16[640,256]{1,0:T(8,128)(2,1)S(1)} %collective-permute-done.8.refs_2_) | copy-start | bytes 983044
  79.2 6.1 %copy-start.14 = (bf16[160,1024]{1,0:T(8,128)(2,1)}, bf16[160,1024]{1,0:T(8,128)(2,1)S(1)}, u32[]{:S(2)}) copy-start(bf16[160,1024]{1,0:T(8,128)(2,1)S(1)} %collective-permute-done.13.refs_11_) | copy-start | bytes 983044
  (6 other events, 20.9 us)

commit v4 on v3

v4 whole, which is shorter than its diff:
```python
import functools

import jax
import jax.numpy as jnp
from jax import lax
from jax.experimental import pallas as pl
from jax.experimental.pallas import tpu as pltpu
from jax.sharding import PartitionSpec as P

F32 = jnp.float32
BF16 = jnp.bfloat16
POINTS = 16
SIDE = 4
DEVICE_AXES = ("elem", "sec")
NT = (((1,), (1,)), ((), ()))
VMEM_LIMIT = 40 * 1024 * 1024


def iota(shape, axis):
    return lax.broadcasted_iota(jnp.int32, shape, axis)


def ones_where(mask):
    return jnp.where(mask, 1.0, 0.0).astype(BF16)


def mul(a, b):
    return jnp.dot(a, b, preferred_element_type=F32)


def mul_nt(a, b):
    return lax.dot_general(a, b, NT, preferred_element_type=F32)


def halves(x):
    high = x.astype(BF16)
    return high, (x - high.astype(F32)).astype(BF16)


def operator_blocks(op):
    size = POINTS * POINTS
    repeat = ones_where((iota((size, POINTS), 0) & (POINTS - 1)) == iota((size, POINTS), 1))
    same = (iota((size, size), 0) >> 4) == (iota((size, size), 1) >> 4)
    blocks = []
    for part in halves(op):
        tall = mul(repeat, part).astype(BF16)
        blocks.append(jnp.where(same, mul_nt(tall, repeat), 0.0).astype(BF16))
    return blocks


def neighbour_columns(nbt):
    count = nbt.shape[1]
    rows = count * POINTS
    spread = ones_where((iota((rows, count), 0) >> 4) == iota((rows, count), 1))
    local = (nbt & (count - 1)).astype(F32).astype(BF16)
    return mul_nt(spread, local)


def near_mask(rows, nbt):
    near = neighbour_columns(nbt)
    place = iota((rows, 1), 0) & (POINTS - 1)
    column = place & (SIDE - 1)
    west = column == 0
    east = column == SIDE - 1
    placef = place.astype(F32)
    source = jnp.where(
        west,
        near[:, 0:1] * POINTS + placef + (SIDE - 1),
        jnp.where(east, near[:, 1:2] * POINTS + placef - (SIDE - 1), -1.0),
    )
    return ones_where(iota((rows, rows), 1).astype(F32) == source), west | east


def advance(state, blocks, rates, mask):
    size = POINTS * POINTS
    op_high, op_low = blocks
    pick, on_edge = mask
    moved = []
    for start in range(0, state.shape[0], size):
        high, low = halves(state[start : start + size])
        moved.append(mul(op_high, high) + (mul(op_high, low) + mul(op_low, high)))
    first = state + rates * jnp.concatenate(moved, axis=0)
    high, low = halves(first)
    far = mul(pick, high) + mul(pick, low)
    return jnp.where(on_edge, 0.5 * (first + far), first)


def edge_rows(shape, axis, first):
    row = iota(shape, axis) + first
    part = row & (POINTS * SIDE - 1)
    element = ((row >> 7) << 4) + (part >> 2)
    return element, (row >> 6) & 1, part & (SIDE - 1)


def edge_advance(state, op, rates, nbt):
    size = POINTS * POINTS
    half = size // 2
    count = nbt.shape[1]
    element, side, place = edge_rows((half, 1), 0, 0)
    point = place + (1 - side) * (POINTS - SIDE)
    here = ones_where(iota((half, size), 1) == element * POINTS + point)
    same = (iota((half, size), 1) >> 4) == element
    rows = ones_where(iota((half, POINTS), 1) == point)
    repeat = ones_where((iota((size, POINTS), 0) & (POINTS - 1)) == iota((size, POINTS), 1))
    op_high, op_low = (
        jnp.where(same, mul_nt(mul(rows, part).astype(BF16), repeat), 0.0).astype(BF16) for part in halves(op)
    )
    first = []
    for start in range(0, state.shape[0], size):
        high, low = halves(state[start : start + size])
        moved = mul(op_high, high) + (mul(op_high, low) + mul(op_low, high))
        first.append(mul(here, high) + mul(here, low) + rates * moved)
    first = jnp.concatenate(first, axis=0)
    total = first.shape[0]
    element, side, place = edge_rows((total, 1), 0, 0)
    spread = ones_where(iota((total, count), 1) == element)
    near = mul_nt(spread, (nbt & (count - 1)).astype(F32).astype(BF16)).astype(jnp.int32)
    west = place == 0
    east = place == SIDE - 1
    other = jnp.where(west, near[:, 0:1], near[:, 1:2])
    there = ((other >> 4) << 7) + (side << 6) + ((other & (POINTS - 1)) << 2) + jnp.where(west, SIDE - 1, 0)
    pick = ones_where(iota((total, total), 1) == jnp.where(west | east, there, -1))
    high, low = halves(first)
    far = mul(pick, high) + mul(pick, low)
    second = jnp.where(west | east, 0.5 * (first + far), first).astype(BF16)
    quarter = half // 2
    north = [second[i : i + quarter] for i in range(0, total, half)]
    south = [second[i + quarter : i + half] for i in range(0, total, half)]
    return jnp.concatenate(north, axis=0), jnp.concatenate(south, axis=0)


def meet(second, below, above, nbt):
    rows = second.shape[0]
    count = below.shape[0]
    near = neighbour_columns(nbt)
    place = iota((rows, 1), 0) & (POINTS - 1)
    south = place < SIDE
    north = place >= POINTS - SIDE
    placef = place.astype(F32)
    source = jnp.where(
        south,
        near[:, 2:3] * SIDE + placef,
        jnp.where(north, near[:, 3:4] * SIDE + placef + (count - (POINTS - SIDE)), -1.0),
    )
    pick = ones_where(iota((rows, 2 * count), 1).astype(F32) == source)
    far = mul(pick, jnp.concatenate([below, above], axis=0))
    return jnp.where(south | north, 0.5 * (second + far), second)


def start_edge_kernel(
    state_ref, nbt_ref, op_ref, rates_ref, north_ref, south_ref, state, nbt, op, rates, sems
):
    pairs = [(state_ref, state), (nbt_ref, nbt), (op_ref, op), (rates_ref, rates)]
    copies = [pltpu.make_async_copy(a, b, sems.at[i]) for i, (a, b) in enumerate(pairs)]
    for copy in copies:
        copy.start()
    for copy in copies:
        copy.wait()
    north_ref[...], south_ref[...] = edge_advance(state[...], op[...], rates[...].reshape(1, -1), nbt[...])


def start_kernel(capacity, groups, state_ref, nbt_ref, op_ref, rates_ref, ids_ref, second_ref, pick_ref):
    state = state_ref[...]
    mask = near_mask(state.shape[0], nbt_ref[...])
    second_ref[...] = advance(state, operator_blocks(op_ref[...]), rates_ref[...].reshape(1, -1), mask)
    rows = state.shape[0]
    named = iota((groups, rows), 0) == ids_ref[...]
    upto = ones_where(iota((rows, rows), 0) <= iota((rows, rows), 1))
    rank = mul(ones_where(named), upto)
    base = (iota((groups, rows), 0) * capacity - 1).astype(F32)
    slot = jnp.sum(jnp.where(named, base + rank, 0.0), axis=0, keepdims=True)
    pick_ref[...] = ones_where(iota((groups * capacity, rows), 0).astype(F32) == slot)


def step_edge_kernel(
    prev_ref, below_ref, above_ref, nbt_ref, op_ref, rates_ref, *refs
):
    north_ref, south_ref = refs[-2:]
    nbt = nbt_ref[...]
    state = meet(prev_ref[...], below_ref[...], above_ref[...], nbt)
    north_ref[...], south_ref[...] = edge_advance(state, op_ref[...], rates_ref[...].reshape(1, -1), nbt)


def step_kernel(prev_ref, below_ref, above_ref, nbt_ref, op_ref, rates_ref, second_ref):
    nbt = nbt_ref[...]
    state = meet(prev_ref[...], below_ref[...], above_ref[...], nbt)
    mask = near_mask(state.shape[0], nbt)
    second_ref[...] = advance(state, operator_blocks(op_ref[...]), rates_ref[...].reshape(1, -1), mask)


def send_kernel(
    prev_ref, below_ref, above_ref, nbt_ref, pick_ref, hidden_ref, *refs
):
    state_ref, out_ref, *copy_refs, sem = refs[-5:]
    hand_on = [pltpu.make_async_copy(hidden_ref.at[i], copy_refs[i], sem.at[i]) for i in range(2)]
    for copy in hand_on:
        copy.start()
    state = meet(prev_ref[...], below_ref[...], above_ref[...], nbt_ref[...])
    state_ref[...] = state
    out_ref[...] = mul(pick_ref[...], state.astype(BF16)).astype(BF16)
    for copy in hand_on:
        copy.wait()


def add_kernel(capacity, groups, state_ref, back_ref, ids_ref, out_ref):
    rows = state_ref.shape[0]
    same = ones_where(iota((rows, rows), 0) == iota((rows, rows), 1))
    ids = jnp.broadcast_to(ids_ref[...].astype(F32).astype(BF16), (8, rows))
    regime = mul_nt(same, ids)[:, 0:1]
    lanes = iota((rows, groups), 1)
    named = lanes.astype(F32) == regime
    upto = ones_where(iota((rows, rows), 1) <= iota((rows, rows), 0))
    rank = mul(upto, ones_where(named))
    base = (lanes * capacity - 1).astype(F32)
    slot = jnp.sum(jnp.where(named, base + rank, 0.0), axis=1, keepdims=True)
    pick = ones_where(iota((rows, groups * capacity), 1).astype(F32) == slot)
    out_ref[...] = state_ref[...] + mul(pick, back_ref[...])


def pass_kernel(in_ref, out_ref):
    pass


def silu(v):
    half = 0.5 * v
    return (half + half * jnp.tanh(half)).astype(BF16)


def network_kernel(tile, sec_ref, rows_ref, *refs):
    first_in, hidden_in, last_in, out_ref = refs[0:4], refs[4:11], refs[11:15], refs[15]
    first, middle, last, hold_a, hold_b, rows, result, sems, row_sems, out_sems = refs[16:]
    layers = middle.shape[1]
    tiles = rows.shape[0]
    places = [(sec_ref[0] + k) & 3 for k in range(4)]
    width = first.shape[2]
    at = [pl.ds(step * tile, tile) for step in range(tiles)]
    incoming = [pltpu.make_async_copy(rows_ref.at[at[i]], rows.at[i], row_sems.at[i]) for i in range(tiles)]
    outgoing = [pltpu.make_async_copy(result.at[i], out_ref.at[at[i]], out_sems.at[i]) for i in range(tiles)]
    weights = [[] for _ in range(layers + 2)]
    for k in range(4):
        pairs = [(first_in[k], first.at[places[k]], 0)]
        for layer in range(layers):
            source = hidden_in[2 * k - 1 + layer] if k else hidden_in[0].at[layer]
            pairs += [(source, middle.at[places[k], layer], 1 + layer)]
        pairs += [(last_in[k], last.at[places[k]], 1 + layers)]
        for source, target, group in pairs:
            weights[group].append(pltpu.make_async_copy(source, target, sems.at[k, group]))
    groups = [[*incoming, *weights[0]], *weights[1:]]

    def begin(group):
        for copy in groups[group]:
            copy.start()

    def arrived(group):
        for copy in groups[group]:
            copy.wait()
        if group + 1 < len(groups):
            begin(group + 1)

    columns = [pl.ds(k * width, width) for k in range(4)]
    begin(0)
    arrived(0)
    for step in range(tiles):
        for k in range(4):
            hold_a[step, :, columns[k]] = silu(mul(rows[step], first[k]))
    now, later = hold_a, hold_b
    for layer in range(layers):
        arrived(1 + layer)
        for step in range(tiles):
            for k in range(4):
                later[step, :, columns[k]] = silu(mul(now[step], middle[k, layer]))
        now, later = later, now
    arrived(1 + layers)
    matrix = last[...].reshape(out_ref.shape[1], now.shape[2])
    for step in range(tiles):
        result[step] = mul_nt(now[step], matrix).astype(BF16)
        outgoing[step].start()
    for copy in outgoing:
        copy.wait()


def call(kernel, out, *args, passed=(), scratch=(), flops=0, specs=None, outs=None, aliases=None, limit=VMEM_LIMIT):
    size = sum(a.size * a.dtype.itemsize for a in args)
    size += sum(o.size * o.dtype.itemsize for o in out)
    vmem = pl.BlockSpec(memory_space=pltpu.VMEM)
    return pl.pallas_call(
        kernel,
        out_shape=[jax.ShapeDtypeStruct(o.shape, o.dtype) for o in out],
        in_specs=(specs or [vmem] * len(args)) + [pl.BlockSpec(memory_space=pl.ANY)] * len(passed),
        out_specs=outs or [vmem] * len(out),
        scratch_shapes=scratch,
        input_output_aliases=aliases or {},
        compiler_params=pltpu.CompilerParams(vmem_limit_bytes=limit),
        cost_estimate=pl.CostEstimate(flops=flops, bytes_accessed=size, transcendentals=0),
    )(*args, *passed)


def ring(count, step):
    return [(i, (i + step) % count) for i in range(count)]


def exchange(north, south):
    total = lax.axis_size(DEVICE_AXES)
    below = lax.ppermute(north, DEVICE_AXES, ring(total, 1))
    above = lax.ppermute(south, DEVICE_AXES, ring(total, -1))
    return below, above


def from_sides(*shards):
    below = [lax.ppermute(x, "sec", ring(4, 1)) for x in shards]
    above = [lax.ppermute(x, "sec", ring(4, -1)) for x in shards]
    return below, above


def from_far(below, above):
    return lax.ppermute(below, "sec", ring(4, 1)), lax.ppermute(above, "sec", ring(4, -1))


def on_device(
    fields, neighbours, operator, rates, regime_ids, input_proj, hidden_proj, output_proj
):
    count, points, width = fields.shape
    rows_dev = count * points
    groups = lax.axis_size("elem")
    capacity = 2 * rows_dev // groups
    slots = groups * capacity
    shape = jax.ShapeDtypeStruct
    nbt = neighbours.T
    ids = regime_ids.T

    mine = (input_proj[0], output_proj[0].T)
    below, above = from_sides(*mine)
    first, last = ([m, a, None, b] for m, a, b in zip(mine, above, below))
    first[2], last[2] = from_far(below[0], above[1])
    anywhere = pl.BlockSpec(memory_space=pl.ANY)
    vmem = pl.BlockSpec(memory_space=pltpu.VMEM)

    edge = shape((count * SIDE, width), BF16)
    inner = shape((rows_dev, width), F32)
    start = fields.reshape(rows_dev, width)
    north, south = call(
        start_edge_kernel, [edge] * 2, start, nbt, operator, rates,
        scratch=[
            pltpu.VMEM((rows_dev, width), F32),
            pltpu.VMEM(nbt.shape, jnp.int32),
            pltpu.VMEM(operator.shape, F32),
            pltpu.VMEM(rates.shape, F32),
            pltpu.SemaphoreType.DMA((4,)),
        ],
        specs=[anywhere] * 4,
        limit=58 * 1024 * 1024,
        flops=2 * 10**9,
    )
    prev, next_ = exchange(north, south)
    second, pick = call(
        functools.partial(start_kernel, capacity, groups),
        [inner, shape((slots, rows_dev), BF16)],
        start, nbt, operator, rates, ids, flops=3 * 10**9,
    )
    step_args = (second, prev, next_, nbt, operator, rates)
    north, south = call(
        step_edge_kernel, [edge] * 2, *step_args, passed=(below[0], above[0]), flops=2 * 10**9
    )
    (second,) = call(step_kernel, [inner], *step_args, flops=3 * 10**9)
    prev, next_ = exchange(north, south)
    state, outgoing, *layer = call(
        send_kernel,
        [
            shape((rows_dev, width), F32),
            shape((slots, width), BF16),
            *[shape(hidden_proj.shape[2:], BF16)] * 2,
        ],
        second, prev, next_, nbt, pick, hidden_proj[0],
        passed=(below[1], above[1]),
        specs=[vmem] * 5 + [anywhere],
        outs=[vmem] * 2 + [anywhere] * 2,
        scratch=[pltpu.SemaphoreType.DMA((2,))],
        flops=3 * 10**9,
    )
    hidden_below, hidden_above = from_sides(*layer)
    (low,) = call(
        pass_kernel, [layer[0]], hidden_below[0],
        specs=[anywhere], outs=[anywhere], aliases={0: 0}, limit=58 * 1024 * 1024, flops=60 * 10**9,
    )
    far = from_far(low, hidden_above[1])
    incoming = lax.all_to_all(
        outgoing.reshape(groups, capacity, width), "elem", split_axis=0, concat_axis=0, tiled=True
    )
    hid = hidden_proj.shape[2]
    tile = 512
    sec = lax.axis_index("sec").astype(jnp.int32).reshape(1)
    (result,) = call(
        functools.partial(network_kernel, tile),
        [shape((slots, width), BF16)],
        sec, incoming.reshape(slots, width), *first, hidden_proj[0], *hidden_above, *far, low, hidden_below[1], *last,
        scratch=[
            pltpu.VMEM((4, *input_proj.shape[1:2], hid // 4), BF16),
            pltpu.VMEM((4, *hidden_proj.shape[1:3], hid // 4), BF16),
            pltpu.VMEM((4, width // 4, hid), BF16),
            pltpu.VMEM((slots // tile, tile, hid), BF16),
            pltpu.VMEM((slots // tile, tile, hid), BF16),
            pltpu.VMEM((slots // tile, tile, width), BF16),
            pltpu.VMEM((slots // tile, tile, width), BF16),
            pltpu.SemaphoreType.DMA((4, 2 + hidden_proj.shape[1])),
            pltpu.SemaphoreType.DMA((slots // tile,)),
            pltpu.SemaphoreType.DMA((slots // tile,)),
        ],
        specs=[pl.BlockSpec(memory_space=pltpu.SMEM)] + [anywhere] * 16,
        outs=[anywhere],
        limit=58 * 1024 * 1024,
        flops=7 * 10**9,
    )
    returned = lax.all_to_all(
        result.reshape(groups, capacity, width), "elem", split_axis=0, concat_axis=0, tiled=True
    )
    (updated,) = call(
        functools.partial(add_kernel, capacity, groups),
        [shape((rows_dev, width), F32)],
        state, returned.reshape(slots, width), ids, flops=10**9,
    )
    return updated.reshape(count, points, width)


def solution(mesh):
    return jax.shard_map(
        on_device,
        mesh=mesh,
        in_specs=(
            P(DEVICE_AXES, None, None),
            P(DEVICE_AXES, None),
            P(),
            P(),
            P(DEVICE_AXES, None),
            P("elem", None, "sec"),
            P("elem", None, None, "sec"),
            P("elem", None, "sec"),
        ),
        out_specs=P(DEVICE_AXES, None, None),
        check_vma=False,
    )
```

time: 149 us -> 144 us (0.966)
  blocking collectives: 47.2 us -> 41 us
  local copies, waits for them, and re-layouts: 1.91 us -> 0.05 us
    ppermute x2, waiting for transfers between devices: 0.01 us -> 13.7 us  [from_far(): lax.ppermute(above, 'sec', ring(4, -1))]
    ppermute x2, waiting for transfers between devices: 12.4 us -> 1.74 us  [from_far(): lax.ppermute(below, 'sec', ring(4, 1))]
    ppermute x3 -> x4, waiting for transfers between devices: 8.01 us -> 0.01 us  [from_sides(): below = [lax.ppermute(x, 'sec', ring(4, 1)) for x in shards]]
    all_to_all x1, blocking collectives: 47.2 us -> 41 us  [on_device(): lax.all_to_all(result.reshape(groups, capacity, width), 'elem', split_axi...]
    all_to_all x1, waiting for transfers between devices: 6.07 us -> 11.4 us  [on_device(): lax.all_to_all(outgoing.reshape(groups, capacity, width), 'elem', split_a...]
    ppermute x3 -> x4, waiting for transfers between devices: 0.01 us -> 2.76 us  [from_sides(): above = [lax.ppermute(x, 'sec', ring(4, -1)) for x in shards]]
    ppermute x3 -> x4, starting transfers between devices: 6.62 us -> 9.3 us  [from_sides(): above = [lax.ppermute(x, 'sec', ring(4, -1)) for x in shards]]
    ppermute x2, waiting for transfers between devices: 8.26 us -> 6.17 us  [exchange(): below = lax.ppermute(north, DEVICE_AXES, ring(total, 1))]
  transfers between devices with their start and end apart: 15 -> 17, of which waited for: 6 -> 6; matrix products, arithmetic and copies ran while one was open for 0% -> 0% of each run, Pallas kernels for 6% -> 8%
where the time goes in v4:
time: 144 us; the launch traced here: 143 us
  blocking collectives  41 us (28%)
  starting transfers between devices  37.4 us (26%)
  waiting for transfers between devices  35.8 us (25%)
  Pallas kernels  28.4 us (20%)
    all_to_all x1, blocking collectives, on_device(): lax.all_to_all(result.reshape(groups, capacity, width), 'elem', split_axi...  41 us
    pallas_call x8, Pallas kernels, call(): pl.pallas_call(kernel, out_shape=[jax.ShapeDtypeStruct(o.shape, o.dtype)...  28.4 us
    ppermute x2, waiting for transfers between devices, from_far(): lax.ppermute(above, 'sec', ring(4, -1))  13.7 us
    all_to_all x1, starting transfers between devices, on_device(): lax.all_to_all(outgoing.reshape(groups, capacity, width), 'elem', split_a...  13.4 us
    all_to_all x1, waiting for transfers between devices, on_device(): lax.all_to_all(outgoing.reshape(groups, capacity, width), 'elem', split_a...  11.4 us
    ppermute x2, starting transfers between devices, exchange(): above = lax.ppermute(south, DEVICE_AXES, ring(total, -1))  10.3 us
    ppermute x4, starting transfers between devices, from_sides(): above = [lax.ppermute(x, 'sec', ring(4, -1)) for x in shards]  9.3 us
    ppermute x2, waiting for transfers between devices, exchange(): below = lax.ppermute(north, DEVICE_AXES, ring(total, 1))  6.17 us
  transfers between devices with their start and end apart: 17, of which 6 were waited for; matrix products, arithmetic and copies ran while one was open for 0% of the time, Pallas kernels for 8%

profile of v4, /device:TPU:1, one launch (start us, length us, event | category | flops | bytes accessed | tf_op | source)
XLA Modules:
  0.0 142.9 jit_solution(5720545351337088405)
XLA Ops:
  0.0 3.3 %collective-permute-start.3 = (bf16[640,256]{1,0:T(8,128)(2,1)}, bf16[640,256]{1,0:T(8,128)(2,1)S(1)}, u32[]{:S(2)}, u32[]{:S(2)}) collective-permute-start(bf16[640,256]{1,0:T(8,128)(2,1)} %bitcast.27), channel_id=1, source_target_pairs={{0,3},{1,0},{2,1},{3,2},{4,7},{5,4},{6,5},{7,6},{8,11},{9,8},{10,9... | collective-permute-start | bytes 983048 | tf_op jit(solution)/shard_map/ppermute | solution.py:311
  3.4 3.7 %shard_map.83 = (bf16[128,640]{1,0:T(8,128)(2,1)}, bf16[128,640]{1,0:T(8,128)(2,1)}) custom-call(f32[512,640]{1,0:T(8,128)} %bitcast.17, s32[4,32]{1,0:T(4,128)} %bitcast.21, f32[16,16]{1,0:T(8,128)} %op_ref.7, f32[640]{0:T(1024)} %rates_ref.7), custom_call_target="tpu_custom_call" | custom-call | flops 2000000000 | bytes 1642496 | tf_op jit(solution)/shard_map/pallas_call | solution.py:286
  7.1 0.3 collective-permute-start
  7.3 3.7 %collective-permute-start.1 = (bf16[128,640]{1,0:T(8,128)(2,1)}, bf16[128,640]{1,0:T(8,128)(2,1)S(1)}, u32[]{:S(2)}, u32[]{:S(2)}) collective-permute-start(bf16[128,640]{1,0:T(8,128)(2,1)} %get-tuple-element.17), channel_id=1, source_target_pairs={{0,255},{1,0},{2,1},{3,2},{4,3},{5,4},{6,5},{7,6},{8,7},{9,8},{10,... | collective-permute-start | bytes 491528 | tf_op jit(solution)/shard_map/ppermute | solution.py:305
  11.0 0.7 collective-permute-start.7
  11.7 2.4 %shard_map.82 = (f32[512,640]{1,0:T(8,128)S(1)}, bf16[1024,512]{1,0:T(8,128)(2,1)S(1)}) custom-call(f32[512,640]{1,0:T(8,128)S(1)} %bitcast.18, s32[4,32]{1,0:T(4,128)S(1)} %bitcast.22, f32[16,16]{1,0:T(8,128)S(1)} %copy-done.7, f32[640]{0:T(1024)S(1)} %copy-done.8, s32[1,512]{1,0:T(1,128)S(1)} %bitcast.15), custom_call_target="tpu_custom_call" | custom-call | flops 3000000000 | bytes 3676160 | tf_op jit(solution)/shard_map/pallas_call | solution.py:286
  14.1 3.6 %collective-permute-done.below_ref = bf16[128,640]{1,0:T(8,128)(2,1)S(1)} collective-permute-done((bf16[128,640]{1,0:T(8,128)(2,1)}, bf16[128,640]{1,0:T(8,128)(2,1)S(1)}, u32[]{:S(2)}, u32[]{:S(2)}) %collective-permute-start) | collective-permute-done | bytes 163872 | tf_op jit(solution)/shard_map/ppermute | solution.py:304
  17.7 2.2 %shard_map.85 = (bf16[128,640]{1,0:T(8,128)(2,1)S(1)}, bf16[128,640]{1,0:T(8,128)(2,1)S(1)}) custom-call(f32[512,640]{1,0:T(8,128)S(1)} %get-tuple-element.15.prev_ref, bf16[128,640]{1,0:T(8,128)(2,1)S(1)} %collective-permute-done.below_ref, bf16[128,640]{1,0:T(8,128)(2,1)S(1)} %collective-permute-done.1.above_ref, s32[4,32]{1,0:T(4,128)S(1)} %bitcast.23, ...), custom_call_target="tpu_custom_call" | custom-call | flops 2000000000 | bytes 1970176 | tf_op jit(solution)/shard_map/pallas_call | solution.py:286
  20.0 6.6 %collective-permute-start.5 = (bf16[128,640]{1,0:T(8,128)(2,1)S(1)}, bf16[128,640]{1,0:T(8,128)(2,1)S(1)}, u32[]{:S(2)}, u32[]{:S(2)}) collective-permute-start(bf16[128,640]{1,0:T(8,128)(2,1)S(1)} %get-tuple-element.19), channel_id=1, source_target_pairs={{0,255},{1,0},{2,1},{3,2},{4,3},{5,4},{6,5},{7,6},{8,7},{9,8},{10,... | collective-permute-start | bytes 491528 | tf_op jit(solution)/shard_map/ppermute | solution.py:305
  26.6 2.6 %shard_map.84.prev_ref = f32[512,640]{1,0:T(8,128)S(1)} custom-call(f32[512,640]{1,0:T(8,128)S(1)} %get-tuple-element.15.prev_ref, bf16[128,640]{1,0:T(8,128)(2,1)S(1)} %collective-permute-done.below_ref, bf16[128,640]{1,0:T(8,128)(2,1)S(1)} %collective-permute-done.1.above_ref, s32[4,32]{1,0:T(4,128)S(1)} %bitcast.24, f32[16,16]{1,0:T(8,128)S(1)} %copy-done.7, ...), custom_call_target="tpu_custom_call" | custom-call | flops 3000000000 | bytes 2953216 | tf_op jit(solution)/shard_map/pallas_call | solution.py:286
  29.2 2.6 %collective-permute-done.4.below_ref = bf16[128,640]{1,0:T(8,128)(2,1)S(1)} collective-permute-done((bf16[128,640]{1,0:T(8,128)(2,1)S(1)}, bf16[128,640]{1,0:T(8,128)(2,1)S(1)}, u32[]{:S(2)}, u32[]{:S(2)}) %collective-permute-start.4) | collective-permute-done | bytes 163872 | tf_op jit(solution)/shard_map/ppermute | solution.py:304
  31.8 2.8 %shard_map.86 = (f32[512,640]{1,0:T(8,128)S(1)}, bf16[1024,640]{1,0:T(8,128)(2,1)}, bf16[1024,256]{1,0:T(8,128)(2,1)S(1)}, bf16[1024,256]{1,0:T(8,128)(2,1)S(1)}) custom-call(f32[512,640]{1,0:T(8,128)S(1)} %shard_map.84.prev_ref, bf16[128,640]{1,0:T(8,128)(2,1)S(1)} %collective-permute-done.4.below_ref, ...), custom_call_target="tpu_custom_call" | custom-call | flops 3000000000 | bytes 7406080 | tf_op jit(solution)/shard_map/pallas_call | solution.py:286
  34.8 2.7 %collective-permute-start.9 = (bf16[1024,256]{1,0:T(8,128)(2,1)S(1)}, bf16[1024,256]{1,0:T(8,128)(2,1)S(1)}, u32[]{:S(2)}, u32[]{:S(2)}) collective-permute-start(bf16[1024,256]{1,0:T(8,128)(2,1)S(1)} %get-tuple-element.23), channel_id=1, source_target_pairs={{0,3},{1,0},{2,1},{3,2},{4,7},{5,4},{6,5},{7,6},{8,11},{9,8},{10,9... | collective-permute-start | bytes 1572872 | tf_op jit(solution)/shard_map/ppermute | solution.py:311
  37.5 2.7 %collective-permute-start.10 = (bf16[1024,256]{1,0:T(8,128)(2,1)S(1)}, bf16[1024,256]{1,0:T(8,128)(2,1)}, u32[]{:S(2)}, u32[]{:S(2)}) collective-permute-start(bf16[1024,256]{1,0:T(8,128)(2,1)S(1)} %get-tuple-element.24), channel_id=1, source_target_pairs={{0,3},{1,0},{2,1},{3,2},{4,7},{5,4},{6,5},{7,6},{8,11},{9,8},{10,9... | collective-permute-start | bytes 1572872 | tf_op jit(solution)/shard_map/ppermute | solution.py:311
  40.2 13.4 %all-to-all-start = ((bf16[64,16,640]{2,1,0:T(8,128)(2,1)}), bf16[64,16,640]{2,1,0:T(8,128)(2,1)}, u32[]{:S(2)}, u32[]{:S(2)}) async-start(bf16[64,16,640]{2,1,0:T(8,128)(2,1)} %bitcast.9), calls=%async_computation | async-start | bytes 2621440 | tf_op jit(solution)/shard_map/all_to_all | solution.py:386
  53.7 2.8 %collective-permute-done.10.refs_6_ = bf16[1024,256]{1,0:T(8,128)(2,1)} collective-permute-done((bf16[1024,256]{1,0:T(8,128)(2,1)S(1)}, bf16[1024,256]{1,0:T(8,128)(2,1)}, u32[]{:S(2)}, u32[]{:S(2)}) %collective-permute-start.10) | collective-permute-done | bytes 524320 | tf_op jit(solution)/shard_map/ppermute | solution.py:311
  56.5 3.5 %collective-permute-start.13 = (bf16[1024,256]{1,0:T(8,128)(2,1)}, bf16[1024,256]{1,0:T(8,128)(2,1)}, u32[]{:S(2)}, u32[]{:S(2)}) collective-permute-start(bf16[1024,256]{1,0:T(8,128)(2,1)} %collective-permute-done.10.refs_6_), channel_id=1, source_target_pairs={{0,3},{1,0},{2,1},{3,2},{4,7},{5,4},{6,5},{7,6},{8,11},{9,8},{10,9... | collective-permute-start | bytes 1572872 | tf_op jit(solution)/shard_map/ppermute | solution.py:316
  60.0 0.3 collective-permute-start.15
  60.3 13.7 %collective-permute-done.15.refs_13_ = bf16[160,1024]{1,0:T(8,128)(2,1)} collective-permute-done((bf16[160,1024]{1,0:T(8,128)(2,1)S(1)}, bf16[160,1024]{1,0:T(8,128)(2,1)}, u32[]{:S(2)}, u32[]{:S(2)}) %collective-permute-start.15) | collective-permute-done | bytes 327712 | tf_op jit(solution)/shard_map/ppermute | solution.py:316
  74.0 1.7 %collective-permute-done.12.refs_7_ = bf16[1024,256]{1,0:T(8,128)(2,1)} collective-permute-done((bf16[1024,256]{1,0:T(8,128)(2,1)}, bf16[1024,256]{1,0:T(8,128)(2,1)}, u32[]{:S(2)}, u32[]{:S(2)}) %collective-permute-start.12) | collective-permute-done | bytes 524320 | tf_op jit(solution)/shard_map/ppermute | solution.py:316
  75.7 11.4 %all-to-all-done = bf16[64,16,640]{2,1,0:T(8,128)(2,1)} async-done(((bf16[64,16,640]{2,1,0:T(8,128)(2,1)}), bf16[64,16,640]{2,1,0:T(8,128)(2,1)}, u32[]{:S(2)}, u32[]{:S(2)}) %all-to-all-start) | async-done | bytes 1310752 | tf_op jit(solution)/shard_map/all_to_all | solution.py:386
  87.1 11.9 %shard_map.88 = bf16[1024,640]{1,0:T(8,128)(2,1)} custom-call(s32[1]{0:T(128)} %bitcast.8.sec_ref, bf16[1024,640]{1,0:T(8,128)(2,1)} %bitcast.10.rows_ref, bf16[640,256]{1,0:T(8,128)(2,1)} %bitcast.29, bf16[640,256]{1,0:T(8,128)(2,1)} %copy-done.3, bf16[640,256]{1,0:T(8,128)(2,1)} %collective-permute-done.8.refs_2_, ...), custom_call_target="tpu_custom_call" | custom-call | flops 7000000000 | bytes 9437188 | tf_op jit(solution)/shard_map/pallas_call | solution.py:286
  99.1 41.0 %all_to_all.10 = bf16[64,16,640]{2,1,0:T(8,128)(2,1)S(1)} all-to-all(bf16[64,16,640]{2,1,0:T(8,128)(2,1)} %bitcast.26), channel_id=1, replica_groups=mesh['elem'=64,'sec'=4] {'elem'}, dimensions={0} | all-to-all | bytes 2621440 | tf_op jit(solution)/shard_map/all_to_all | solution.py:413
  140.1 2.8 %shard_map.89 = f32[512,640]{1,0:T(8,128)} custom-call(f32[512,640]{1,0:T(8,128)S(1)} %get-tuple-element.21.state_ref, bf16[1024,640]{1,0:T(8,128)(2,1)S(1)} %bitcast.14, s32[1,512]{1,0:T(1,128)S(1)} %bitcast.16), custom_call_target="tpu_custom_call" | custom-call | flops 1000000000 | bytes 3934208 | tf_op jit(solution)/shard_map/pallas_call | solution.py:286
  (43 shorter events, 0.4 us)
Async XLA Ops:
  0.0 17.7 %collective-permute-start.3 = (bf16[640,256]{1,0:T(8,128)(2,1)}, bf16[640,256]{1,0:T(8,128)(2,1)S(1)}, u32[]{:S(2)}, u32[]{:S(2)}) collective-permute-start(bf16[640,256]{1,0:T(8,128)(2,1)} %bitcast.27), channel_id=1, source_target_pairs={{0,3},{1,0},{2,1},{3,2},{4,7},{5,4},{6,5},{7,6},{8,11},{9,8},{10,9... | collective-permute-start | bytes 983048 | tf_op jit(solution)/shard_map/ppermute | solution.py:311
  3.3 14.4 %collective-permute-start.2 = (bf16[640,256]{1,0:T(8,128)(2,1)}, bf16[640,256]{1,0:T(8,128)(2,1)}, u32[]{:S(2)}, u32[]{:S(2)}) collective-permute-start(bf16[640,256]{1,0:T(8,128)(2,1)} %bitcast.28), channel_id=1, source_target_pairs={{0,1},{1,2},{2,3},{3,0},{4,5},{5,6},{6,7},{7,4},{8,9},{9,10},{10,1... | collective-permute-start | bytes 983048 | tf_op jit(solution)/shard_map/ppermute | solution.py:310
  3.3 8.4 %copy-start = (s32[512,1]{0,1:T(1,128)S(1)}, s32[512,1]{0,1:T(1,128)}, u32[]{:S(2)}) copy-start(s32[512,1]{0,1:T(1,128)} %param.12) | copy-start | bytes 6148
  3.3 8.4 %copy-start.1 = (f32[32,16,640]{2,1,0:T(8,128)S(1)}, f32[32,16,640]{2,1,0:T(8,128)}, u32[]{:S(2)}) copy-start(f32[32,16,640]{2,1,0:T(8,128)} %param.8) | copy-start | bytes 3932164
  3.3 8.4 %copy-start.7 = (f32[16,16]{1,0:T(8,128)S(1)}, f32[16,16]{1,0:T(8,128)}, u32[]{:S(2)}) copy-start(f32[16,16]{1,0:T(8,128)} %op_ref.7) | copy-start | bytes 3076
  3.3 8.4 %copy-start.8 = (f32[640]{0:T(1024)S(1)}, f32[640]{0:T(1024)}, u32[]{:S(2)}) copy-start(f32[640]{0:T(1024)} %rates_ref.7) | copy-start | bytes 7684
  3.3 8.4 %copy-start.9 = (s32[32,4]{0,1:T(4,128)S(1)}, s32[32,4]{0,1:T(4,128)}, u32[]{:S(2)}) copy-start(s32[32,4]{0,1:T(4,128)} %param.9) | copy-start | bytes 1540
  7.1 10.6 %collective-permute-start = (bf16[128,640]{1,0:T(8,128)(2,1)}, bf16[128,640]{1,0:T(8,128)(2,1)S(1)}, u32[]{:S(2)}, u32[]{:S(2)}) collective-permute-start(bf16[128,640]{1,0:T(8,128)(2,1)} %get-tuple-element.16), channel_id=1, source_target_pairs={{0,1},{1,2},{2,3},{3,4},{4,5},{5,6},{6,7},{7,8},{8,9},{9,10},{10,1... | collective-permute-start | bytes 491528 | tf_op jit(solution)/shard_map/ppermute | solution.py:304
  7.3 10.4 %collective-permute-start.1 = (bf16[128,640]{1,0:T(8,128)(2,1)}, bf16[128,640]{1,0:T(8,128)(2,1)S(1)}, u32[]{:S(2)}, u32[]{:S(2)}) collective-permute-start(bf16[128,640]{1,0:T(8,128)(2,1)} %get-tuple-element.17), channel_id=1, source_target_pairs={{0,255},{1,0},{2,1},{3,2},{4,3},{5,4},{6,5},{7,6},{8,7},{9,8},{10,... | collective-permute-start | bytes 491528 | tf_op jit(solution)/shard_map/ppermute | solution.py:305
  11.0 18.2 %collective-permute-start.7 = (bf16[160,1024]{1,0:T(8,128)(2,1)S(1)}, bf16[160,1024]{1,0:T(8,128)(2,1)S(1)}, u32[]{:S(2)}, u32[]{:S(2)}) collective-permute-start(bf16[160,1024]{1,0:T(8,128)(2,1)S(1)} %bitcast.31), channel_id=1, source_target_pairs={{0,3},{1,0},{2,1},{3,2},{4,7},{5,4},{6,5},{7,6},{8,11},{9,8},{10,9... | collective-permute-start | bytes 983048 | tf_op jit(solution)/shard_map/ppermute | solution.py:311
  17.7 11.6 %collective-permute-start.6 = (bf16[160,1024]{1,0:T(8,128)(2,1)S(1)}, bf16[160,1024]{1,0:T(8,128)(2,1)S(1)}, u32[]{:S(2)}, u32[]{:S(2)}) collective-permute-start(bf16[160,1024]{1,0:T(8,128)(2,1)S(1)} %bitcast.32), channel_id=1, source_target_pairs={{0,1},{1,2},{2,3},{3,0},{4,5},{5,6},{6,7},{7,4},{8,9},{9,10},{10,1... | collective-permute-start | bytes 983048 | tf_op jit(solution)/shard_map/ppermute | solution.py:310
  19.9 11.9 %collective-permute-start.4 = (bf16[128,640]{1,0:T(8,128)(2,1)S(1)}, bf16[128,640]{1,0:T(8,128)(2,1)S(1)}, u32[]{:S(2)}, u32[]{:S(2)}) collective-permute-start(bf16[128,640]{1,0:T(8,128)(2,1)S(1)} %get-tuple-element.18), channel_id=1, source_target_pairs={{0,1},{1,2},{2,3},{3,4},{4,5},{5,6},{6,7},{7,8},{8,9},{9,10},{10,1... | collective-permute-start | bytes 491528 | tf_op jit(solution)/shard_map/ppermute | solution.py:304
  20.0 11.8 %copy-start.2 = (bf16[1,2,1024,256]{3,2,1,0:T(8,128)(2,1)S(1)}, bf16[1,2,1024,256]{3,2,1,0:T(8,128)(2,1)}, u32[]{:S(2)}) copy-start(bf16[1,2,1024,256]{3,2,1,0:T(8,128)(2,1)} %param.14) | copy-start | bytes 3145732
  20.0 11.8 %collective-permute-start.5 = (bf16[128,640]{1,0:T(8,128)(2,1)S(1)}, bf16[128,640]{1,0:T(8,128)(2,1)S(1)}, u32[]{:S(2)}, u32[]{:S(2)}) collective-permute-start(bf16[128,640]{1,0:T(8,128)(2,1)S(1)} %get-tuple-element.19), channel_id=1, source_target_pairs={{0,255},{1,0},{2,1},{3,2},{4,3},{5,4},{6,5},{7,6},{8,7},{9,8},{10,... | collective-permute-start | bytes 491528 | tf_op jit(solution)/shard_map/ppermute | solution.py:305
  34.7 18.9 %collective-permute-start.11 = (bf16[1024,256]{1,0:T(8,128)(2,1)S(1)}, bf16[1024,256]{1,0:T(8,128)(2,1)}, u32[]{:S(2)}, u32[]{:S(2)}) collective-permute-start(bf16[1024,256]{1,0:T(8,128)(2,1)S(1)} %get-tuple-element.23), channel_id=1, source_target_pairs={{0,1},{1,2},{2,3},{3,0},{4,5},{5,6},{6,7},{7,4},{8,9},{9,10},{10,1... | collective-permute-start | bytes 1572872 | tf_op jit(solution)/shard_map/ppermute | solution.py:310
  34.7 25.2 %collective-permute-start.8 = (bf16[640,256]{1,0:T(8,128)(2,1)}, bf16[640,256]{1,0:T(8,128)(2,1)}, u32[]{:S(2)}, u32[]{:S(2)}) collective-permute-start(bf16[640,256]{1,0:T(8,128)(2,1)} %collective-permute-done.2.refs_0_.refs_3_), channel_id=1, source_target_pairs={{0,1},{1,2},{2,3},{3,0},{4,5},{5,6},{6,7},{7,4},{8,9},{9,10},{10,1... | collective-permute-start | bytes 983048 | tf_op jit(solution)/shard_map/ppermute | solution.py:316
  34.8 39.2 %collective-permute-start.9 = (bf16[1024,256]{1,0:T(8,128)(2,1)S(1)}, bf16[1024,256]{1,0:T(8,128)(2,1)S(1)}, u32[]{:S(2)}, u32[]{:S(2)}) collective-permute-start(bf16[1024,256]{1,0:T(8,128)(2,1)S(1)} %get-tuple-element.23), channel_id=1, source_target_pairs={{0,3},{1,0},{2,1},{3,2},{4,7},{5,4},{6,5},{7,6},{8,11},{9,8},{10,9... | collective-permute-start | bytes 1572872 | tf_op jit(solution)/shard_map/ppermute | solution.py:311
  37.5 36.5 %collective-permute-start.14 = (bf16[1024,256]{1,0:T(8,128)(2,1)S(1)}, bf16[1024,256]{1,0:T(8,128)(2,1)}, u32[]{:S(2)}, u32[]{:S(2)}) collective-permute-start(bf16[1024,256]{1,0:T(8,128)(2,1)S(1)} %get-tuple-element.24), channel_id=1, source_target_pairs={{0,1},{1,2},{2,3},{3,0},{4,5},{5,6},{6,7},{7,4},{8,9},{9,10},{10,1... | collective-permute-start | bytes 1572872 | tf_op jit(solution)/shard_map/ppermute | solution.py:310
  37.5 18.9 %collective-permute-start.10 = (bf16[1024,256]{1,0:T(8,128)(2,1)S(1)}, bf16[1024,256]{1,0:T(8,128)(2,1)}, u32[]{:S(2)}, u32[]{:S(2)}) collective-permute-start(bf16[1024,256]{1,0:T(8,128)(2,1)S(1)} %get-tuple-element.24), channel_id=1, source_target_pairs={{0,3},{1,0},{2,1},{3,2},{4,7},{5,4},{6,5},{7,6},{8,11},{9,8},{10,9... | collective-permute-start | bytes 1572872 | tf_op jit(solution)/shard_map/ppermute | solution.py:311
  40.2 46.9 %all-to-all-start = ((bf16[64,16,640]{2,1,0:T(8,128)(2,1)}), bf16[64,16,640]{2,1,0:T(8,128)(2,1)}, u32[]{:S(2)}, u32[]{:S(2)}) async-start(bf16[64,16,640]{2,1,0:T(8,128)(2,1)} %bitcast.9), calls=%async_computation | async-start | bytes 2621440 | tf_op jit(solution)/shard_map/all_to_all | solution.py:386
  53.6 22.1 %collective-permute-start.12 = (bf16[1024,256]{1,0:T(8,128)(2,1)}, bf16[1024,256]{1,0:T(8,128)(2,1)}, u32[]{:S(2)}, u32[]{:S(2)}) collective-permute-start(bf16[1024,256]{1,0:T(8,128)(2,1)} %shard_map.87.refs_9_), channel_id=1, source_target_pairs={{0,1},{1,2},{2,3},{3,0},{4,5},{5,6},{6,7},{7,4},{8,9},{9,10},{10,1... | collective-permute-start | bytes 1572872 | tf_op jit(solution)/shard_map/ppermute | solution.py:316
  56.5 19.3 %collective-permute-start.13 = (bf16[1024,256]{1,0:T(8,128)(2,1)}, bf16[1024,256]{1,0:T(8,128)(2,1)}, u32[]{:S(2)}, u32[]{:S(2)}) collective-permute-start(bf16[1024,256]{1,0:T(8,128)(2,1)} %collective-permute-done.10.refs_6_), channel_id=1, source_target_pairs={{0,3},{1,0},{2,1},{3,2},{4,7},{5,4},{6,5},{7,6},{8,11},{9,8},{10,9... | collective-permute-start | bytes 1572872 | tf_op jit(solution)/shard_map/ppermute | solution.py:316
  60.0 14.0 %collective-permute-start.15 = (bf16[160,1024]{1,0:T(8,128)(2,1)S(1)}, bf16[160,1024]{1,0:T(8,128)(2,1)}, u32[]{:S(2)}, u32[]{:S(2)}) collective-permute-start(bf16[160,1024]{1,0:T(8,128)(2,1)S(1)} %copy-done.5), channel_id=1, source_target_pairs={{0,3},{1,0},{2,1},{3,2},{4,7},{5,4},{6,5},{7,6},{8,11},{9,8},{10,9... | collective-permute-start | bytes 983048 | tf_op jit(solution)/shard_map/ppermute | solution.py:316
  74.0 13.1 %copy-start.10 = (bf16[1024,256]{1,0:T(8,128)(2,1)}, bf16[1024,256]{1,0:T(8,128)(2,1)S(1)}, u32[]{:S(2)}) copy-start(bf16[1024,256]{1,0:T(8,128)(2,1)S(1)} %collective-permute-done.9.refs_5_) | copy-start | bytes 1572868
  (5 other events, 27.1 us)

commit v5 on v4

--- a/solution.py
+++ b/solution.py
@@ -217,7 +217,7 @@
     out_ref[...] = state_ref[...] + mul(pick, back_ref[...])
 
 
-def pass_kernel(in_ref, out_ref):
+def pass_kernel(*refs):
     pass
 
 
@@ -378,11 +378,11 @@
         flops=3 * 10**9,
     )
     hidden_below, hidden_above = from_sides(*layer)
-    (low,) = call(
-        pass_kernel, [layer[0]], hidden_below[0],
-        specs=[anywhere], outs=[anywhere], aliases={0: 0}, limit=58 * 1024 * 1024, flops=60 * 10**9,
-    )
-    far = from_far(low, hidden_above[1])
+    low_below, low_above = call(
+        pass_kernel, [layer[0]] * 2, hidden_below[0], hidden_above[0],
+        specs=[anywhere] * 2, outs=[anywhere] * 2, aliases={0: 0, 1: 1}, limit=58 * 1024 * 1024, flops=22 * 10**9,
+    )
+    far = from_far(low_below, hidden_above[1])
     incoming = lax.all_to_all(
         outgoing.reshape(groups, capacity, width), "elem", split_axis=0, concat_axis=0, tiled=True
     )
@@ -392,7 +392,7 @@
     (result,) = call(
         functools.partial(network_kernel, tile),
         [shape((slots, width), BF16)],
-        sec, incoming.reshape(slots, width), *first, hidden_proj[0], *hidden_above, *far, low, hidden_below[1], *last,
+        sec, incoming.reshape(slots, width), *first, hidden_proj[0], low_above, hidden_above[1], *far, low_below, hidden_below[1], *last,
         scratch=[
             pltpu.VMEM((4, *input_proj.shape[1:2], hid // 4), BF16),
             pltpu.VMEM((4, *hidden_proj.shape[1:3], hid // 4), BF16),

time: 144 us -> 143 us (level)
    ppermute x2, waiting for transfers between devices: 13.7 us -> 0.01 us  [from_far(): lax.ppermute(above, 'sec', ring(4, -1))]
    ppermute x2, waiting for transfers between devices: 1.74 us -> 15.4 us  [from_far(): lax.ppermute(below, 'sec', ring(4, 1))]
    ppermute x4, starting transfers between devices: 9.3 us -> 6.69 us  [from_sides(): above = [lax.ppermute(x, 'sec', ring(4, -1)) for x in shards]]
  transfers between devices with their start and end apart: 17 -> 17, of which waited for: 6 -> 5; matrix products, arithmetic and copies ran while one was open for 0% -> 0% of each run, Pallas kernels for 8% -> 8%
where the time goes in v5:
time: 143 us; the launch traced here: 142 us
  blocking collectives  41.4 us (29%)
  starting transfers between devices  36.4 us (25%)
  waiting for transfers between devices  35.3 us (25%)
  Pallas kernels  28.4 us (20%)
    all_to_all x1, blocking collectives, on_device(): lax.all_to_all(result.reshape(groups, capacity, width), 'elem', split_axi...  41.4 us
    pallas_call x8, Pallas kernels, call(): pl.pallas_call(kernel, out_shape=[jax.ShapeDtypeStruct(o.shape, o.dtype)...  28.4 us
    ppermute x2, waiting for transfers between devices, from_far(): lax.ppermute(below, 'sec', ring(4, 1))  15.4 us
    all_to_all x1, starting transfers between devices, on_device(): lax.all_to_all(outgoing.reshape(groups, capacity, width), 'elem', split_a...  13.4 us
    ppermute x2, starting transfers between devices, exchange(): above = lax.ppermute(south, DEVICE_AXES, ring(total, -1))  10.3 us
    all_to_all x1, waiting for transfers between devices, on_device(): lax.all_to_all(outgoing.reshape(groups, capacity, width), 'elem', split_a...  10 us
    ppermute x4, starting transfers between devices, from_sides(): above = [lax.ppermute(x, 'sec', ring(4, -1)) for x in shards]  6.69 us
    ppermute x2, waiting for transfers between devices, exchange(): below = lax.ppermute(north, DEVICE_AXES, ring(total, 1))  6.08 us
  transfers between devices with their start and end apart: 17, of which 5 were waited for; matrix products, arithmetic and copies ran while one was open for 0% of the time, Pallas kernels for 8%

profile of v5, /device:TPU:1, one launch (start us, length us, event | category | flops | bytes accessed | tf_op | source)
XLA Modules:
  0.0 141.9 jit_solution(16098751812011025310)
XLA Ops:
  0.0 3.3 %collective-permute-start.3 = (bf16[640,256]{1,0:T(8,128)(2,1)}, bf16[640,256]{1,0:T(8,128)(2,1)S(1)}, u32[]{:S(2)}, u32[]{:S(2)}) collective-permute-start(bf16[640,256]{1,0:T(8,128)(2,1)} %bitcast.27), channel_id=1, source_target_pairs={{0,3},{1,0},{2,1},{3,2},{4,7},{5,4},{6,5},{7,6},{8,11},{9,8},{10,9... | collective-permute-start | bytes 983048 | tf_op jit(solution)/shard_map/ppermute | solution.py:311
  3.4 3.7 %shard_map.83 = (bf16[128,640]{1,0:T(8,128)(2,1)}, bf16[128,640]{1,0:T(8,128)(2,1)}) custom-call(f32[512,640]{1,0:T(8,128)} %bitcast.17, s32[4,32]{1,0:T(4,128)} %bitcast.21, f32[16,16]{1,0:T(8,128)} %op_ref.7, f32[640]{0:T(1024)} %rates_ref.7), custom_call_target="tpu_custom_call" | custom-call | flops 2000000000 | bytes 1642496 | tf_op jit(solution)/shard_map/pallas_call | solution.py:286
  7.1 0.3 collective-permute-start
  7.3 3.7 %collective-permute-start.1 = (bf16[128,640]{1,0:T(8,128)(2,1)}, bf16[128,640]{1,0:T(8,128)(2,1)S(1)}, u32[]{:S(2)}, u32[]{:S(2)}) collective-permute-start(bf16[128,640]{1,0:T(8,128)(2,1)} %get-tuple-element.19), channel_id=1, source_target_pairs={{0,255},{1,0},{2,1},{3,2},{4,3},{5,4},{6,5},{7,6},{8,7},{9,8},{10,... | collective-permute-start | bytes 491528 | tf_op jit(solution)/shard_map/ppermute | solution.py:305
  11.0 0.7 collective-permute-start.7
  11.7 2.4 %shard_map.82 = (f32[512,640]{1,0:T(8,128)S(1)}, bf16[1024,512]{1,0:T(8,128)(2,1)S(1)}) custom-call(f32[512,640]{1,0:T(8,128)S(1)} %bitcast.18, s32[4,32]{1,0:T(4,128)S(1)} %bitcast.22, f32[16,16]{1,0:T(8,128)S(1)} %copy-done.9, f32[640]{0:T(1024)S(1)} %copy-done.10, s32[1,512]{1,0:T(1,128)S(1)} %bitcast.15), custom_call_target="tpu_custom_call" | custom-call | flops 3000000000 | bytes 3676160 | tf_op jit(solution)/shard_map/pallas_call | solution.py:286
  14.1 3.6 %collective-permute-done.below_ref = bf16[128,640]{1,0:T(8,128)(2,1)S(1)} collective-permute-done((bf16[128,640]{1,0:T(8,128)(2,1)}, bf16[128,640]{1,0:T(8,128)(2,1)S(1)}, u32[]{:S(2)}, u32[]{:S(2)}) %collective-permute-start) | collective-permute-done | bytes 163872 | tf_op jit(solution)/shard_map/ppermute | solution.py:304
  17.7 2.2 %shard_map.85 = (bf16[128,640]{1,0:T(8,128)(2,1)S(1)}, bf16[128,640]{1,0:T(8,128)(2,1)S(1)}) custom-call(f32[512,640]{1,0:T(8,128)S(1)} %get-tuple-element.17.prev_ref, bf16[128,640]{1,0:T(8,128)(2,1)S(1)} %collective-permute-done.below_ref, bf16[128,640]{1,0:T(8,128)(2,1)S(1)} %collective-permute-done.1.above_ref, s32[4,32]{1,0:T(4,128)S(1)} %bitcast.23, ...), custom_call_target="tpu_custom_call" | custom-call | flops 2000000000 | bytes 1970176 | tf_op jit(solution)/shard_map/pallas_call | solution.py:286
  19.9 0.1 collective-permute-start.4
  20.1 6.6 %collective-permute-start.5 = (bf16[128,640]{1,0:T(8,128)(2,1)S(1)}, bf16[128,640]{1,0:T(8,128)(2,1)S(1)}, u32[]{:S(2)}, u32[]{:S(2)}) collective-permute-start(bf16[128,640]{1,0:T(8,128)(2,1)S(1)} %get-tuple-element.21), channel_id=1, source_target_pairs={{0,255},{1,0},{2,1},{3,2},{4,3},{5,4},{6,5},{7,6},{8,7},{9,8},{10,... | collective-permute-start | bytes 491528 | tf_op jit(solution)/shard_map/ppermute | solution.py:305
  26.6 2.6 %shard_map.84.prev_ref = f32[512,640]{1,0:T(8,128)S(1)} custom-call(f32[512,640]{1,0:T(8,128)S(1)} %get-tuple-element.17.prev_ref, bf16[128,640]{1,0:T(8,128)(2,1)S(1)} %collective-permute-done.below_ref, bf16[128,640]{1,0:T(8,128)(2,1)S(1)} %collective-permute-done.1.above_ref, s32[4,32]{1,0:T(4,128)S(1)} %bitcast.24, f32[16,16]{1,0:T(8,128)S(1)} %copy-done.9, ...), custom_call_target="tpu_custom_call" | custom-call | flops 3000000000 | bytes 2953216 | tf_op jit(solution)/shard_map/pallas_call | solution.py:286
  29.3 2.5 %collective-permute-done.4.below_ref = bf16[128,640]{1,0:T(8,128)(2,1)S(1)} collective-permute-done((bf16[128,640]{1,0:T(8,128)(2,1)S(1)}, bf16[128,640]{1,0:T(8,128)(2,1)S(1)}, u32[]{:S(2)}, u32[]{:S(2)}) %collective-permute-start.4) | collective-permute-done | bytes 163872 | tf_op jit(solution)/shard_map/ppermute | solution.py:304
  31.8 2.8 %shard_map.86 = (f32[512,640]{1,0:T(8,128)S(1)}, bf16[1024,640]{1,0:T(8,128)(2,1)}, bf16[1024,256]{1,0:T(8,128)(2,1)S(1)}, bf16[1024,256]{1,0:T(8,128)(2,1)S(1)}) custom-call(f32[512,640]{1,0:T(8,128)S(1)} %shard_map.84.prev_ref, bf16[128,640]{1,0:T(8,128)(2,1)S(1)} %collective-permute-done.4.below_ref, ...), custom_call_target="tpu_custom_call" | custom-call | flops 3000000000 | bytes 7406080 | tf_op jit(solution)/shard_map/pallas_call | solution.py:286
  34.7 1.5 %collective-permute-start.9 = (bf16[1024,256]{1,0:T(8,128)(2,1)S(1)}, bf16[1024,256]{1,0:T(8,128)(2,1)}, u32[]{:S(2)}, u32[]{:S(2)}) collective-permute-start(bf16[1024,256]{1,0:T(8,128)(2,1)S(1)} %get-tuple-element.25), channel_id=1, source_target_pairs={{0,1},{1,2},{2,3},{3,0},{4,5},{5,6},{6,7},{7,4},{8,9},{9,10},{10,1... | collective-permute-start | bytes 1572872 | tf_op jit(solution)/shard_map/ppermute | solution.py:310
  36.2 2.6 %collective-permute-start.11 = (bf16[1024,256]{1,0:T(8,128)(2,1)S(1)}, bf16[1024,256]{1,0:T(8,128)(2,1)}, u32[]{:S(2)}, u32[]{:S(2)}) collective-permute-start(bf16[1024,256]{1,0:T(8,128)(2,1)S(1)} %get-tuple-element.27), channel_id=1, source_target_pairs={{0,3},{1,0},{2,1},{3,2},{4,7},{5,4},{6,5},{7,6},{8,11},{9,8},{10,9... | collective-permute-start | bytes 1572872 | tf_op jit(solution)/shard_map/ppermute | solution.py:311
  38.9 13.4 %all-to-all-start = ((bf16[64,16,640]{2,1,0:T(8,128)(2,1)}), bf16[64,16,640]{2,1,0:T(8,128)(2,1)}, u32[]{:S(2)}, u32[]{:S(2)}) async-start(bf16[64,16,640]{2,1,0:T(8,128)(2,1)} %bitcast.9), calls=%async_computation | async-start | bytes 2621440 | tf_op jit(solution)/shard_map/all_to_all | solution.py:386
  52.4 3.8 %collective-permute-done.11.refs_6_ = bf16[1024,256]{1,0:T(8,128)(2,1)} collective-permute-done((bf16[1024,256]{1,0:T(8,128)(2,1)S(1)}, bf16[1024,256]{1,0:T(8,128)(2,1)}, u32[]{:S(2)}, u32[]{:S(2)}) %collective-permute-start.11) | collective-permute-done | bytes 524320 | tf_op jit(solution)/shard_map/ppermute | solution.py:311
  56.2 1.5 %collective-permute-start.13 = (bf16[1024,256]{1,0:T(8,128)(2,1)}, bf16[1024,256]{1,0:T(8,128)(2,1)}, u32[]{:S(2)}, u32[]{:S(2)}) collective-permute-start(bf16[1024,256]{1,0:T(8,128)(2,1)} %collective-permute-done.11.refs_6_), channel_id=1, source_target_pairs={{0,3},{1,0},{2,1},{3,2},{4,7},{5,4},{6,5},{7,6},{8,11},{9,8},{10,9... | collective-permute-start | bytes 1572872 | tf_op jit(solution)/shard_map/ppermute | solution.py:316
  57.7 2.7 %collective-permute-start.15 = (bf16[160,1024]{1,0:T(8,128)(2,1)S(1)}, bf16[160,1024]{1,0:T(8,128)(2,1)}, u32[]{:S(2)}, u32[]{:S(2)}) collective-permute-start(bf16[160,1024]{1,0:T(8,128)(2,1)S(1)} %copy-done.7), channel_id=1, source_target_pairs={{0,3},{1,0},{2,1},{3,2},{4,7},{5,4},{6,5},{7,6},{8,11},{9,8},{10,9... | collective-permute-start | bytes 983048 | tf_op jit(solution)/shard_map/ppermute | solution.py:316
  60.4 15.4 %collective-permute-done.8.refs_2_ = bf16[640,256]{1,0:T(8,128)(2,1)S(1)} collective-permute-done((bf16[640,256]{1,0:T(8,128)(2,1)S(1)}, bf16[640,256]{1,0:T(8,128)(2,1)S(1)}, u32[]{:S(2)}, u32[]{:S(2)}) %collective-permute-start.8) | collective-permute-done | bytes 327712 | tf_op jit(solution)/shard_map/ppermute | solution.py:316
  75.8 10.0 %all-to-all-done = bf16[64,16,640]{2,1,0:T(8,128)(2,1)} async-done(((bf16[64,16,640]{2,1,0:T(8,128)(2,1)}), bf16[64,16,640]{2,1,0:T(8,128)(2,1)}, u32[]{:S(2)}, u32[]{:S(2)}) %all-to-all-start) | async-done | bytes 1310752 | tf_op jit(solution)/shard_map/all_to_all | solution.py:386
  85.8 11.9 %shard_map.88 = bf16[1024,640]{1,0:T(8,128)(2,1)} custom-call(s32[1]{0:T(128)} %bitcast.8.sec_ref, bf16[1024,640]{1,0:T(8,128)(2,1)} %bitcast.10.rows_ref, bf16[640,256]{1,0:T(8,128)(2,1)} %bitcast.29, bf16[640,256]{1,0:T(8,128)(2,1)} %copy-done.3, bf16[640,256]{1,0:T(8,128)(2,1)} %copy-done.14, bf16[640,256]{1,0:T(8,128)(2,1)} %copy-done.4, ...), custom_call_target="tpu_custom_call" | custom-call | flops 7000000000 | bytes 9437188 | tf_op jit(solution)/shard_map/pallas_call | solution.py:286
  97.8 41.4 %all_to_all.10 = bf16[64,16,640]{2,1,0:T(8,128)(2,1)S(1)} all-to-all(bf16[64,16,640]{2,1,0:T(8,128)(2,1)} %bitcast.26), channel_id=1, replica_groups=mesh['elem'=64,'sec'=4] {'elem'}, dimensions={0} | all-to-all | bytes 2621440 | tf_op jit(solution)/shard_map/all_to_all | solution.py:413
  139.1 2.8 %shard_map.89 = f32[512,640]{1,0:T(8,128)} custom-call(f32[512,640]{1,0:T(8,128)S(1)} %get-tuple-element.23.state_ref, bf16[1024,640]{1,0:T(8,128)(2,1)S(1)} %bitcast.14, s32[1,512]{1,0:T(1,128)S(1)} %bitcast.16), custom_call_target="tpu_custom_call" | custom-call | flops 1000000000 | bytes 3934208 | tf_op jit(solution)/shard_map/pallas_call | solution.py:286
  (49 shorter events, 0.3 us)
Async XLA Ops:
  0.0 17.7 %collective-permute-start.3 = (bf16[640,256]{1,0:T(8,128)(2,1)}, bf16[640,256]{1,0:T(8,128)(2,1)S(1)}, u32[]{:S(2)}, u32[]{:S(2)}) collective-permute-start(bf16[640,256]{1,0:T(8,128)(2,1)} %bitcast.27), channel_id=1, source_target_pairs={{0,3},{1,0},{2,1},{3,2},{4,7},{5,4},{6,5},{7,6},{8,11},{9,8},{10,9... | collective-permute-start | bytes 983048 | tf_op jit(solution)/shard_map/ppermute | solution.py:311
  3.3 14.4 %collective-permute-start.2 = (bf16[640,256]{1,0:T(8,128)(2,1)}, bf16[640,256]{1,0:T(8,128)(2,1)S(1)}, u32[]{:S(2)}, u32[]{:S(2)}) collective-permute-start(bf16[640,256]{1,0:T(8,128)(2,1)} %bitcast.28), channel_id=1, source_target_pairs={{0,1},{1,2},{2,3},{3,0},{4,5},{5,6},{6,7},{7,4},{8,9},{9,10},{10,1... | collective-permute-start | bytes 983048 | tf_op jit(solution)/shard_map/ppermute | solution.py:310
  3.3 8.4 %copy-start = (s32[512,1]{0,1:T(1,128)S(1)}, s32[512,1]{0,1:T(1,128)}, u32[]{:S(2)}) copy-start(s32[512,1]{0,1:T(1,128)} %param.12) | copy-start | bytes 6148
  3.3 8.4 %copy-start.1 = (f32[32,16,640]{2,1,0:T(8,128)S(1)}, f32[32,16,640]{2,1,0:T(8,128)}, u32[]{:S(2)}) copy-start(f32[32,16,640]{2,1,0:T(8,128)} %param.8) | copy-start | bytes 3932164
  3.3 8.4 %copy-start.9 = (f32[16,16]{1,0:T(8,128)S(1)}, f32[16,16]{1,0:T(8,128)}, u32[]{:S(2)}) copy-start(f32[16,16]{1,0:T(8,128)} %op_ref.7) | copy-start | bytes 3076
  3.3 8.4 %copy-start.10 = (f32[640]{0:T(1024)S(1)}, f32[640]{0:T(1024)}, u32[]{:S(2)}) copy-start(f32[640]{0:T(1024)} %rates_ref.7) | copy-start | bytes 7684
  7.1 10.6 %collective-permute-start = (bf16[128,640]{1,0:T(8,128)(2,1)}, bf16[128,640]{1,0:T(8,128)(2,1)S(1)}, u32[]{:S(2)}, u32[]{:S(2)}) collective-permute-start(bf16[128,640]{1,0:T(8,128)(2,1)} %get-tuple-element.18), channel_id=1, source_target_pairs={{0,1},{1,2},{2,3},{3,4},{4,5},{5,6},{6,7},{7,8},{8,9},{9,10},{10,1... | collective-permute-start | bytes 491528 | tf_op jit(solution)/shard_map/ppermute | solution.py:304
  7.3 10.4 %collective-permute-start.1 = (bf16[128,640]{1,0:T(8,128)(2,1)}, bf16[128,640]{1,0:T(8,128)(2,1)S(1)}, u32[]{:S(2)}, u32[]{:S(2)}) collective-permute-start(bf16[128,640]{1,0:T(8,128)(2,1)} %get-tuple-element.19), channel_id=1, source_target_pairs={{0,255},{1,0},{2,1},{3,2},{4,3},{5,4},{6,5},{7,6},{8,7},{9,8},{10,... | collective-permute-start | bytes 491528 | tf_op jit(solution)/shard_map/ppermute | solution.py:305
  11.0 18.3 %collective-permute-start.7 = (bf16[160,1024]{1,0:T(8,128)(2,1)S(1)}, bf16[160,1024]{1,0:T(8,128)(2,1)S(1)}, u32[]{:S(2)}, u32[]{:S(2)}) collective-permute-start(bf16[160,1024]{1,0:T(8,128)(2,1)S(1)} %bitcast.31), channel_id=1, source_target_pairs={{0,3},{1,0},{2,1},{3,2},{4,7},{5,4},{6,5},{7,6},{8,11},{9,8},{10,9... | collective-permute-start | bytes 983048 | tf_op jit(solution)/shard_map/ppermute | solution.py:311
  17.7 11.6 %collective-permute-start.6 = (bf16[160,1024]{1,0:T(8,128)(2,1)S(1)}, bf16[160,1024]{1,0:T(8,128)(2,1)S(1)}, u32[]{:S(2)}, u32[]{:S(2)}) collective-permute-start(bf16[160,1024]{1,0:T(8,128)(2,1)S(1)} %bitcast.32), channel_id=1, source_target_pairs={{0,1},{1,2},{2,3},{3,0},{4,5},{5,6},{6,7},{7,4},{8,9},{9,10},{10,1... | collective-permute-start | bytes 983048 | tf_op jit(solution)/shard_map/ppermute | solution.py:310
  19.9 11.9 %collective-permute-start.4 = (bf16[128,640]{1,0:T(8,128)(2,1)S(1)}, bf16[128,640]{1,0:T(8,128)(2,1)S(1)}, u32[]{:S(2)}, u32[]{:S(2)}) collective-permute-start(bf16[128,640]{1,0:T(8,128)(2,1)S(1)} %get-tuple-element.20), channel_id=1, source_target_pairs={{0,1},{1,2},{2,3},{3,4},{4,5},{5,6},{6,7},{7,8},{8,9},{9,10},{10,1... | collective-permute-start | bytes 491528 | tf_op jit(solution)/shard_map/ppermute | solution.py:304
  20.0 11.8 %copy-start.2 = (bf16[1,2,1024,256]{3,2,1,0:T(8,128)(2,1)S(1)}, bf16[1,2,1024,256]{3,2,1,0:T(8,128)(2,1)}, u32[]{:S(2)}) copy-start(bf16[1,2,1024,256]{3,2,1,0:T(8,128)(2,1)} %param.14) | copy-start | bytes 3145732
  20.1 11.8 %collective-permute-start.5 = (bf16[128,640]{1,0:T(8,128)(2,1)S(1)}, bf16[128,640]{1,0:T(8,128)(2,1)S(1)}, u32[]{:S(2)}, u32[]{:S(2)}) collective-permute-start(bf16[128,640]{1,0:T(8,128)(2,1)S(1)} %get-tuple-element.21), channel_id=1, source_target_pairs={{0,255},{1,0},{2,1},{3,2},{4,3},{5,4},{6,5},{7,6},{8,7},{9,8},{10,... | collective-permute-start | bytes 491528 | tf_op jit(solution)/shard_map/ppermute | solution.py:305
  34.7 17.6 %collective-permute-start.10 = (bf16[1024,256]{1,0:T(8,128)(2,1)S(1)}, bf16[1024,256]{1,0:T(8,128)(2,1)}, u32[]{:S(2)}, u32[]{:S(2)}) collective-permute-start(bf16[1024,256]{1,0:T(8,128)(2,1)S(1)} %get-tuple-element.25), channel_id=1, source_target_pairs={{0,3},{1,0},{2,1},{3,2},{4,7},{5,4},{6,5},{7,6},{8,11},{9,8},{10,9... | collective-permute-start | bytes 1572872 | tf_op jit(solution)/shard_map/ppermute | solution.py:311
  34.7 17.6 %collective-permute-start.9 = (bf16[1024,256]{1,0:T(8,128)(2,1)S(1)}, bf16[1024,256]{1,0:T(8,128)(2,1)}, u32[]{:S(2)}, u32[]{:S(2)}) collective-permute-start(bf16[1024,256]{1,0:T(8,128)(2,1)S(1)} %get-tuple-element.25), channel_id=1, source_target_pairs={{0,1},{1,2},{2,3},{3,0},{4,5},{5,6},{6,7},{7,4},{8,9},{9,10},{10,1... | collective-permute-start | bytes 1572872 | tf_op jit(solution)/shard_map/ppermute | solution.py:310
  36.2 39.6 %collective-permute-start.14 = (bf16[1024,256]{1,0:T(8,128)(2,1)S(1)}, bf16[1024,256]{1,0:T(8,128)(2,1)}, u32[]{:S(2)}, u32[]{:S(2)}) collective-permute-start(bf16[1024,256]{1,0:T(8,128)(2,1)S(1)} %get-tuple-element.27), channel_id=1, source_target_pairs={{0,1},{1,2},{2,3},{3,0},{4,5},{5,6},{6,7},{7,4},{8,9},{9,10},{10,1... | collective-permute-start | bytes 1572872 | tf_op jit(solution)/shard_map/ppermute | solution.py:310
  36.2 20.0 %collective-permute-start.11 = (bf16[1024,256]{1,0:T(8,128)(2,1)S(1)}, bf16[1024,256]{1,0:T(8,128)(2,1)}, u32[]{:S(2)}, u32[]{:S(2)}) collective-permute-start(bf16[1024,256]{1,0:T(8,128)(2,1)S(1)} %get-tuple-element.27), channel_id=1, source_target_pairs={{0,3},{1,0},{2,1},{3,2},{4,7},{5,4},{6,5},{7,6},{8,11},{9,8},{10,9... | collective-permute-start | bytes 1572872 | tf_op jit(solution)/shard_map/ppermute | solution.py:311
  38.9 46.9 %all-to-all-start = ((bf16[64,16,640]{2,1,0:T(8,128)(2,1)}), bf16[64,16,640]{2,1,0:T(8,128)(2,1)}, u32[]{:S(2)}, u32[]{:S(2)}) async-start(bf16[64,16,640]{2,1,0:T(8,128)(2,1)} %bitcast.9), calls=%async_computation | async-start | bytes 2621440 | tf_op jit(solution)/shard_map/all_to_all | solution.py:386
  52.3 23.5 %collective-permute-start.12 = (bf16[1024,256]{1,0:T(8,128)(2,1)}, bf16[1024,256]{1,0:T(8,128)(2,1)S(1)}, u32[]{:S(2)}, u32[]{:S(2)}) collective-permute-start(bf16[1024,256]{1,0:T(8,128)(2,1)} %get-tuple-element.28.refs_9_), channel_id=1, source_target_pairs={{0,1},{1,2},{2,3},{3,0},{4,5},{5,6},{6,7},{7,4},{8,9},{9,10},{10,1... | collective-permute-start | bytes 1572872 | tf_op jit(solution)/shard_map/ppermute | solution.py:316
  56.2 19.6 %collective-permute-start.13 = (bf16[1024,256]{1,0:T(8,128)(2,1)}, bf16[1024,256]{1,0:T(8,128)(2,1)}, u32[]{:S(2)}, u32[]{:S(2)}) collective-permute-start(bf16[1024,256]{1,0:T(8,128)(2,1)} %collective-permute-done.11.refs_6_), channel_id=1, source_target_pairs={{0,3},{1,0},{2,1},{3,2},{4,7},{5,4},{6,5},{7,6},{8,11},{9,8},{10,9... | collective-permute-start | bytes 1572872 | tf_op jit(solution)/shard_map/ppermute | solution.py:316
  57.7 18.1 %collective-permute-start.8 = (bf16[640,256]{1,0:T(8,128)(2,1)S(1)}, bf16[640,256]{1,0:T(8,128)(2,1)S(1)}, u32[]{:S(2)}, u32[]{:S(2)}) collective-permute-start(bf16[640,256]{1,0:T(8,128)(2,1)S(1)} %copy-done.5), channel_id=1, source_target_pairs={{0,1},{1,2},{2,3},{3,0},{4,5},{5,6},{6,7},{7,4},{8,9},{9,10},{10,1... | collective-permute-start | bytes 983048 | tf_op jit(solution)/shard_map/ppermute | solution.py:316
  57.7 18.1 %collective-permute-start.15 = (bf16[160,1024]{1,0:T(8,128)(2,1)S(1)}, bf16[160,1024]{1,0:T(8,128)(2,1)}, u32[]{:S(2)}, u32[]{:S(2)}) collective-permute-start(bf16[160,1024]{1,0:T(8,128)(2,1)S(1)} %copy-done.7), channel_id=1, source_target_pairs={{0,3},{1,0},{2,1},{3,2},{4,7},{5,4},{6,5},{7,6},{8,11},{9,8},{10,9... | collective-permute-start | bytes 983048 | tf_op jit(solution)/shard_map/ppermute | solution.py:316
  75.8 10.0 %copy-start.14 = (bf16[640,256]{1,0:T(8,128)(2,1)}, bf16[640,256]{1,0:T(8,128)(2,1)S(1)}, u32[]{:S(2)}) copy-start(bf16[640,256]{1,0:T(8,128)(2,1)S(1)} %collective-permute-done.8.refs_2_) | copy-start | bytes 983044
  75.8 10.0 %copy-start.12 = (bf16[1024,256]{1,0:T(8,128)(2,1)}, bf16[1024,256]{1,0:T(8,128)(2,1)S(1)}, u32[]{:S(2)}) copy-start(bf16[1024,256]{1,0:T(8,128)(2,1)S(1)} %collective-permute-done.12.refs_7_) | copy-start | bytes 1572868
  (8 other events, 42.1 us)

commit v6 on v5

--- a/solution.py
+++ b/solution.py
@@ -331,7 +331,7 @@
     mine = (input_proj[0], output_proj[0].T)
     below, above = from_sides(*mine)
     first, last = ([m, a, None, b] for m, a, b in zip(mine, above, below))
-    first[2], last[2] = from_far(below[0], above[1])
+    ends_far = from_far(below[0], above[1])
     anywhere = pl.BlockSpec(memory_space=pl.ANY)
     vmem = pl.BlockSpec(memory_space=pltpu.VMEM)
 
@@ -380,9 +380,13 @@
     hidden_below, hidden_above = from_sides(*layer)
     low_below, low_above = call(
         pass_kernel, [layer[0]] * 2, hidden_below[0], hidden_above[0],
-        specs=[anywhere] * 2, outs=[anywhere] * 2, aliases={0: 0, 1: 1}, limit=58 * 1024 * 1024, flops=22 * 10**9,
+        specs=[anywhere] * 2, outs=[anywhere] * 2, aliases={0: 0, 1: 1}, limit=58 * 1024 * 1024, flops=19 * 10**9,
     )
     far = from_far(low_below, hidden_above[1])
+    first[2], last[2] = call(
+        pass_kernel, ends_far, *ends_far,
+        specs=[anywhere] * 2, outs=[anywhere] * 2, aliases={0: 0, 1: 1}, limit=58 * 1024 * 1024, flops=10 * 10**9,
+    )
     incoming = lax.all_to_all(
         outgoing.reshape(groups, capacity, width), "elem", split_axis=0, concat_axis=0, tiled=True
     )

time: 143 us -> 142 us (level)
    ppermute x4, waiting for transfers between devices: 3.81 us -> 11.5 us  [from_sides(): above = [lax.ppermute(x, 'sec', ring(4, -1)) for x in shards]]
    ppermute x2, waiting for transfers between devices: 15.4 us -> 9.88 us  [from_far(): lax.ppermute(below, 'sec', ring(4, 1))]
    all_to_all x1, waiting for transfers between devices: 10 us -> 6.45 us  [on_device(): lax.all_to_all(outgoing.reshape(groups, capacity, width), 'elem', split_a...]
    pallas_call x8 -> x9, Pallas kernels: 28.4 us -> 28.6 us  [call(): pl.pallas_call(kernel, out_shape=[jax.ShapeDtypeStruct(o.shape, o.dtype)...]
  transfers between devices with their start and end apart: 17 -> 17, of which waited for: 5 -> 6; matrix products, arithmetic and copies ran while one was open for 0% -> 0% of each run, Pallas kernels for 8% -> 8%
where the time goes in v6:
time: 142 us; the launch traced here: 141 us
  blocking collectives  40.6 us (29%)
  starting transfers between devices  37.4 us (26%)
  waiting for transfers between devices  34.4 us (24%)
  Pallas kernels  28.6 us (20%)
    all_to_all x1, blocking collectives, on_device(): lax.all_to_all(result.reshape(groups, capacity, width), 'elem', split_axi...  40.6 us
    pallas_call x9, Pallas kernels, call(): pl.pallas_call(kernel, out_shape=[jax.ShapeDtypeStruct(o.shape, o.dtype)...  28.6 us
    all_to_all x1, starting transfers between devices, on_device(): lax.all_to_all(outgoing.reshape(groups, capacity, width), 'elem', split_a...  13.4 us
    ppermute x4, waiting for transfers between devices, from_sides(): above = [lax.ppermute(x, 'sec', ring(4, -1)) for x in shards]  11.5 us
    ppermute x2, starting transfers between devices, exchange(): above = lax.ppermute(south, DEVICE_AXES, ring(total, -1))  10.3 us
    ppermute x2, waiting for transfers between devices, from_far(): lax.ppermute(below, 'sec', ring(4, 1))  9.88 us
    ppermute x4, starting transfers between devices, from_sides(): above = [lax.ppermute(x, 'sec', ring(4, -1)) for x in shards]  6.71 us
    all_to_all x1, waiting for transfers between devices, on_device(): lax.all_to_all(outgoing.reshape(groups, capacity, width), 'elem', split_a...  6.45 us
  transfers between devices with their start and end apart: 17, of which 6 were waited for; matrix products, arithmetic and copies ran while one was open for 0% of the time, Pallas kernels for 8%

profile of v6, /device:TPU:1, one launch (start us, length us, event | category | flops | bytes accessed | tf_op | source)
XLA Modules:
  0.0 141.2 jit_solution(17186079501091344943)
XLA Ops:
  0.0 3.3 %collective-permute-start.3 = (bf16[640,256]{1,0:T(8,128)(2,1)}, bf16[640,256]{1,0:T(8,128)(2,1)S(1)}, u32[]{:S(2)}, u32[]{:S(2)}) collective-permute-start(bf16[640,256]{1,0:T(8,128)(2,1)} %bitcast.27), channel_id=1, source_target_pairs={{0,3},{1,0},{2,1},{3,2},{4,7},{5,4},{6,5},{7,6},{8,11},{9,8},{10,9... | collective-permute-start | bytes 983048 | tf_op jit(solution)/shard_map/ppermute | solution.py:311
  3.4 3.7 %shard_map.83 = (bf16[128,640]{1,0:T(8,128)(2,1)}, bf16[128,640]{1,0:T(8,128)(2,1)}) custom-call(f32[512,640]{1,0:T(8,128)} %bitcast.17, s32[4,32]{1,0:T(4,128)} %bitcast.21, f32[16,16]{1,0:T(8,128)} %op_ref.7, f32[640]{0:T(1024)} %rates_ref.7), custom_call_target="tpu_custom_call" | custom-call | flops 2000000000 | bytes 1642496 | tf_op jit(solution)/shard_map/pallas_call | solution.py:286
  7.1 0.3 collective-permute-start
  7.3 3.7 %collective-permute-start.1 = (bf16[128,640]{1,0:T(8,128)(2,1)}, bf16[128,640]{1,0:T(8,128)(2,1)S(1)}, u32[]{:S(2)}, u32[]{:S(2)}) collective-permute-start(bf16[128,640]{1,0:T(8,128)(2,1)} %get-tuple-element.21), channel_id=1, source_target_pairs={{0,255},{1,0},{2,1},{3,2},{4,3},{5,4},{6,5},{7,6},{8,7},{9,8},{10,... | collective-permute-start | bytes 491528 | tf_op jit(solution)/shard_map/ppermute | solution.py:305
  11.0 0.7 collective-permute-start.7
  11.7 2.4 %shard_map.82 = (f32[512,640]{1,0:T(8,128)S(1)}, bf16[1024,512]{1,0:T(8,128)(2,1)S(1)}) custom-call(f32[512,640]{1,0:T(8,128)S(1)} %bitcast.18, s32[4,32]{1,0:T(4,128)S(1)} %bitcast.22, f32[16,16]{1,0:T(8,128)S(1)} %copy-done.7, f32[640]{0:T(1024)S(1)} %copy-done.8, s32[1,512]{1,0:T(1,128)S(1)} %bitcast.15), custom_call_target="tpu_custom_call" | custom-call | flops 3000000000 | bytes 3676160 | tf_op jit(solution)/shard_map/pallas_call | solution.py:286
  14.2 3.5 %collective-permute-done.below_ref = bf16[128,640]{1,0:T(8,128)(2,1)S(1)} collective-permute-done((bf16[128,640]{1,0:T(8,128)(2,1)}, bf16[128,640]{1,0:T(8,128)(2,1)S(1)}, u32[]{:S(2)}, u32[]{:S(2)}) %collective-permute-start) | collective-permute-done | bytes 163872 | tf_op jit(solution)/shard_map/ppermute | solution.py:304
  17.7 2.2 %shard_map.85 = (bf16[128,640]{1,0:T(8,128)(2,1)S(1)}, bf16[128,640]{1,0:T(8,128)(2,1)S(1)}) custom-call(f32[512,640]{1,0:T(8,128)S(1)} %get-tuple-element.19.prev_ref, bf16[128,640]{1,0:T(8,128)(2,1)S(1)} %collective-permute-done.below_ref, bf16[128,640]{1,0:T(8,128)(2,1)S(1)} %collective-permute-done.1.above_ref, s32[4,32]{1,0:T(4,128)S(1)} %bitcast.23, ...), custom_call_target="tpu_custom_call" | custom-call | flops 2000000000 | bytes 1970176 | tf_op jit(solution)/shard_map/pallas_call | solution.py:286
  20.0 6.6 %collective-permute-start.5 = (bf16[128,640]{1,0:T(8,128)(2,1)S(1)}, bf16[128,640]{1,0:T(8,128)(2,1)S(1)}, u32[]{:S(2)}, u32[]{:S(2)}) collective-permute-start(bf16[128,640]{1,0:T(8,128)(2,1)S(1)} %get-tuple-element.23), channel_id=1, source_target_pairs={{0,255},{1,0},{2,1},{3,2},{4,3},{5,4},{6,5},{7,6},{8,7},{9,8},{10,... | collective-permute-start | bytes 491528 | tf_op jit(solution)/shard_map/ppermute | solution.py:305
  26.6 2.7 %shard_map.84.prev_ref = f32[512,640]{1,0:T(8,128)S(1)} custom-call(f32[512,640]{1,0:T(8,128)S(1)} %get-tuple-element.19.prev_ref, bf16[128,640]{1,0:T(8,128)(2,1)S(1)} %collective-permute-done.below_ref, bf16[128,640]{1,0:T(8,128)(2,1)S(1)} %collective-permute-done.1.above_ref, s32[4,32]{1,0:T(4,128)S(1)} %bitcast.24, f32[16,16]{1,0:T(8,128)S(1)} %copy-done.7, ...), custom_call_target="tpu_custom_call" | custom-call | flops 3000000000 | bytes 2953216 | tf_op jit(solution)/shard_map/pallas_call | solution.py:286
  29.3 2.5 %collective-permute-done.4.below_ref = bf16[128,640]{1,0:T(8,128)(2,1)S(1)} collective-permute-done((bf16[128,640]{1,0:T(8,128)(2,1)S(1)}, bf16[128,640]{1,0:T(8,128)(2,1)S(1)}, u32[]{:S(2)}, u32[]{:S(2)}) %collective-permute-start.4) | collective-permute-done | bytes 163872 | tf_op jit(solution)/shard_map/ppermute | solution.py:304
  31.8 2.8 %shard_map.86 = (f32[512,640]{1,0:T(8,128)S(1)}, bf16[1024,640]{1,0:T(8,128)(2,1)}, bf16[1024,256]{1,0:T(8,128)(2,1)S(1)}, bf16[1024,256]{1,0:T(8,128)(2,1)S(1)}) custom-call(f32[512,640]{1,0:T(8,128)S(1)} %shard_map.84.prev_ref, bf16[128,640]{1,0:T(8,128)(2,1)S(1)} %collective-permute-done.4.below_ref, ...), custom_call_target="tpu_custom_call" | custom-call | flops 3000000000 | bytes 7406080 | tf_op jit(solution)/shard_map/pallas_call | solution.py:286
  34.7 1.5 %collective-permute-start.10 = (bf16[1024,256]{1,0:T(8,128)(2,1)S(1)}, bf16[1024,256]{1,0:T(8,128)(2,1)}, u32[]{:S(2)}, u32[]{:S(2)}) collective-permute-start(bf16[1024,256]{1,0:T(8,128)(2,1)S(1)} %get-tuple-element.28), channel_id=1, source_target_pairs={{0,1},{1,2},{2,3},{3,0},{4,5},{5,6},{6,7},{7,4},{8,9},{9,10},{10,1... | collective-permute-start | bytes 1572872 | tf_op jit(solution)/shard_map/ppermute | solution.py:310
  36.2 2.6 %collective-permute-start.9 = (bf16[160,1024]{1,0:T(8,128)(2,1)S(1)}, bf16[160,1024]{1,0:T(8,128)(2,1)}, u32[]{:S(2)}, u32[]{:S(2)}) collective-permute-start(bf16[160,1024]{1,0:T(8,128)(2,1)S(1)} %collective-permute-done.7.refs_1_.refs_12_), channel_id=1, source_target_pairs={{0,3},{1,0},{2,1},{3,2},{4,7},{5,4},{6,5},{7,6},{8,11},{9,8},{10,9... | collective-permute-start | bytes 983048 | tf_op jit(solution)/shard_map/ppermute | solution.py:316
  38.9 13.4 %all-to-all-start = ((bf16[64,16,640]{2,1,0:T(8,128)(2,1)}), bf16[64,16,640]{2,1,0:T(8,128)(2,1)}, u32[]{:S(2)}, u32[]{:S(2)}) async-start(bf16[64,16,640]{2,1,0:T(8,128)(2,1)} %bitcast.9), calls=%async_computation | async-start | bytes 2621440 | tf_op jit(solution)/shard_map/all_to_all | solution.py:390
  52.4 2.7 %collective-permute-start.12 = (bf16[1024,256]{1,0:T(8,128)(2,1)S(1)}, bf16[1024,256]{1,0:T(8,128)(2,1)S(1)}, u32[]{:S(2)}, u32[]{:S(2)}) collective-permute-start(bf16[1024,256]{1,0:T(8,128)(2,1)S(1)} %get-tuple-element.30), channel_id=1, source_target_pairs={{0,3},{1,0},{2,1},{3,2},{4,7},{5,4},{6,5},{7,6},{8,11},{9,8},{10,9... | collective-permute-start | bytes 1572872 | tf_op jit(solution)/shard_map/ppermute | solution.py:311
  55.0 11.5 %collective-permute-done.12.refs_6_ = bf16[1024,256]{1,0:T(8,128)(2,1)S(1)} collective-permute-done((bf16[1024,256]{1,0:T(8,128)(2,1)S(1)}, bf16[1024,256]{1,0:T(8,128)(2,1)S(1)}, u32[]{:S(2)}, u32[]{:S(2)}) %collective-permute-start.12) | collective-permute-done | bytes 524320 | tf_op jit(solution)/shard_map/ppermute | solution.py:311
  66.6 2.4 %collective-permute-start.14 = (bf16[1024,256]{1,0:T(8,128)(2,1)S(1)}, bf16[1024,256]{1,0:T(8,128)(2,1)}, u32[]{:S(2)}, u32[]{:S(2)}) collective-permute-start(bf16[1024,256]{1,0:T(8,128)(2,1)S(1)} %collective-permute-done.12.refs_6_), channel_id=1, source_target_pairs={{0,3},{1,0},{2,1},{3,2},{4,7},{5,4},{6,5},{7,6},{8,11},{9,8},{10,9... | collective-permute-start | bytes 1572872 | tf_op jit(solution)/shard_map/ppermute | solution.py:316
  69.0 9.9 %collective-permute-done.13.refs_7_ = bf16[1024,256]{1,0:T(8,128)(2,1)S(1)} collective-permute-done((bf16[1024,256]{1,0:T(8,128)(2,1)}, bf16[1024,256]{1,0:T(8,128)(2,1)S(1)}, u32[]{:S(2)}, u32[]{:S(2)}) %collective-permute-start.13) | collective-permute-done | bytes 524320 | tf_op jit(solution)/shard_map/ppermute | solution.py:316
  78.9 0.5 collective-permute-done.14.refs_8_
  79.4 6.4 %all-to-all-done = bf16[64,16,640]{2,1,0:T(8,128)(2,1)} async-done(((bf16[64,16,640]{2,1,0:T(8,128)(2,1)}), bf16[64,16,640]{2,1,0:T(8,128)(2,1)}, u32[]{:S(2)}, u32[]{:S(2)}) %all-to-all-start) | async-done | bytes 1310752 | tf_op jit(solution)/shard_map/all_to_all | solution.py:390
  85.8 12.0 %shard_map.89 = bf16[1024,640]{1,0:T(8,128)(2,1)} custom-call(s32[1]{0:T(128)} %bitcast.8.sec_ref, bf16[1024,640]{1,0:T(8,128)(2,1)} %bitcast.10.rows_ref, bf16[640,256]{1,0:T(8,128)(2,1)} %bitcast.29, bf16[640,256]{1,0:T(8,128)(2,1)} %copy-done.3, bf16[640,256]{1,0:T(8,128)(2,1)} %get-tuple-element.27.refs_2_, bf16[640,256]{1,0:T(8,128)(2,1)} %copy-done.4, ...), custom_call_target="tpu_custom_call" | custom-call | flops 7000000000 | bytes 9437188 | tf_op jit(solution)/shard_map/pallas_call | solution.py:286
  97.8 40.6 %all_to_all.10 = bf16[64,16,640]{2,1,0:T(8,128)(2,1)S(1)} all-to-all(bf16[64,16,640]{2,1,0:T(8,128)(2,1)} %bitcast.26), channel_id=1, replica_groups=mesh['elem'=64,'sec'=4] {'elem'}, dimensions={0} | all-to-all | bytes 2621440 | tf_op jit(solution)/shard_map/all_to_all | solution.py:417
  138.4 2.8 %shard_map.90 = f32[512,640]{1,0:T(8,128)} custom-call(f32[512,640]{1,0:T(8,128)S(1)} %get-tuple-element.25.state_ref, bf16[1024,640]{1,0:T(8,128)(2,1)S(1)} %bitcast.14, s32[1,512]{1,0:T(1,128)S(1)} %bitcast.16), custom_call_target="tpu_custom_call" | custom-call | flops 1000000000 | bytes 3934208 | tf_op jit(solution)/shard_map/pallas_call | solution.py:286
  (48 shorter events, 0.4 us)
Async XLA Ops:
  0.0 17.7 %collective-permute-start.3 = (bf16[640,256]{1,0:T(8,128)(2,1)}, bf16[640,256]{1,0:T(8,128)(2,1)S(1)}, u32[]{:S(2)}, u32[]{:S(2)}) collective-permute-start(bf16[640,256]{1,0:T(8,128)(2,1)} %bitcast.27), channel_id=1, source_target_pairs={{0,3},{1,0},{2,1},{3,2},{4,7},{5,4},{6,5},{7,6},{8,11},{9,8},{10,9... | collective-permute-start | bytes 983048 | tf_op jit(solution)/shard_map/ppermute | solution.py:311
  3.3 14.4 %collective-permute-start.2 = (bf16[640,256]{1,0:T(8,128)(2,1)}, bf16[640,256]{1,0:T(8,128)(2,1)S(1)}, u32[]{:S(2)}, u32[]{:S(2)}) collective-permute-start(bf16[640,256]{1,0:T(8,128)(2,1)} %bitcast.28), channel_id=1, source_target_pairs={{0,1},{1,2},{2,3},{3,0},{4,5},{5,6},{6,7},{7,4},{8,9},{9,10},{10,1... | collective-permute-start | bytes 983048 | tf_op jit(solution)/shard_map/ppermute | solution.py:310
  3.3 8.4 %copy-start = (s32[512,1]{0,1:T(1,128)S(1)}, s32[512,1]{0,1:T(1,128)}, u32[]{:S(2)}) copy-start(s32[512,1]{0,1:T(1,128)} %param.12) | copy-start | bytes 6148
  3.3 8.4 %copy-start.1 = (f32[32,16,640]{2,1,0:T(8,128)S(1)}, f32[32,16,640]{2,1,0:T(8,128)}, u32[]{:S(2)}) copy-start(f32[32,16,640]{2,1,0:T(8,128)} %param.8) | copy-start | bytes 3932164
  3.3 8.4 %copy-start.7 = (f32[16,16]{1,0:T(8,128)S(1)}, f32[16,16]{1,0:T(8,128)}, u32[]{:S(2)}) copy-start(f32[16,16]{1,0:T(8,128)} %op_ref.7) | copy-start | bytes 3076
  3.3 8.4 %copy-start.8 = (f32[640]{0:T(1024)S(1)}, f32[640]{0:T(1024)}, u32[]{:S(2)}) copy-start(f32[640]{0:T(1024)} %rates_ref.7) | copy-start | bytes 7684
  7.1 10.6 %collective-permute-start = (bf16[128,640]{1,0:T(8,128)(2,1)}, bf16[128,640]{1,0:T(8,128)(2,1)S(1)}, u32[]{:S(2)}, u32[]{:S(2)}) collective-permute-start(bf16[128,640]{1,0:T(8,128)(2,1)} %get-tuple-element.20), channel_id=1, source_target_pairs={{0,1},{1,2},{2,3},{3,4},{4,5},{5,6},{6,7},{7,8},{8,9},{9,10},{10,1... | collective-permute-start | bytes 491528 | tf_op jit(solution)/shard_map/ppermute | solution.py:304
  7.3 10.4 %collective-permute-start.1 = (bf16[128,640]{1,0:T(8,128)(2,1)}, bf16[128,640]{1,0:T(8,128)(2,1)S(1)}, u32[]{:S(2)}, u32[]{:S(2)}) collective-permute-start(bf16[128,640]{1,0:T(8,128)(2,1)} %get-tuple-element.21), channel_id=1, source_target_pairs={{0,255},{1,0},{2,1},{3,2},{4,3},{5,4},{6,5},{7,6},{8,7},{9,8},{10,... | collective-permute-start | bytes 491528 | tf_op jit(solution)/shard_map/ppermute | solution.py:305
  11.0 18.3 %collective-permute-start.7 = (bf16[160,1024]{1,0:T(8,128)(2,1)S(1)}, bf16[160,1024]{1,0:T(8,128)(2,1)S(1)}, u32[]{:S(2)}, u32[]{:S(2)}) collective-permute-start(bf16[160,1024]{1,0:T(8,128)(2,1)S(1)} %bitcast.31), channel_id=1, source_target_pairs={{0,3},{1,0},{2,1},{3,2},{4,7},{5,4},{6,5},{7,6},{8,11},{9,8},{10,9... | collective-permute-start | bytes 983048 | tf_op jit(solution)/shard_map/ppermute | solution.py:311
  17.7 11.6 %collective-permute-start.6 = (bf16[160,1024]{1,0:T(8,128)(2,1)S(1)}, bf16[160,1024]{1,0:T(8,128)(2,1)S(1)}, u32[]{:S(2)}, u32[]{:S(2)}) collective-permute-start(bf16[160,1024]{1,0:T(8,128)(2,1)S(1)} %bitcast.32), channel_id=1, source_target_pairs={{0,1},{1,2},{2,3},{3,0},{4,5},{5,6},{6,7},{7,4},{8,9},{9,10},{10,1... | collective-permute-start | bytes 983048 | tf_op jit(solution)/shard_map/ppermute | solution.py:310
  17.7 18.5 %copy-start.4 = (bf16[640,256]{1,0:T(8,128)(2,1)}, bf16[640,256]{1,0:T(8,128)(2,1)S(1)}, u32[]{:S(2)}) copy-start(bf16[640,256]{1,0:T(8,128)(2,1)S(1)} %collective-permute-done.2.refs_0_.refs_3_) | copy-start | bytes 983044
  19.9 11.9 %collective-permute-start.4 = (bf16[128,640]{1,0:T(8,128)(2,1)S(1)}, bf16[128,640]{1,0:T(8,128)(2,1)S(1)}, u32[]{:S(2)}, u32[]{:S(2)}) collective-permute-start(bf16[128,640]{1,0:T(8,128)(2,1)S(1)} %get-tuple-element.22), channel_id=1, source_target_pairs={{0,1},{1,2},{2,3},{3,4},{4,5},{5,6},{6,7},{7,8},{8,9},{9,10},{10,1... | collective-permute-start | bytes 491528 | tf_op jit(solution)/shard_map/ppermute | solution.py:304
  20.0 11.8 %copy-start.2 = (bf16[1,2,1024,256]{3,2,1,0:T(8,128)(2,1)S(1)}, bf16[1,2,1024,256]{3,2,1,0:T(8,128)(2,1)}, u32[]{:S(2)}) copy-start(bf16[1,2,1024,256]{3,2,1,0:T(8,128)(2,1)} %param.14) | copy-start | bytes 3145732
  20.0 11.8 %collective-permute-start.5 = (bf16[128,640]{1,0:T(8,128)(2,1)S(1)}, bf16[128,640]{1,0:T(8,128)(2,1)S(1)}, u32[]{:S(2)}, u32[]{:S(2)}) collective-permute-start(bf16[128,640]{1,0:T(8,128)(2,1)S(1)} %get-tuple-element.23), channel_id=1, source_target_pairs={{0,255},{1,0},{2,1},{3,2},{4,3},{5,4},{6,5},{7,6},{8,7},{9,8},{10,... | collective-permute-start | bytes 491528 | tf_op jit(solution)/shard_map/ppermute | solution.py:305
  34.7 17.7 %collective-permute-start.11 = (bf16[1024,256]{1,0:T(8,128)(2,1)S(1)}, bf16[1024,256]{1,0:T(8,128)(2,1)}, u32[]{:S(2)}, u32[]{:S(2)}) collective-permute-start(bf16[1024,256]{1,0:T(8,128)(2,1)S(1)} %get-tuple-element.28), channel_id=1, source_target_pairs={{0,3},{1,0},{2,1},{3,2},{4,7},{5,4},{6,5},{7,6},{8,11},{9,8},{10,9... | collective-permute-start | bytes 1572872 | tf_op jit(solution)/shard_map/ppermute | solution.py:311
  34.7 20.3 %collective-permute-start.10 = (bf16[1024,256]{1,0:T(8,128)(2,1)S(1)}, bf16[1024,256]{1,0:T(8,128)(2,1)}, u32[]{:S(2)}, u32[]{:S(2)}) collective-permute-start(bf16[1024,256]{1,0:T(8,128)(2,1)S(1)} %get-tuple-element.28), channel_id=1, source_target_pairs={{0,1},{1,2},{2,3},{3,0},{4,5},{5,6},{6,7},{7,4},{8,9},{9,10},{10,1... | collective-permute-start | bytes 1572872 | tf_op jit(solution)/shard_map/ppermute | solution.py:310
  36.2 32.8 %collective-permute-start.8 = (bf16[640,256]{1,0:T(8,128)(2,1)S(1)}, bf16[640,256]{1,0:T(8,128)(2,1)}, u32[]{:S(2)}, u32[]{:S(2)}) collective-permute-start(bf16[640,256]{1,0:T(8,128)(2,1)S(1)} %collective-permute-done.2.refs_0_.refs_3_), channel_id=1, source_target_pairs={{0,1},{1,2},{2,3},{3,0},{4,5},{5,6},{6,7},{7,4},{8,9},{9,10},{10,1... | collective-permute-start | bytes 983048 | tf_op jit(solution)/shard_map/ppermute | solution.py:316
  36.2 32.8 %collective-permute-start.9 = (bf16[160,1024]{1,0:T(8,128)(2,1)S(1)}, bf16[160,1024]{1,0:T(8,128)(2,1)}, u32[]{:S(2)}, u32[]{:S(2)}) collective-permute-start(bf16[160,1024]{1,0:T(8,128)(2,1)S(1)} %collective-permute-done.7.refs_1_.refs_12_), channel_id=1, source_target_pairs={{0,3},{1,0},{2,1},{3,2},{4,7},{5,4},{6,5},{7,6},{8,11},{9,8},{10,9... | collective-permute-start | bytes 983048 | tf_op jit(solution)/shard_map/ppermute | solution.py:316
  38.9 46.9 %all-to-all-start = ((bf16[64,16,640]{2,1,0:T(8,128)(2,1)}), bf16[64,16,640]{2,1,0:T(8,128)(2,1)}, u32[]{:S(2)}, u32[]{:S(2)}) async-start(bf16[64,16,640]{2,1,0:T(8,128)(2,1)} %bitcast.9), calls=%async_computation | async-start | bytes 2621440 | tf_op jit(solution)/shard_map/all_to_all | solution.py:390
  52.3 16.7 %collective-permute-start.15 = (bf16[1024,256]{1,0:T(8,128)(2,1)S(1)}, bf16[1024,256]{1,0:T(8,128)(2,1)S(1)}, u32[]{:S(2)}, u32[]{:S(2)}) collective-permute-start(bf16[1024,256]{1,0:T(8,128)(2,1)S(1)} %get-tuple-element.30), channel_id=1, source_target_pairs={{0,1},{1,2},{2,3},{3,0},{4,5},{5,6},{6,7},{7,4},{8,9},{9,10},{10,1... | collective-permute-start | bytes 1572872 | tf_op jit(solution)/shard_map/ppermute | solution.py:310
  52.4 14.2 %collective-permute-start.12 = (bf16[1024,256]{1,0:T(8,128)(2,1)S(1)}, bf16[1024,256]{1,0:T(8,128)(2,1)S(1)}, u32[]{:S(2)}, u32[]{:S(2)}) collective-permute-start(bf16[1024,256]{1,0:T(8,128)(2,1)S(1)} %get-tuple-element.30), channel_id=1, source_target_pairs={{0,3},{1,0},{2,1},{3,2},{4,7},{5,4},{6,5},{7,6},{8,11},{9,8},{10,9... | collective-permute-start | bytes 1572872 | tf_op jit(solution)/shard_map/ppermute | solution.py:311
  55.0 23.9 %collective-permute-start.13 = (bf16[1024,256]{1,0:T(8,128)(2,1)}, bf16[1024,256]{1,0:T(8,128)(2,1)S(1)}, u32[]{:S(2)}, u32[]{:S(2)}) collective-permute-start(bf16[1024,256]{1,0:T(8,128)(2,1)} %get-tuple-element.31.refs_9_), channel_id=1, source_target_pairs={{0,1},{1,2},{2,3},{3,0},{4,5},{5,6},{6,7},{7,4},{8,9},{9,10},{10,1... | collective-permute-start | bytes 1572872 | tf_op jit(solution)/shard_map/ppermute | solution.py:316
  66.6 12.8 %collective-permute-start.14 = (bf16[1024,256]{1,0:T(8,128)(2,1)S(1)}, bf16[1024,256]{1,0:T(8,128)(2,1)}, u32[]{:S(2)}, u32[]{:S(2)}) collective-permute-start(bf16[1024,256]{1,0:T(8,128)(2,1)S(1)} %collective-permute-done.12.refs_6_), channel_id=1, source_target_pairs={{0,3},{1,0},{2,1},{3,2},{4,7},{5,4},{6,5},{7,6},{8,11},{9,8},{10,9... | collective-permute-start | bytes 1572872 | tf_op jit(solution)/shard_map/ppermute | solution.py:316
  69.0 16.8 %copy-start.10 = (bf16[1024,256]{1,0:T(8,128)(2,1)}, bf16[1024,256]{1,0:T(8,128)(2,1)S(1)}, u32[]{:S(2)}) copy-start(bf16[1024,256]{1,0:T(8,128)(2,1)S(1)} %collective-permute-done.15.refs_10_) | copy-start | bytes 1572868
  (7 other events, 39.9 us)

commit v7 on v6

--- a/solution.py
+++ b/solution.py
@@ -120,8 +120,7 @@
     other = jnp.where(west, near[:, 0:1], near[:, 1:2])
     there = ((other >> 4) << 7) + (side << 6) + ((other & (POINTS - 1)) << 2) + jnp.where(west, SIDE - 1, 0)
     pick = ones_where(iota((total, total), 1) == jnp.where(west | east, there, -1))
-    high, low = halves(first)
-    far = mul(pick, high) + mul(pick, low)
+    far = mul(pick, first.astype(BF16))
     second = jnp.where(west | east, 0.5 * (first + far), first).astype(BF16)
     quarter = half // 2
     north = [second[i : i + quarter] for i in range(0, total, half)]

time: 142 us -> 142 us (level)
  no operation moved by 1% of the time
where the time goes in v7:
time: 142 us; the launch traced here: 141 us
  blocking collectives  40.6 us (29%)
  starting transfers between devices  37.2 us (26%)
  waiting for transfers between devices  34.6 us (24%)
  Pallas kernels  28.4 us (20%)
    all_to_all x1, blocking collectives, on_device(): lax.all_to_all(result.reshape(groups, capacity, width), 'elem', split_axi...  40.6 us
    pallas_call x9, Pallas kernels, call(): pl.pallas_call(kernel, out_shape=[jax.ShapeDtypeStruct(o.shape, o.dtype)...  28.4 us
    all_to_all x1, starting transfers between devices, on_device(): lax.all_to_all(outgoing.reshape(groups, capacity, width), 'elem', split_a...  13.3 us
    ppermute x4, waiting for transfers between devices, from_sides(): above = [lax.ppermute(x, 'sec', ring(4, -1)) for x in shards]  11.5 us
    ppermute x2, starting transfers between devices, exchange(): above = lax.ppermute(south, DEVICE_AXES, ring(total, -1))  10.2 us
    ppermute x2, waiting for transfers between devices, from_far(): lax.ppermute(below, 'sec', ring(4, 1))  9.88 us
    ppermute x4, starting transfers between devices, from_sides(): above = [lax.ppermute(x, 'sec', ring(4, -1)) for x in shards]  6.71 us
    all_to_all x1, waiting for transfers between devices, on_device(): lax.all_to_all(outgoing.reshape(groups, capacity, width), 'elem', split_a...  6.58 us
  transfers between devices with their start and end apart: 17, of which 6 were waited for; matrix products, arithmetic and copies ran while one was open for 0% of the time, Pallas kernels for 8%

profile of v7, /device:TPU:1, one launch (start us, length us, event | category | flops | bytes accessed | tf_op | source)
XLA Modules:
  0.0 141.1 jit_solution(1123757587896288526)
XLA Ops:
  0.0 3.3 %collective-permute-start.3 = (bf16[640,256]{1,0:T(8,128)(2,1)}, bf16[640,256]{1,0:T(8,128)(2,1)S(1)}, u32[]{:S(2)}, u32[]{:S(2)}) collective-permute-start(bf16[640,256]{1,0:T(8,128)(2,1)} %bitcast.27), channel_id=1, source_target_pairs={{0,3},{1,0},{2,1},{3,2},{4,7},{5,4},{6,5},{7,6},{8,11},{9,8},{10,9... | collective-permute-start | bytes 983048 | tf_op jit(solution)/shard_map/ppermute | solution.py:310
  3.4 3.6 %shard_map.83 = (bf16[128,640]{1,0:T(8,128)(2,1)}, bf16[128,640]{1,0:T(8,128)(2,1)}) custom-call(f32[512,640]{1,0:T(8,128)} %bitcast.17, s32[4,32]{1,0:T(4,128)} %bitcast.21, f32[16,16]{1,0:T(8,128)} %op_ref.7, f32[640]{0:T(1024)} %rates_ref.7), custom_call_target="tpu_custom_call" | custom-call | flops 2000000000 | bytes 1642496 | tf_op jit(solution)/shard_map/pallas_call | solution.py:285
  7.0 0.3 collective-permute-start
  7.2 3.7 %collective-permute-start.1 = (bf16[128,640]{1,0:T(8,128)(2,1)}, bf16[128,640]{1,0:T(8,128)(2,1)S(1)}, u32[]{:S(2)}, u32[]{:S(2)}) collective-permute-start(bf16[128,640]{1,0:T(8,128)(2,1)} %get-tuple-element.21), channel_id=1, source_target_pairs={{0,255},{1,0},{2,1},{3,2},{4,3},{5,4},{6,5},{7,6},{8,7},{9,8},{10,... | collective-permute-start | bytes 491528 | tf_op jit(solution)/shard_map/ppermute | solution.py:304
  10.9 0.7 collective-permute-start.7
  11.6 2.4 %shard_map.82 = (f32[512,640]{1,0:T(8,128)S(1)}, bf16[1024,512]{1,0:T(8,128)(2,1)S(1)}) custom-call(f32[512,640]{1,0:T(8,128)S(1)} %bitcast.18, s32[4,32]{1,0:T(4,128)S(1)} %bitcast.22, f32[16,16]{1,0:T(8,128)S(1)} %copy-done.7, f32[640]{0:T(1024)S(1)} %copy-done.8, s32[1,512]{1,0:T(1,128)S(1)} %bitcast.15), custom_call_target="tpu_custom_call" | custom-call | flops 3000000000 | bytes 3676160 | tf_op jit(solution)/shard_map/pallas_call | solution.py:285
  14.1 3.6 %collective-permute-done.below_ref = bf16[128,640]{1,0:T(8,128)(2,1)S(1)} collective-permute-done((bf16[128,640]{1,0:T(8,128)(2,1)}, bf16[128,640]{1,0:T(8,128)(2,1)S(1)}, u32[]{:S(2)}, u32[]{:S(2)}) %collective-permute-start) | collective-permute-done | bytes 163872 | tf_op jit(solution)/shard_map/ppermute | solution.py:303
  17.7 2.2 %shard_map.85 = (bf16[128,640]{1,0:T(8,128)(2,1)S(1)}, bf16[128,640]{1,0:T(8,128)(2,1)S(1)}) custom-call(f32[512,640]{1,0:T(8,128)S(1)} %get-tuple-element.19.prev_ref, bf16[128,640]{1,0:T(8,128)(2,1)S(1)} %collective-permute-done.below_ref, bf16[128,640]{1,0:T(8,128)(2,1)S(1)} %collective-permute-done.1.above_ref, s32[4,32]{1,0:T(4,128)S(1)} %bitcast.23, ...), custom_call_target="tpu_custom_call" | custom-call | flops 2000000000 | bytes 1970176 | tf_op jit(solution)/shard_map/pallas_call | solution.py:285
  20.0 6.5 %collective-permute-start.5 = (bf16[128,640]{1,0:T(8,128)(2,1)S(1)}, bf16[128,640]{1,0:T(8,128)(2,1)S(1)}, u32[]{:S(2)}, u32[]{:S(2)}) collective-permute-start(bf16[128,640]{1,0:T(8,128)(2,1)S(1)} %get-tuple-element.23), channel_id=1, source_target_pairs={{0,255},{1,0},{2,1},{3,2},{4,3},{5,4},{6,5},{7,6},{8,7},{9,8},{10,... | collective-permute-start | bytes 491528 | tf_op jit(solution)/shard_map/ppermute | solution.py:304
  26.5 2.7 %shard_map.84.prev_ref = f32[512,640]{1,0:T(8,128)S(1)} custom-call(f32[512,640]{1,0:T(8,128)S(1)} %get-tuple-element.19.prev_ref, bf16[128,640]{1,0:T(8,128)(2,1)S(1)} %collective-permute-done.below_ref, bf16[128,640]{1,0:T(8,128)(2,1)S(1)} %collective-permute-done.1.above_ref, s32[4,32]{1,0:T(4,128)S(1)} %bitcast.24, f32[16,16]{1,0:T(8,128)S(1)} %copy-done.7, ...), custom_call_target="tpu_custom_call" | custom-call | flops 3000000000 | bytes 2953216 | tf_op jit(solution)/shard_map/pallas_call | solution.py:285
  29.2 2.6 %collective-permute-done.4.below_ref = bf16[128,640]{1,0:T(8,128)(2,1)S(1)} collective-permute-done((bf16[128,640]{1,0:T(8,128)(2,1)S(1)}, bf16[128,640]{1,0:T(8,128)(2,1)S(1)}, u32[]{:S(2)}, u32[]{:S(2)}) %collective-permute-start.4) | collective-permute-done | bytes 163872 | tf_op jit(solution)/shard_map/ppermute | solution.py:303
  31.8 2.8 %shard_map.86 = (f32[512,640]{1,0:T(8,128)S(1)}, bf16[1024,640]{1,0:T(8,128)(2,1)}, bf16[1024,256]{1,0:T(8,128)(2,1)S(1)}, bf16[1024,256]{1,0:T(8,128)(2,1)S(1)}) custom-call(f32[512,640]{1,0:T(8,128)S(1)} %shard_map.84.prev_ref, bf16[128,640]{1,0:T(8,128)(2,1)S(1)} %collective-permute-done.4.below_ref, ...), custom_call_target="tpu_custom_call" | custom-call | flops 3000000000 | bytes 7406080 | tf_op jit(solution)/shard_map/pallas_call | solution.py:285
  34.7 1.5 %collective-permute-start.10 = (bf16[1024,256]{1,0:T(8,128)(2,1)S(1)}, bf16[1024,256]{1,0:T(8,128)(2,1)}, u32[]{:S(2)}, u32[]{:S(2)}) collective-permute-start(bf16[1024,256]{1,0:T(8,128)(2,1)S(1)} %get-tuple-element.28), channel_id=1, source_target_pairs={{0,1},{1,2},{2,3},{3,0},{4,5},{5,6},{6,7},{7,4},{8,9},{9,10},{10,1... | collective-permute-start | bytes 1572872 | tf_op jit(solution)/shard_map/ppermute | solution.py:309
  36.2 2.6 %collective-permute-start.9 = (bf16[160,1024]{1,0:T(8,128)(2,1)S(1)}, bf16[160,1024]{1,0:T(8,128)(2,1)}, u32[]{:S(2)}, u32[]{:S(2)}) collective-permute-start(bf16[160,1024]{1,0:T(8,128)(2,1)S(1)} %collective-permute-done.7.refs_1_.refs_12_), channel_id=1, source_target_pairs={{0,3},{1,0},{2,1},{3,2},{4,7},{5,4},{6,5},{7,6},{8,11},{9,8},{10,9... | collective-permute-start | bytes 983048 | tf_op jit(solution)/shard_map/ppermute | solution.py:315
  38.9 13.3 %all-to-all-start = ((bf16[64,16,640]{2,1,0:T(8,128)(2,1)}), bf16[64,16,640]{2,1,0:T(8,128)(2,1)}, u32[]{:S(2)}, u32[]{:S(2)}) async-start(bf16[64,16,640]{2,1,0:T(8,128)(2,1)} %bitcast.9), calls=%async_computation | async-start | bytes 2621440 | tf_op jit(solution)/shard_map/all_to_all | solution.py:389
  52.3 2.7 %collective-permute-start.12 = (bf16[1024,256]{1,0:T(8,128)(2,1)S(1)}, bf16[1024,256]{1,0:T(8,128)(2,1)S(1)}, u32[]{:S(2)}, u32[]{:S(2)}) collective-permute-start(bf16[1024,256]{1,0:T(8,128)(2,1)S(1)} %get-tuple-element.30), channel_id=1, source_target_pairs={{0,3},{1,0},{2,1},{3,2},{4,7},{5,4},{6,5},{7,6},{8,11},{9,8},{10,9... | collective-permute-start | bytes 1572872 | tf_op jit(solution)/shard_map/ppermute | solution.py:310
  54.9 11.5 %collective-permute-done.12.refs_6_ = bf16[1024,256]{1,0:T(8,128)(2,1)S(1)} collective-permute-done((bf16[1024,256]{1,0:T(8,128)(2,1)S(1)}, bf16[1024,256]{1,0:T(8,128)(2,1)S(1)}, u32[]{:S(2)}, u32[]{:S(2)}) %collective-permute-start.12) | collective-permute-done | bytes 524320 | tf_op jit(solution)/shard_map/ppermute | solution.py:310
  66.5 2.4 %collective-permute-start.14 = (bf16[1024,256]{1,0:T(8,128)(2,1)S(1)}, bf16[1024,256]{1,0:T(8,128)(2,1)}, u32[]{:S(2)}, u32[]{:S(2)}) collective-permute-start(bf16[1024,256]{1,0:T(8,128)(2,1)S(1)} %collective-permute-done.12.refs_6_), channel_id=1, source_target_pairs={{0,3},{1,0},{2,1},{3,2},{4,7},{5,4},{6,5},{7,6},{8,11},{9,8},{10,9... | collective-permute-start | bytes 1572872 | tf_op jit(solution)/shard_map/ppermute | solution.py:315
  68.9 9.9 %collective-permute-done.13.refs_7_ = bf16[1024,256]{1,0:T(8,128)(2,1)S(1)} collective-permute-done((bf16[1024,256]{1,0:T(8,128)(2,1)}, bf16[1024,256]{1,0:T(8,128)(2,1)S(1)}, u32[]{:S(2)}, u32[]{:S(2)}) %collective-permute-start.13) | collective-permute-done | bytes 524320 | tf_op jit(solution)/shard_map/ppermute | solution.py:315
  78.8 0.3 collective-permute-done.14.refs_8_
  79.1 6.6 %all-to-all-done = bf16[64,16,640]{2,1,0:T(8,128)(2,1)} async-done(((bf16[64,16,640]{2,1,0:T(8,128)(2,1)}), bf16[64,16,640]{2,1,0:T(8,128)(2,1)}, u32[]{:S(2)}, u32[]{:S(2)}) %all-to-all-start) | async-done | bytes 1310752 | tf_op jit(solution)/shard_map/all_to_all | solution.py:389
  85.7 12.0 %shard_map.89 = bf16[1024,640]{1,0:T(8,128)(2,1)} custom-call(s32[1]{0:T(128)} %bitcast.8.sec_ref, bf16[1024,640]{1,0:T(8,128)(2,1)} %bitcast.10.rows_ref, bf16[640,256]{1,0:T(8,128)(2,1)} %bitcast.29, bf16[640,256]{1,0:T(8,128)(2,1)} %copy-done.3, bf16[640,256]{1,0:T(8,128)(2,1)} %get-tuple-element.27.refs_2_, bf16[640,256]{1,0:T(8,128)(2,1)} %copy-done.4, ...), custom_call_target="tpu_custom_call" | custom-call | flops 7000000000 | bytes 9437188 | tf_op jit(solution)/shard_map/pallas_call | solution.py:285
  97.7 40.6 %all_to_all.10 = bf16[64,16,640]{2,1,0:T(8,128)(2,1)S(1)} all-to-all(bf16[64,16,640]{2,1,0:T(8,128)(2,1)} %bitcast.26), channel_id=1, replica_groups=mesh['elem'=64,'sec'=4] {'elem'}, dimensions={0} | all-to-all | bytes 2621440 | tf_op jit(solution)/shard_map/all_to_all | solution.py:416
  138.3 2.8 %shard_map.90 = f32[512,640]{1,0:T(8,128)} custom-call(f32[512,640]{1,0:T(8,128)S(1)} %get-tuple-element.25.state_ref, bf16[1024,640]{1,0:T(8,128)(2,1)S(1)} %bitcast.14, s32[1,512]{1,0:T(1,128)S(1)} %bitcast.16), custom_call_target="tpu_custom_call" | custom-call | flops 1000000000 | bytes 3934208 | tf_op jit(solution)/shard_map/pallas_call | solution.py:285
  (48 shorter events, 0.4 us)
Async XLA Ops:
  0.0 17.7 %collective-permute-start.3 = (bf16[640,256]{1,0:T(8,128)(2,1)}, bf16[640,256]{1,0:T(8,128)(2,1)S(1)}, u32[]{:S(2)}, u32[]{:S(2)}) collective-permute-start(bf16[640,256]{1,0:T(8,128)(2,1)} %bitcast.27), channel_id=1, source_target_pairs={{0,3},{1,0},{2,1},{3,2},{4,7},{5,4},{6,5},{7,6},{8,11},{9,8},{10,9... | collective-permute-start | bytes 983048 | tf_op jit(solution)/shard_map/ppermute | solution.py:310
  3.3 14.4 %collective-permute-start.2 = (bf16[640,256]{1,0:T(8,128)(2,1)}, bf16[640,256]{1,0:T(8,128)(2,1)S(1)}, u32[]{:S(2)}, u32[]{:S(2)}) collective-permute-start(bf16[640,256]{1,0:T(8,128)(2,1)} %bitcast.28), channel_id=1, source_target_pairs={{0,1},{1,2},{2,3},{3,0},{4,5},{5,6},{6,7},{7,4},{8,9},{9,10},{10,1... | collective-permute-start | bytes 983048 | tf_op jit(solution)/shard_map/ppermute | solution.py:309
  3.3 8.3 %copy-start = (s32[512,1]{0,1:T(1,128)S(1)}, s32[512,1]{0,1:T(1,128)}, u32[]{:S(2)}) copy-start(s32[512,1]{0,1:T(1,128)} %param.12) | copy-start | bytes 6148
  3.3 8.3 %copy-start.1 = (f32[32,16,640]{2,1,0:T(8,128)S(1)}, f32[32,16,640]{2,1,0:T(8,128)}, u32[]{:S(2)}) copy-start(f32[32,16,640]{2,1,0:T(8,128)} %param.8) | copy-start | bytes 3932164
  3.3 8.3 %copy-start.7 = (f32[16,16]{1,0:T(8,128)S(1)}, f32[16,16]{1,0:T(8,128)}, u32[]{:S(2)}) copy-start(f32[16,16]{1,0:T(8,128)} %op_ref.7) | copy-start | bytes 3076
  3.3 8.3 %copy-start.8 = (f32[640]{0:T(1024)S(1)}, f32[640]{0:T(1024)}, u32[]{:S(2)}) copy-start(f32[640]{0:T(1024)} %rates_ref.7) | copy-start | bytes 7684
  7.0 10.7 %collective-permute-start = (bf16[128,640]{1,0:T(8,128)(2,1)}, bf16[128,640]{1,0:T(8,128)(2,1)S(1)}, u32[]{:S(2)}, u32[]{:S(2)}) collective-permute-start(bf16[128,640]{1,0:T(8,128)(2,1)} %get-tuple-element.20), channel_id=1, source_target_pairs={{0,1},{1,2},{2,3},{3,4},{4,5},{5,6},{6,7},{7,8},{8,9},{9,10},{10,1... | collective-permute-start | bytes 491528 | tf_op jit(solution)/shard_map/ppermute | solution.py:303
  7.2 10.5 %collective-permute-start.1 = (bf16[128,640]{1,0:T(8,128)(2,1)}, bf16[128,640]{1,0:T(8,128)(2,1)S(1)}, u32[]{:S(2)}, u32[]{:S(2)}) collective-permute-start(bf16[128,640]{1,0:T(8,128)(2,1)} %get-tuple-element.21), channel_id=1, source_target_pairs={{0,255},{1,0},{2,1},{3,2},{4,3},{5,4},{6,5},{7,6},{8,7},{9,8},{10,... | collective-permute-start | bytes 491528 | tf_op jit(solution)/shard_map/ppermute | solution.py:304
  10.9 18.2 %collective-permute-start.7 = (bf16[160,1024]{1,0:T(8,128)(2,1)S(1)}, bf16[160,1024]{1,0:T(8,128)(2,1)S(1)}, u32[]{:S(2)}, u32[]{:S(2)}) collective-permute-start(bf16[160,1024]{1,0:T(8,128)(2,1)S(1)} %bitcast.31), channel_id=1, source_target_pairs={{0,3},{1,0},{2,1},{3,2},{4,7},{5,4},{6,5},{7,6},{8,11},{9,8},{10,9... | collective-permute-start | bytes 983048 | tf_op jit(solution)/shard_map/ppermute | solution.py:310
  17.7 11.5 %collective-permute-start.6 = (bf16[160,1024]{1,0:T(8,128)(2,1)S(1)}, bf16[160,1024]{1,0:T(8,128)(2,1)S(1)}, u32[]{:S(2)}, u32[]{:S(2)}) collective-permute-start(bf16[160,1024]{1,0:T(8,128)(2,1)S(1)} %bitcast.32), channel_id=1, source_target_pairs={{0,1},{1,2},{2,3},{3,0},{4,5},{5,6},{6,7},{7,4},{8,9},{9,10},{10,1... | collective-permute-start | bytes 983048 | tf_op jit(solution)/shard_map/ppermute | solution.py:309
  17.7 18.5 %copy-start.4 = (bf16[640,256]{1,0:T(8,128)(2,1)}, bf16[640,256]{1,0:T(8,128)(2,1)S(1)}, u32[]{:S(2)}) copy-start(bf16[640,256]{1,0:T(8,128)(2,1)S(1)} %collective-permute-done.2.refs_0_.refs_3_) | copy-start | bytes 983044
  19.9 11.9 %collective-permute-start.4 = (bf16[128,640]{1,0:T(8,128)(2,1)S(1)}, bf16[128,640]{1,0:T(8,128)(2,1)S(1)}, u32[]{:S(2)}, u32[]{:S(2)}) collective-permute-start(bf16[128,640]{1,0:T(8,128)(2,1)S(1)} %get-tuple-element.22), channel_id=1, source_target_pairs={{0,1},{1,2},{2,3},{3,4},{4,5},{5,6},{6,7},{7,8},{8,9},{9,10},{10,1... | collective-permute-start | bytes 491528 | tf_op jit(solution)/shard_map/ppermute | solution.py:303
  20.0 11.8 %copy-start.2 = (bf16[1,2,1024,256]{3,2,1,0:T(8,128)(2,1)S(1)}, bf16[1,2,1024,256]{3,2,1,0:T(8,128)(2,1)}, u32[]{:S(2)}) copy-start(bf16[1,2,1024,256]{3,2,1,0:T(8,128)(2,1)} %param.14) | copy-start | bytes 3145732
  20.0 11.8 %collective-permute-start.5 = (bf16[128,640]{1,0:T(8,128)(2,1)S(1)}, bf16[128,640]{1,0:T(8,128)(2,1)S(1)}, u32[]{:S(2)}, u32[]{:S(2)}) collective-permute-start(bf16[128,640]{1,0:T(8,128)(2,1)S(1)} %get-tuple-element.23), channel_id=1, source_target_pairs={{0,255},{1,0},{2,1},{3,2},{4,3},{5,4},{6,5},{7,6},{8,7},{9,8},{10,... | collective-permute-start | bytes 491528 | tf_op jit(solution)/shard_map/ppermute | solution.py:304
  34.7 17.6 %collective-permute-start.11 = (bf16[1024,256]{1,0:T(8,128)(2,1)S(1)}, bf16[1024,256]{1,0:T(8,128)(2,1)}, u32[]{:S(2)}, u32[]{:S(2)}) collective-permute-start(bf16[1024,256]{1,0:T(8,128)(2,1)S(1)} %get-tuple-element.28), channel_id=1, source_target_pairs={{0,3},{1,0},{2,1},{3,2},{4,7},{5,4},{6,5},{7,6},{8,11},{9,8},{10,9... | collective-permute-start | bytes 1572872 | tf_op jit(solution)/shard_map/ppermute | solution.py:310
  34.7 20.2 %collective-permute-start.10 = (bf16[1024,256]{1,0:T(8,128)(2,1)S(1)}, bf16[1024,256]{1,0:T(8,128)(2,1)}, u32[]{:S(2)}, u32[]{:S(2)}) collective-permute-start(bf16[1024,256]{1,0:T(8,128)(2,1)S(1)} %get-tuple-element.28), channel_id=1, source_target_pairs={{0,1},{1,2},{2,3},{3,0},{4,5},{5,6},{6,7},{7,4},{8,9},{9,10},{10,1... | collective-permute-start | bytes 1572872 | tf_op jit(solution)/shard_map/ppermute | solution.py:309
  36.2 32.7 %collective-permute-start.8 = (bf16[640,256]{1,0:T(8,128)(2,1)S(1)}, bf16[640,256]{1,0:T(8,128)(2,1)}, u32[]{:S(2)}, u32[]{:S(2)}) collective-permute-start(bf16[640,256]{1,0:T(8,128)(2,1)S(1)} %collective-permute-done.2.refs_0_.refs_3_), channel_id=1, source_target_pairs={{0,1},{1,2},{2,3},{3,0},{4,5},{5,6},{6,7},{7,4},{8,9},{9,10},{10,1... | collective-permute-start | bytes 983048 | tf_op jit(solution)/shard_map/ppermute | solution.py:315
  36.2 32.7 %collective-permute-start.9 = (bf16[160,1024]{1,0:T(8,128)(2,1)S(1)}, bf16[160,1024]{1,0:T(8,128)(2,1)}, u32[]{:S(2)}, u32[]{:S(2)}) collective-permute-start(bf16[160,1024]{1,0:T(8,128)(2,1)S(1)} %collective-permute-done.7.refs_1_.refs_12_), channel_id=1, source_target_pairs={{0,3},{1,0},{2,1},{3,2},{4,7},{5,4},{6,5},{7,6},{8,11},{9,8},{10,9... | collective-permute-start | bytes 983048 | tf_op jit(solution)/shard_map/ppermute | solution.py:315
  38.9 46.8 %all-to-all-start = ((bf16[64,16,640]{2,1,0:T(8,128)(2,1)}), bf16[64,16,640]{2,1,0:T(8,128)(2,1)}, u32[]{:S(2)}, u32[]{:S(2)}) async-start(bf16[64,16,640]{2,1,0:T(8,128)(2,1)} %bitcast.9), calls=%async_computation | async-start | bytes 2621440 | tf_op jit(solution)/shard_map/all_to_all | solution.py:389
  52.2 16.7 %collective-permute-start.15 = (bf16[1024,256]{1,0:T(8,128)(2,1)S(1)}, bf16[1024,256]{1,0:T(8,128)(2,1)S(1)}, u32[]{:S(2)}, u32[]{:S(2)}) collective-permute-start(bf16[1024,256]{1,0:T(8,128)(2,1)S(1)} %get-tuple-element.30), channel_id=1, source_target_pairs={{0,1},{1,2},{2,3},{3,0},{4,5},{5,6},{6,7},{7,4},{8,9},{9,10},{10,1... | collective-permute-start | bytes 1572872 | tf_op jit(solution)/shard_map/ppermute | solution.py:309
  52.3 14.2 %collective-permute-start.12 = (bf16[1024,256]{1,0:T(8,128)(2,1)S(1)}, bf16[1024,256]{1,0:T(8,128)(2,1)S(1)}, u32[]{:S(2)}, u32[]{:S(2)}) collective-permute-start(bf16[1024,256]{1,0:T(8,128)(2,1)S(1)} %get-tuple-element.30), channel_id=1, source_target_pairs={{0,3},{1,0},{2,1},{3,2},{4,7},{5,4},{6,5},{7,6},{8,11},{9,8},{10,9... | collective-permute-start | bytes 1572872 | tf_op jit(solution)/shard_map/ppermute | solution.py:310
  54.9 23.9 %collective-permute-start.13 = (bf16[1024,256]{1,0:T(8,128)(2,1)}, bf16[1024,256]{1,0:T(8,128)(2,1)S(1)}, u32[]{:S(2)}, u32[]{:S(2)}) collective-permute-start(bf16[1024,256]{1,0:T(8,128)(2,1)} %get-tuple-element.31.refs_9_), channel_id=1, source_target_pairs={{0,1},{1,2},{2,3},{3,0},{4,5},{5,6},{6,7},{7,4},{8,9},{9,10},{10,1... | collective-permute-start | bytes 1572872 | tf_op jit(solution)/shard_map/ppermute | solution.py:315
  66.5 12.7 %collective-permute-start.14 = (bf16[1024,256]{1,0:T(8,128)(2,1)S(1)}, bf16[1024,256]{1,0:T(8,128)(2,1)}, u32[]{:S(2)}, u32[]{:S(2)}) collective-permute-start(bf16[1024,256]{1,0:T(8,128)(2,1)S(1)} %collective-permute-done.12.refs_6_), channel_id=1, source_target_pairs={{0,3},{1,0},{2,1},{3,2},{4,7},{5,4},{6,5},{7,6},{8,11},{9,8},{10,9... | collective-permute-start | bytes 1572872 | tf_op jit(solution)/shard_map/ppermute | solution.py:315
  68.9 16.8 %copy-start.10 = (bf16[1024,256]{1,0:T(8,128)(2,1)}, bf16[1024,256]{1,0:T(8,128)(2,1)S(1)}, u32[]{:S(2)}) copy-start(bf16[1024,256]{1,0:T(8,128)(2,1)S(1)} %collective-permute-done.15.refs_10_) | copy-start | bytes 1572868
  (7 other events, 39.9 us)
